TPU v7x, 256 devices: a whole 4x4x8 slice. The times are simulated.
256 devices in a mesh: sector: 32 (over x, y, core), op: 8 (over z).
Axes of the slice: x: 4, y: 4, z: 8, core: 2. Of those that a mesh axis runs over, the one named last changes fastest.
Arguments:
- theta: float32 [128, 128, 128], P('sector'), may hold values from -6 to 6
- left_env: bfloat16 [128, 128, 128, 128], P('sector', 'op'), may hold values from -3 to 3
- right_env: bfloat16 [128, 128, 128, 128], P('sector', 'op'), may hold values from -3 to 3
- perm: int32 [128], replicated, may hold values from 0 to 127, each once
- dims: int32 [128, 2], P('sector'), may hold values from 32 to 128, as said below
Outputs:
- lanczos_vec: float32 [128, 128, 128], P('sector')
- coeffs: float32 [6], replicated
- density: float32 [128, 128, 128], P('sector')
Inputs may be any that keep to these rules, and one draw needn't show every extreme that they name: `dims`: each entry is a kept dimension of 32 to 128; the first position has 128 on both sides.
All inputs are finite; a program needn't handle non-finite values.
Results may differ from a plain program's by a relative error of at most 0.012.
Values may be sent and summed in bfloat16 or wider, within the bound.
No kernel may reach another device: no remote copies, remote signals or barrier semaphores. Data moves between devices by JAX's collectives and lax.ppermute only.
A program may use at most 64 MiB of HBM per device.

v0:
```python
import jax
import jax.numpy as jnp
from jax import lax
from jax.sharding import PartitionSpec as P


def local_mask(dims, row_count, width):
    rows = jnp.arange(row_count, dtype=jnp.int32)
    cols = jnp.arange(width, dtype=jnp.int32)
    inside_rows = (rows[None, :] < dims[:, 0:1]).astype(jnp.float32)
    inside_cols = (cols[None, :] < dims[:, 1:2]).astype(jnp.float32)
    return inside_rows[:, :, None] * inside_cols[:, None, :]


def neighbour_positions(perm, sec_dev):
    total = perm.shape[0]
    pos_of = jnp.argsort(perm)
    first = lax.axis_index("sector") * sec_dev
    mine = lax.dynamic_slice_in_dim(perm, first, sec_dev, 0)
    shifts = jnp.arange(3, dtype=jnp.int32) - 1
    return pos_of[(mine[:, None] + shifts[None, :]) % total].reshape(-1)


def pick_blocks(src_flat):

    def fold_fn(carry, piece, start):
        count = piece.shape[0]
        hits = (src_flat[:, None] == jnp.arange(count, dtype=jnp.int32)[None, :]).astype(
            jnp.bfloat16
        )
        return jnp.dot(hits, piece.reshape(count, -1), preferred_element_type=jnp.float32)

    return fold_fn


def term_products(nbrs, left_env, right_env):
    term_dev = left_env.shape[1]
    global_terms = lax.axis_index("op") * term_dev + jnp.arange(term_dev, dtype=jnp.int32)
    selector = jax.nn.one_hot(global_terms % 3, 3, dtype=jnp.bfloat16)
    picked = jnp.einsum("wq,pqjk->pwjk", selector, nbrs, preferred_element_type=jnp.float32).astype(
        jnp.bfloat16
    )
    inner = jnp.einsum(
        "pwij,pwjk->pwik", left_env, picked, preferred_element_type=jnp.float32
    ).astype(jnp.bfloat16)
    return jnp.einsum("pwik,pwkl->pil", inner, right_env, preferred_element_type=jnp.float32)


def per_device(theta, left_env, right_env, perm, dims):
    sec_dev, width, _ = theta.shape
    n_op = lax.axis_size("op")
    terms_all = left_env.shape[1] * n_op
    count = jnp.float32(lax.axis_size("sector") * sec_dev * width * width)
    scale = 1.0 / jnp.sqrt(jnp.float32(terms_all))
    src_flat = neighbour_positions(perm, sec_dev)
    fold_fn = pick_blocks(src_flat)
    mask = local_mask(dims, width, width)

    def sq_sum(first):
        return lax.psum(jnp.sum(first * first), "sector")

    start_vec = theta * mask
    vector = start_vec / jnp.sqrt(sq_sum(start_vec) / count + 1e-06)
    previous = jnp.zeros_like(vector)
    beta = jnp.float32(0.0)
    alphas = []
    betas = []
    for step in range(3):
        empty = jnp.zeros((sec_dev * 3, width * width), jnp.float32)
        carry = fold_fn(
            empty,
            lax.all_gather(vector.astype(jnp.bfloat16), "sector", axis=0, tiled=True),
            jnp.int32(0),
        )
        nbrs = carry.astype(jnp.bfloat16).reshape(sec_dev, 3, width, width)
        partial_sum = term_products(nbrs, left_env, right_env)
        image = lax.psum(partial_sum, "op") * scale * mask
        alpha = lax.psum(jnp.sum(vector * image), "sector") / count
        resid = image - alpha * vector - beta * previous
        beta_next = jnp.sqrt(sq_sum(resid) / count + 1e-06)
        beta = beta_next
        previous, vector = (vector, resid / beta)
        alphas.append(alpha)
        betas.append(beta)
    coeffs = jnp.stack(alphas + betas)
    density = jnp.einsum("pij,pkj->pik", vector, vector, precision=lax.Precision.HIGHEST) / width
    return (vector, coeffs, density)


def solution(mesh):
    placed = (
        P("sector", None, None),
        P("sector", "op", None, None),
        P("sector", "op", None, None),
        P(),
        P("sector", None),
    )
    return jax.shard_map(
        per_device,
        mesh=mesh,
        in_specs=placed,
        out_specs=(P("sector", None, None), P(), P("sector", None, None)),
        check_vma=False,
    )
```

profile of v0, /device:TPU:1, one launch (start us, length us, event | category | flops | bytes accessed | tf_op | source)
XLA Modules:
  0.0 876.9 jit_solution(8300611472373750814)
XLA Ops:
  7.2 0.0 copy-start
  7.2 0.0 all-gather.4.cloned.1.call-start
  7.2 0.8 slice_bitcast_fusion.1
  8.1 0.1 fusion.56
  8.1 1.7 multiply_reduce_fusion.6
  9.8 65.9 %psum.70 = f32[]{:T(128)} all-reduce(f32[]{:T(128)} %multiply_reduce_fusion.6), channel_id=1, replica_groups=mesh['sector'=32,'op'=8] {'sector'}, use_global_device_ids=true, to_apply=%region_2.3 | all-reduce | flops 1 | bytes 8 | tf_op jit(solution)/shard_map/psum | solution.py:60
  76.4 1.7 fusion.63
  78.2 0.0 all-gather.4.cloned.1.call-update
  78.2 0.0 all-reduce.4.cloned.1.call-start
  78.2 0.7 dynamic_slice.3
  79.0 3.2 sort.17
  82.2 0.1 compare_select_fusion
  82.2 0.1 reshape.175
  82.3 0.7 gather_fusion
  83.0 47.6 %all-gather.4.cloned.1.call-done = bf16[128,128,128]{2,1,0:T(8,128)(2,1)} async-done(((bf16[4,128,128]{2,1,0:T(8,128)(2,1)}), bf16[128,128,128]{2,1,0:T(8,128)(2,1)}) %all-gather.4.cloned.1.call-update) | async-done | bytes 4194320 | tf_op jit(solution)/shard_map/all_gather | solution.py:72
  130.6 4.5 convolution_convert_fusion.2
  135.1 0.1 copy.25
  135.2 2.1 convert_bitcast_fusion.2
  137.4 0.0 copy-done
  137.4 0.0 copy-start.1
  137.4 5.0 fusion.33
  142.4 0.0 all-reduce.4.cloned.1.call-update
  142.4 0.0 all-gather.6.cloned.1.call-start
  142.5 67.1 %all-reduce.4.cloned.1.call-done = f32[4,128,128]{2,1,0:T(8,128)} async-done(((f32[4,128,128]{2,1,0:T(8,128)}), f32[4,128,128]{2,1,0:T(8,128)}) %all-reduce.4.cloned.1.call-update) | async-done | bytes 262160 | tf_op jit(solution)/shard_map/psum | solution.py:77
  209.6 0.0 copy-done.1
  209.6 1.7 multiply_reduce_fusion.5
  211.3 67.8 %psum.72 = f32[]{:T(128)} all-reduce(f32[]{:T(128)} %multiply_reduce_fusion.5), channel_id=1, replica_groups=mesh['sector'=32,'op'=8] {'sector'}, use_global_device_ids=true, to_apply=%region_5.6 | all-reduce | flops 1 | bytes 8 | tf_op jit(solution)/shard_map/psum | solution.py:78
  279.8 1.7 multiply_reduce_fusion.4
  281.5 63.3 %psum.73 = f32[]{:T(128)} all-reduce(f32[]{:T(128)} %multiply_reduce_fusion.4), channel_id=1, replica_groups=mesh['sector'=32,'op'=8] {'sector'}, use_global_device_ids=true, to_apply=%region_7.8 | all-reduce | flops 1 | bytes 8 | tf_op jit(solution)/shard_map/psum | solution.py:60
  345.5 1.8 fusion.64
  347.2 0.0 all-gather.6.cloned.1.call-update
  347.2 0.0 all-reduce.6.cloned.1.call-start
  347.3 45.2 %all-gather.6.cloned.1.call-done = bf16[128,128,128]{2,1,0:T(8,128)(2,1)} async-done(((bf16[4,128,128]{2,1,0:T(8,128)(2,1)}), bf16[128,128,128]{2,1,0:T(8,128)(2,1)}) %all-gather.6.cloned.1.call-update) | async-done | bytes 4194320 | tf_op jit(solution)/shard_map/all_gather | solution.py:72
  392.4 4.5 convolution_convert_fusion.1
  397.0 0.1 copy.27
  397.1 2.1 convert_bitcast_fusion.1
  399.2 5.0 fusion.38
  404.2 0.0 all-reduce.6.cloned.1.call-update
  404.2 0.0 all-gather.8.cloned.1.call-start
  404.3 67.1 %all-reduce.6.cloned.1.call-done = f32[4,128,128]{2,1,0:T(8,128)} async-done(((f32[4,128,128]{2,1,0:T(8,128)}), f32[4,128,128]{2,1,0:T(8,128)}) %all-reduce.6.cloned.1.call-update) | async-done | bytes 262160 | tf_op jit(solution)/shard_map/psum | solution.py:77
  471.4 1.7 multiply_reduce_fusion.3
  473.1 68.0 %psum.75 = f32[]{:T(128)} all-reduce(f32[]{:T(128)} %multiply_reduce_fusion.3), channel_id=1, replica_groups=mesh['sector'=32,'op'=8] {'sector'}, use_global_device_ids=true, to_apply=%region_10.11 | all-reduce | flops 1 | bytes 8 | tf_op jit(solution)/shard_map/psum | solution.py:78
  541.7 1.7 multiply_reduce_fusion.2
  543.4 63.3 %psum.76 = f32[]{:T(128)} all-reduce(f32[]{:T(128)} %get-tuple-element.7), channel_id=1, replica_groups=mesh['sector'=32,'op'=8] {'sector'}, use_global_device_ids=true, to_apply=%region_12.13 | all-reduce | flops 1 | bytes 8 | tf_op jit(solution)/shard_map/psum | solution.py:60
  607.4 0.7 fusion.62
  608.1 0.0 all-gather.8.cloned.1.call-update
  608.1 0.0 all-reduce.8.cloned.1.call-start
  608.2 45.2 %all-gather.8.cloned.1.call-done = bf16[128,128,128]{2,1,0:T(8,128)(2,1)} async-done(((bf16[4,128,128]{2,1,0:T(8,128)(2,1)}), bf16[128,128,128]{2,1,0:T(8,128)(2,1)}) %all-gather.8.cloned.1.call-update) | async-done | bytes 4194320 | tf_op jit(solution)/shard_map/all_gather | solution.py:72
  653.3 4.5 convolution_convert_fusion
  657.8 0.1 copy.29
  658.0 2.1 convert_bitcast_fusion
  660.1 5.0 fusion.43
  665.1 0.0 all-reduce.8.cloned.1.call-update
  665.1 67.1 %all-reduce.8.cloned.1.call-done = f32[4,128,128]{2,1,0:T(8,128)} async-done(((f32[4,128,128]{2,1,0:T(8,128)}), f32[4,128,128]{2,1,0:T(8,128)}) %all-reduce.8.cloned.1.call-update) | async-done | bytes 262160 | tf_op jit(solution)/shard_map/psum | solution.py:77
  732.2 1.7 multiply_reduce_fusion.1
  733.9 67.8 %psum.78 = f32[]{:T(128)} all-reduce(f32[]{:T(128)} %multiply_reduce_fusion.1), channel_id=1, replica_groups=mesh['sector'=32,'op'=8] {'sector'}, use_global_device_ids=true, to_apply=%region_15.16 | all-reduce | flops 1 | bytes 8 | tf_op jit(solution)/shard_map/psum | solution.py:78
  802.4 1.7 multiply_reduce_fusion
  804.1 63.3 %psum.79 = f32[]{:T(128)} all-reduce(f32[]{:T(128)} %get-tuple-element.5), channel_id=1, replica_groups=mesh['sector'=32,'op'=8] {'sector'}, use_global_device_ids=true, to_apply=%region_17.18 | all-reduce | flops 1 | bytes 8 | tf_op jit(solution)/shard_map/psum | solution.py:60
  868.1 0.0 copy-start.2
  868.1 1.4 convolution_multiply_fusion
  869.5 0.6 stack.27
  870.1 0.0 copy-done.2
  (8 shorter events, 0.1 us)
Async XLA Ops:
  7.2 130.2 %copy-start = (bf16[4,16,128,128]{3,2,1,0:T(8,128)(2,1)S(1)}, bf16[4,16,128,128]{3,2,1,0:T(8,128)(2,1)}, u32[]{:S(2)}) copy-start(bf16[4,16,128,128]{3,2,1,0:T(8,128)(2,1)} %param.7) | copy-start | bytes 6291460
  7.2 123.4 %all-gather.4.cloned.1.call-start = ((), (), s32[]{:S(2)}) async-start(), calls=%async_computation | async-start | bytes 4325376 | tf_op jit(solution)/shard_map/all_gather | solution.py:72
  78.2 131.4 %all-reduce.4.cloned.1.call-start = ((), (), s32[]{:S(2)}) async-start(), calls=%async_computation.1 | async-start | bytes 524288 | tf_op jit(solution)/shard_map/psum | solution.py:77
  137.4 72.2 %copy-start.1 = (f32[4,128,128]{2,1,0:T(8,128)S(1)}, f32[4,128,128]{2,1,0:T(8,128)}, u32[]{:S(2)}) copy-start(f32[4,128,128]{2,1,0:T(8,128)} %param.5) | copy-start | bytes 786436
  142.4 250.0 %all-gather.6.cloned.1.call-start = ((), (), s32[]{:S(2)}) async-start(), calls=%async_computation.2 | async-start | bytes 4325376 | tf_op jit(solution)/shard_map/all_gather | solution.py:72
  347.2 124.1 %all-reduce.6.cloned.1.call-start = ((), (), s32[]{:S(2)}) async-start(), calls=%async_computation.3 | async-start | bytes 524288 | tf_op jit(solution)/shard_map/psum | solution.py:77
  404.2 249.1 %all-gather.8.cloned.1.call-start = ((), (), s32[]{:S(2)}) async-start(), calls=%async_computation.4 | async-start | bytes 4325376 | tf_op jit(solution)/shard_map/all_gather | solution.py:72
  608.1 124.1 %all-reduce.8.cloned.1.call-start = ((), (), s32[]{:S(2)}) async-start(), calls=%async_computation.5 | async-start | bytes 524288 | tf_op jit(solution)/shard_map/psum | solution.py:77
  868.1 2.0 copy-start.2
Sparse Core Ops, SparseCore 0:
  78.3 52.2 all-gather.3
  142.5 66.9 all-reduce.3
  347.4 45.0 all-gather.5
  404.4 66.9 all-reduce.5
  608.2 45.0 all-gather.7
  665.2 66.8 all-reduce.7
where the time goes:
time: 878 us; the launch traced here: 877 us
  blocking collectives  459 us (52%)
  waiting for transfers between devices  339 us (39%)
  matrix products  36.3 us (4%)
  other arithmetic  19.5 us (2%)
  between operations  18.9 us (2%)
    psum x4, blocking collectives, sq_sum(): return lax.psum(jnp.sum(first * first), 'sector')  256 us
    psum x3, blocking collectives, per_device(): alpha = lax.psum(jnp.sum(vector * image), 'sector') / count  204 us
    psum x3, waiting for transfers between devices, per_device(): image = lax.psum(partial_sum, 'op') * scale * mask  201 us
    all_gather x3, waiting for transfers between devices, per_device(): lax.all_gather(vector.astype(jnp.bfloat16), 'sector', axis=0, tiled=True)  138 us
  transfers between devices with their start and end apart: 6, of which 6 were waited for; matrix products, arithmetic and copies ran while one was open for 1% of the time, Pallas kernels for 0%

commit v1 on v0

v1 whole, which is shorter than its diff:
```python
import jax
import jax.numpy as jnp
from jax import lax
from jax.experimental import pallas as pl
from jax.experimental.pallas import tpu as pltpu
from jax.sharding import PartitionSpec as P

F32 = jnp.float32
BF16 = jnp.bfloat16
BOTH = ("sector", "op")
W = 128
SEC = 4
SLAB = 8
NZ = 8
CHIPS = 16
GRP = 16
NBLK = 3 * SEC
TERMS_DEV = 16
COUNT = float(128 * W * W)
EPS = 1e-06
SCALE = 1.0 / (128.0**0.5)
NCOL = 4

CZ_GROUPS = [[(2 * chip + c) * NZ + z for c in range(2) for z in range(NZ)] for chip in range(CHIPS)]
XY_GROUPS = [[2 * chip + c for chip in range(CHIPS)] for c in range(2)]
SWAP = [(i, i ^ 1) for i in range(2 * CHIPS)]

VMEM = pl.BlockSpec(memory_space=pltpu.VMEM)
SMEM = pl.BlockSpec(memory_space=pltpu.SMEM)


def core_and_z():
    return lax.rem(lax.axis_index("sector"), 2), lax.axis_index("op")


def call(body, outs, specs, scratch=(), flops=0, nbytes=1 << 18):
    return pl.pallas_call(
        body,
        out_shape=[jax.ShapeDtypeStruct(s, d) for s, d in outs],
        in_specs=specs,
        out_specs=[VMEM] * len(outs),
        scratch_shapes=list(scratch),
        compiler_params=pltpu.CompilerParams(vmem_limit_bytes=32 * 1024 * 1024),
        cost_estimate=pl.CostEstimate(flops=flops, bytes_accessed=nbytes, transcendentals=0),
    )


def iota(shape, dim):
    return lax.broadcasted_iota(jnp.int32, shape, dim)


def row_sum(x):
    return jnp.sum(x, axis=0, keepdims=True)


def split_rows(rows):
    at = iota((16, W), 0)
    tile = jnp.zeros((16, W), F32)
    for k, row in enumerate(rows):
        hi = row.astype(BF16).astype(F32)
        mid = (row - hi).astype(BF16).astype(F32)
        low = row - hi - mid
        for n, part in enumerate((hi, mid, low)):
            tile = jnp.where(at == 3 * k + n, jnp.broadcast_to(part, (16, W)), tile)
    return tile.astype(BF16)


def join_rows(tile, count):
    return [row_sum(tile[3 * k : 3 * k + 3]) for k in range(count)]


def total(row):
    return jnp.sum(row, axis=1, keepdims=True)


def start_kernel(dims, theta, keep, send):
    c, z = core_and_z()
    for slot, out in ((c * NZ + z, keep), ((1 - c) * NZ + z, send)):
        first = pl.multiple_of(slot * SLAB, SLAB)
        rows = iota((SLAB, W), 0) + first
        cols = iota((SLAB, W), 1)
        for i in range(SEC):
            inside = (rows < dims[i, 0]) & (cols < dims[i, 1])
            out[SLAB * i : SLAB * (i + 1), :] = jnp.where(inside, theta[i, pl.ds(first, SLAB), :], 0.0)


def spread_start_kernel(keep, came, msg, slab):
    c, _ = core_and_z()
    half = SEC * SLAB

    @pl.when(c == 0)
    def _():
        slab[:half] = keep[...]
        slab[half:] = came[...]

    @pl.when(c == 1)
    def _():
        slab[:half] = came[...]
        slab[half:] = keep[...]

    rounded = slab[...].astype(BF16)
    for n in range(CHIPS):
        msg[n] = rounded


def source_kernel(perm, src, pos):
    chip = lax.axis_index("sector") // 2

    def put(p, carry):
        pos[perm[p]] = p
        return carry

    lax.fori_loop(0, 128, put, 0)
    for n in range(2 * SEC):
        mine = perm[chip * 2 * SEC + n]
        for q in range(3):
            src[3 * n + q] = pos[lax.rem(mine + (q + 127), 128)]


def select_kernel(rows, src, got, msg, blocks):
    for n in range(CHIPS):
        blocks[2 * SEC * SLAB * n : 2 * SEC * SLAB * (n + 1)] = got[n, : 2 * SEC * SLAB].astype(F32)
    for c in range(2):
        for pair in range(NBLK // 2):
            two = [
                blocks[pl.ds(pl.multiple_of(src[NBLK * c + 2 * pair + k] * SLAB, SLAB), SLAB), :]
                for k in range(2)
            ]
            tile = jnp.concatenate(two, axis=0).astype(BF16)
            for z in range(NZ):
                msg[c * NZ + z, 16 * pair : 16 * (pair + 1)] = tile
    if rows:
        acc = got[0, 2 * SEC * SLAB :].astype(F32)
        for n in range(1, CHIPS):
            acc = acc + got[n, 2 * SEC * SLAB :].astype(F32)
        tile = split_rows(join_rows(acc, rows))
        for s in range(GRP):
            msg[s, NBLK * SLAB :] = tile


def gathered_totals(got, rows):
    acc = got[0, NBLK * SLAB :].astype(F32)
    for s in range(1, GRP):
        acc = acc + got[s, NBLK * SLAB :].astype(F32)
    return [total(r) for r in join_rows(acc, rows)]


def assemble(got, out):
    for s in range(GRP):
        for pair in range(NBLK // 2):
            tile = got[s, 16 * pair : 16 * (pair + 1)].astype(F32)
            for k in range(2):
                out[2 * pair + k, SLAB * s : SLAB * (s + 1), :] = tile[SLAB * k : SLAB * (k + 1)]


def products(dims, blocks, left, right, msg, acc):
    _, z = core_and_z()
    rows = iota((W, W), 0)
    cols = iota((W, W), 1)
    for i in range(SEC):
        inner = []
        order = []
        for r in range(3):
            terms = list(range(r, TERMS_DEV, 3))
            vec = blocks[3 * i + lax.rem(z + r, 3)].astype(BF16)
            lhs = jnp.concatenate([left[i, w] for w in terms], axis=0)
            got = jnp.dot(lhs, vec, preferred_element_type=F32).astype(BF16)
            inner += [got[W * n : W * (n + 1)] for n in range(len(terms))]
            order += terms
        lhs = jnp.concatenate(inner, axis=1)
        rhs = jnp.concatenate([right[i, w] for w in order], axis=0)
        out = jnp.dot(lhs, rhs, preferred_element_type=F32)
        inside = (rows < dims[i, 0]) & (cols < dims[i, 1])
        acc[i] = jnp.where(inside, out * SCALE, 0.0)
    for s in range(GRP):
        at = slice(SLAB * s, SLAB * (s + 1))
        for pair in range(SEC // 2):
            tile = jnp.concatenate([acc[2 * pair, at, :], acc[2 * pair + 1, at, :]], axis=0)
            msg[s, 16 * pair : 16 * (pair + 1)] = tile.astype(BF16)


def put_coefs(out, values):
    at = iota((8, W), 0)
    tile = jnp.zeros((8, W), F32)
    for k, v in enumerate(values):
        tile = jnp.where(at == k, jnp.broadcast_to(v, (8, W)), tile)
    out[...] = tile


def coef(ref, k):
    return ref[k : k + 1, 0:1]


def ham0_kernel(dims, got, left, right, msg, blk, acc):
    assemble(got, blk)
    products(dims, blk, left, right, msg, acc)


def ham1_kernel(dims, got, left, right, blk0, slab0, image0, msg, blk, v0, v1, coefs, acc):
    uu, uw, ww = gathered_totals(got, 3)
    assemble(got, blk)
    n2 = uu / COUNT + EPS
    inv = 1.0 / jnp.sqrt(n2)
    a0 = uw / n2 / COUNT
    rr = (ww - 2.0 * a0 * uw + a0 * a0 * uu) / n2
    b1 = jnp.sqrt(jnp.maximum(rr, 0.0) / COUNT + EPS)
    wc = inv / b1
    vc = a0 * wc
    for n in range(NBLK):
        blk[n] = blk[n] * wc - blk0[n] * vc
    v0[...] = slab0[...] * inv
    v1[...] = image0[...] * wc - slab0[...] * vc
    put_coefs(coefs, (a0, b1, inv))
    products(dims, blk, left, right, msg, acc)


def ham2_kernel(
    dims, got, left, right, blk1, blk0, slab1, rest1, old, msg, own, v2, coefs, blk, acc
):
    vw, vr, rr, vv = gathered_totals(got, 4)
    assemble(got, blk)
    a0, b1, inv = coef(old, 0), coef(old, 1), coef(old, 2)
    a1 = vw / COUNT
    d = a1 - a0
    rest = rr - 2.0 * d * vr + d * d * vv
    b2 = jnp.sqrt(jnp.maximum(rest, 0.0) / COUNT + EPS)
    wc = 1.0 / b2
    vc = a1 * wc
    pc = b1 * inv * wc
    for n in range(NBLK):
        blk[n] = blk[n] * wc - blk1[n] * vc - blk0[n] * pc
    for i in range(SEC):
        own[i] = blk[3 * i + 1]
    v2[...] = (rest1[...] - d * slab1[...]) * wc
    put_coefs(coefs, (a0, a1, b1, b2))
    products(dims, blk, left, right, msg, acc)


def reduced(got):
    parts = []
    for c in range(2):
        acc = got[c * NZ].astype(F32)
        for z in range(1, NZ):
            acc = acc + got[c * NZ + z].astype(F32)
        parts.append(acc)
    return jnp.concatenate(parts, axis=0)


def spread(msg, image, rows):
    msg_rows = 2 * SEC * SLAB
    rounded = image.astype(BF16)
    tile = split_rows(rows)
    for n in range(CHIPS):
        msg[n, :msg_rows] = rounded
        msg[n, msg_rows:] = tile


def reduce0_kernel(got, slab0, msg, image0):
    image = reduced(got)
    image0[...] = image
    vec = slab0[...]
    spread(msg, image, [row_sum(vec * vec), row_sum(vec * image), row_sum(image * image)])


def inner_rows(vec, image, rest):
    return [row_sum(vec * image), row_sum(vec * rest), row_sum(rest * rest), row_sum(vec * vec)]


def reduce1_kernel(got, v1, v0, coefs, msg, rest1):
    image = reduced(got)
    vec = v1[...]
    rest = image - coef(coefs, 1) * v0[...] - coef(coefs, 0) * vec
    rest1[...] = rest
    spread(msg, image, inner_rows(vec, image, rest))


def reduce2_kernel(got, v2, v1, coefs, msg):
    image = reduced(got)
    vec = v2[...]
    rest = image - coef(coefs, 3) * v1[...] - coef(coefs, 1) * vec
    half = SEC * SLAB
    rows = inner_rows(vec, image, rest)
    at = iota((8, W), 0)
    tile = jnp.zeros((8, W), F32)
    for k, row in enumerate(rows):
        tile = jnp.where(at == k, jnp.broadcast_to(row, (8, W)), tile)
    for c in range(2):
        for z in range(NZ):
            msg[c * NZ + z, :half] = rest[half * c : half * (c + 1)]
            msg[c * NZ + z, half:] = tile


def sums_kernel(got, msg):
    half = SEC * SLAB
    acc = got[0, half:]
    for s in range(1, GRP):
        acc = acc + got[s, half:]
    for n in range(CHIPS):
        msg[n] = acc


def finish_kernel(got, sums, own, coefs, vec_out, coef_out, dens_out):
    acc = sums[0]
    for n in range(1, CHIPS):
        acc = acc + sums[n]
    vw, vr, rr, vv = [total(acc[k : k + 1]) for k in range(4)]
    a0, a1, b1, b2 = [coef(coefs, k) for k in range(4)]
    a2 = vw / COUNT
    d = a2 - a1
    rest = rr - 2.0 * d * vr + d * d * vv
    b3 = jnp.sqrt(jnp.maximum(rest, 0.0) / COUNT + EPS)
    put_coefs(coef_out, (a0, a1, a2, b1, b2, b3))
    wc = 1.0 / b3
    vc = d * wc
    for i in range(SEC):
        for s in range(GRP):
            at = slice(SLAB * s, SLAB * (s + 1))
            vec_out[i, at, :] = got[s, SLAB * i : SLAB * (i + 1)] * wc - own[i, at, :] * vc
        v = vec_out[i]
        dens_out[i] = (
            lax.dot_general(
                v, v, (((1,), (1,)), ((), ())), precision=lax.Precision.HIGHEST, preferred_element_type=F32
            )
            / W
        )


def over_cz(x):
    return lax.all_to_all(x, BOTH, 0, 0, axis_index_groups=CZ_GROUPS)


def over_xy(x):
    return lax.all_to_all(x, "sector", 0, 0, axis_index_groups=XY_GROUPS)


def select(rows, got, src):
    extra = 16 if rows else 0
    return call(
        lambda *refs: select_kernel(rows, *refs),
        [((GRP, NBLK * SLAB + extra, W), BF16)],
        [SMEM, VMEM],
        [pltpu.VMEM((8 * SEC * GRP * 2, W), F32)],
    )(src, got)[0]


def per_device(theta, left, right, perm, dims):
    half = (SEC * SLAB, W)
    slab = (2 * SEC * SLAB, W)
    scatter = ((GRP, SEC * SLAB, W), BF16)
    plane = ((CHIPS, 2 * SEC * SLAB + 16, W), BF16)
    blocks = ((NBLK, W, W), F32)
    acc = [pltpu.VMEM((SEC, W, W), F32)]
    coefs = ((8, W), F32)
    flops = 2 * 2 * SEC * TERMS_DEV * W**3
    nbytes = 6 << 20

    src = pl.pallas_call(
        source_kernel,
        out_shape=jax.ShapeDtypeStruct((6 * SEC,), jnp.int32),
        in_specs=[SMEM],
        out_specs=SMEM,
        scratch_shapes=[pltpu.SMEM((128,), jnp.int32)],
    )(perm)

    keep, send = call(start_kernel, [(half, F32)] * 2, [SMEM, VMEM])(dims, theta)
    came = lax.ppermute(send, "sector", SWAP)
    msg, slab0 = call(
        spread_start_kernel, [((CHIPS, 2 * SEC * SLAB, W), BF16), (slab, F32)], [VMEM, VMEM]
    )(keep, came)
    got = over_cz(select(0, over_xy(msg), src))
    msg, blk0 = call(
        ham0_kernel, [scatter, blocks], [SMEM, VMEM, VMEM, VMEM], acc, flops, nbytes
    )(dims, got, left, right)
    msg, image0 = call(reduce0_kernel, [plane, (slab, F32)], [VMEM] * 2)(over_cz(msg), slab0)

    got = over_cz(select(3, over_xy(msg), src))
    msg, blk1, v0, v1, co = call(
        ham1_kernel,
        [scatter, blocks, (slab, F32), (slab, F32), coefs],
        [SMEM] + [VMEM] * 6,
        acc,
        flops,
        nbytes,
    )(dims, got, left, right, blk0, slab0, image0)
    msg, rest1 = call(reduce1_kernel, [plane, (slab, F32)], [VMEM] * 4)(over_cz(msg), v1, v0, co)

    got = over_cz(select(4, over_xy(msg), src))
    msg, own, v2, co = call(
        ham2_kernel,
        [scatter, ((SEC, W, W), F32), (slab, F32), coefs],
        [SMEM] + [VMEM] * 8,
        [pltpu.VMEM((NBLK, W, W), F32)] + acc,
        flops,
        nbytes,
    )(dims, got, left, right, blk1, blk0, v1, rest1, co)
    (msg,) = call(reduce2_kernel, [((GRP, SEC * SLAB + 8, W), F32)], [VMEM] * 4)(
        over_cz(msg), v2, v1, co
    )

    got = over_cz(msg)
    (msg,) = call(sums_kernel, [((CHIPS, 8, W), F32)], [VMEM])(got)
    vec, coef_tile, dens = call(
        finish_kernel, [((SEC, W, W), F32), coefs, ((SEC, W, W), F32)], [VMEM] * 4
    )(got, over_xy(msg), own, co)
    return vec, coef_tile[:6, 0], dens


def solution(mesh):
    placed = (
        P("sector", None, None),
        P("sector", "op", None, None),
        P("sector", "op", None, None),
        P(),
        P("sector", None),
    )
    return jax.shard_map(
        per_device,
        mesh=mesh,
        in_specs=placed,
        out_specs=(P("sector", None, None), P(), P("sector", None, None)),
        check_vma=False,
    )
```

time: 878 us -> 181 us (0.21)
  waiting for transfers between devices: 339 us -> 5.94 us
  blocking collectives: 459 us -> 145 us
  matrix products: 36.3 us -> 0 us
  other arithmetic: 19.5 us -> 0 us
  between operations: 18.9 us -> 0.73 us
  Pallas kernels: 0 us -> 13.9 us
    psum x7 -> x0, blocking collectives: 459 us -> none  [the longest x4 256 us: sq_sum(): return lax.psum(jnp.sum(first * first), 'sector')]
    psum x3 -> x0, waiting for transfers between devices: 201 us -> none  [per_device(): image = lax.psum(partial_sum, 'op') * scale * mask]
    all_to_all x0 -> x10, blocking collectives: none -> 145 us  [the longest x7 114 us: over_cz(): return lax.all_to_all(x, BOTH, 0, 0, axis_index_groups=CZ_GROUPS)]
    all_gather x3 -> x0, waiting for transfers between devices: 138 us -> none  [per_device(): lax.all_gather(vector.astype(jnp.bfloat16), 'sector', axis=0, tiled=True)]
    dot_general x10 -> x0, matrix products: 36.3 us -> none  [the longest x3 15 us: term_products(): jnp.einsum('pwik,pwkl->pil', inner, right_env, preferred_element_type=jnp...]
    pallas_call x0 -> x14, Pallas kernels: none -> 13.9 us  [the longest x1 2.47 us: per_device(): pl.pallas_call(source_kernel, out_shape=jax.ShapeDtypeStruct((6 * SEC,),...]
    reduce_sum x7 -> x0, other arithmetic: 11.9 us -> none  [the longest x4 6.82 us: sq_sum(): return lax.psum(jnp.sum(first * first), 'sector')]
  transfers between devices with their start and end apart: 6 -> 2, of which waited for: 6 -> 2; matrix products, arithmetic and copies ran while one was open for 1% -> 0% of each run, Pallas kernels for 0% -> 1%
where the time goes in v1:
time: 181 us; the launch traced here: 179 us
  blocking collectives  145 us (80%)
  Pallas kernels  13.9 us (8%)
  starting transfers between devices  8.35 us (5%)
  waiting for transfers between devices  5.94 us (3%)
  local copies, waits for them, and re-layouts  4.75 us (3%)
    all_to_all x7, blocking collectives, over_cz(): return lax.all_to_all(x, BOTH, 0, 0, axis_index_groups=CZ_GROUPS)  114 us
    all_to_all x3, blocking collectives, over_xy(): return lax.all_to_all(x, 'sector', 0, 0, axis_index_groups=XY_GROUPS)  31.5 us
    all_to_all x1, waiting for transfers between devices, over_xy(): return lax.all_to_all(x, 'sector', 0, 0, axis_index_groups=XY_GROUPS)  5.1 us
    all_to_all x1, starting transfers between devices, over_xy(): return lax.all_to_all(x, 'sector', 0, 0, axis_index_groups=XY_GROUPS)  5.02 us
    unnamed x13, local copies, waits for them, and re-layouts  4.12 us
  transfers between devices with their start and end apart: 2, of which 2 were waited for; matrix products, arithmetic and copies ran while one was open for 0% of the time, Pallas kernels for 1%

profile of v1, /device:TPU:1, one launch (start us, length us, event | category | flops | bytes accessed | tf_op | source)
XLA Modules:
  0.0 178.8 jit_solution(6730111993987508769)
XLA Ops:
  0.6 0.0 copy-start
  0.6 0.9 copy.15.dims
  1.6 0.0 copy-start.3
  1.6 0.9 copy-done.3
  2.5 0.6 shard_map.77
  3.1 3.3 %collective-permute-start = (f32[32,128]{1,0:T(8,128)S(1)}, f32[32,128]{1,0:T(8,128)S(1)}, u32[]{:S(2)}, u32[]{:S(2)}) collective-permute-start(f32[32,128]{1,0:T(8,128)S(1)} %get-tuple-element.26), channel_id=1, source_target_pairs={{0,8},{8,0},{16,24},{24,16},{32,40},{40,32},{48,56},{56,48},{64,72... | collective-permute-start | bytes 49160 | tf_op jit(solution)/shard_map/ppermute | solution.py:366
  6.4 0.8 collective-permute-done.came
  7.3 0.7 shard_map.78
  8.0 5.0 %all-to-all-start = ((bf16[16,64,128]{2,1,0:T(8,128)(2,1)}), bf16[16,64,128]{2,1,0:T(8,128)(2,1)S(1)}, u32[]{:S(2)}, u32[]{:S(2)}) async-start(bf16[16,64,128]{2,1,0:T(8,128)(2,1)} %get-tuple-element.27), calls=%async_computation | async-start | bytes 524288 | tf_op jit(solution)/shard_map/all_to_all | solution.py:333
  13.0 2.5 %shard_map.76.refs_0_ = s32[24]{0:T(128)} custom-call(s32[128]{0:T(128)} %perm.1), custom_call_target="tpu_custom_call" | custom-call | tf_op jit(solution)/shard_map/pallas_call | solution.py:357
  15.5 5.1 %all-to-all-done.refs_1_ = bf16[16,64,128]{2,1,0:T(8,128)(2,1)S(1)} async-done(((bf16[16,64,128]{2,1,0:T(8,128)(2,1)}), bf16[16,64,128]{2,1,0:T(8,128)(2,1)S(1)}, u32[]{:S(2)}, u32[]{:S(2)}) %all-to-all-start) | async-done | bytes 262176 | tf_op jit(solution)/shard_map/all_to_all | solution.py:333
  20.6 0.0 copy-start.4
  20.6 0.7 copy-done.4
  21.3 0.6 shard_map.79
  21.9 22.6 %all_to_all.55.got = bf16[16,96,128]{2,1,0:T(8,128)(2,1)S(1)} all-to-all(bf16[16,96,128]{2,1,0:T(8,128)(2,1)S(1)} %shard_map.79), channel_id=1, replica_groups={{0,1,2,3,4,5,6,7,8,9,10,11,12,13,14,15},{16,17,18,19,20,21,22,23,24,25,..., dimensions={0} | all-to-all | bytes 786432 | tf_op jit(solution)/shard_map/all_to_all | solution.py:329
  44.5 0.0 copy-done
  44.5 0.0 copy-start.1
  44.5 1.6 copy-done.1
  46.1 2.0 %shard_map.80 = (bf16[16,32,128]{2,1,0:T(8,128)(2,1)S(1)}, f32[12,128,128]{2,1,0:T(8,128)S(1)}) custom-call(s32[4,2]{1,0:T(4,128)S(1)} %copy.15.dims, bf16[16,96,128]{2,1,0:T(8,128)(2,1)S(1)} %all_to_all.55.got, bf16[4,16,128,128]{3,2,1,0:T(8,128)(2,1)S(1)} %copy-done, bf16[4,16,128,128]{3,2,1,0:T(8,128)(2,1)S(1)} %copy-done.1), custom_call_target="tpu_custom_call" | custom-call | flops 536870912 | bytes 6291456 | tf_op jit(solution)/shard_map/pallas_call | solution.py:371
  48.1 0.0 copy-start.2
  48.1 12.2 %all_to_all.56.got = bf16[16,32,128]{2,1,0:T(8,128)(2,1)S(1)} all-to-all(bf16[16,32,128]{2,1,0:T(8,128)(2,1)S(1)} %get-tuple-element.28), channel_id=1, replica_groups={{0,1,2,3,4,5,6,7,8,9,10,11,12,13,14,15},{16,17,18,19,20,21,22,23,24,25,..., dimensions={0} | all-to-all | bytes 262144 | tf_op jit(solution)/shard_map/all_to_all | solution.py:329
  60.4 10.9 %all_to_all.57.refs_1_ = bf16[16,80,128]{2,1,0:T(8,128)(2,1)S(1)} all-to-all(bf16[16,80,128]{2,1,0:T(8,128)(2,1)S(1)} %get-tuple-element.30), channel_id=1, replica_groups={{0,16,32,48,64,80,96,112,128,144,160,176,192,208,224,240},{8,24,40,56,7..., dimensions={0} | all-to-all | bytes 655360 | tf_op jit(solution)/shard_map/all_to_all | solution.py:333
  71.3 0.6 shard_map.82
  71.9 19.6 %all_to_all.58.got = bf16[16,112,128]{2,1,0:T(8,128)(2,1)S(1)} all-to-all(bf16[16,112,128]{2,1,0:T(8,128)(2,1)S(1)} %shard_map.82), channel_id=1, replica_groups={{0,1,2,3,4,5,6,7,8,9,10,11,12,13,14,15},{16,17,18,19,20,21,22,23,24,25,..., dimensions={0} | all-to-all | bytes 917504 | tf_op jit(solution)/shard_map/all_to_all | solution.py:329
  91.5 0.0 copy-done.2
  91.5 0.0 copy-start.5
  91.5 2.2 %shard_map.83 = (bf16[16,32,128]{2,1,0:T(8,128)(2,1)S(1)}, f32[12,128,128]{2,1,0:T(8,128)S(1)}, f32[64,128]{1,0:T(8,128)S(1)}, f32[64,128]{1,0:T(8,128)S(1)}, f32[8,128]{1,0:T(8,128)S(1)}) custom-call(s32[4,2]{1,0:T(4,128)S(1)} %copy.15.dims, bf16[16,112,128]{2,1,0:T(8,128)(2,1)S(1)} %all_to_all.58.got, bf16[4,16,128,128]{3,2,1,0:T(8,128)(2,1)S(1)} %copy-done, ...), custom_call_target="tpu_custom_call" | custom-call | flops 536870912 | bytes 6291456 | tf_op jit(solution)/shard_map/pallas_call | solution.py:377
  93.7 12.3 %all_to_all.59.got = bf16[16,32,128]{2,1,0:T(8,128)(2,1)S(1)} all-to-all(bf16[16,32,128]{2,1,0:T(8,128)(2,1)S(1)} %get-tuple-element.33), channel_id=1, replica_groups={{0,1,2,3,4,5,6,7,8,9,10,11,12,13,14,15},{16,17,18,19,20,21,22,23,24,25,..., dimensions={0} | all-to-all | bytes 262144 | tf_op jit(solution)/shard_map/all_to_all | solution.py:329
  106.0 0.1 shard_map.84
  106.1 10.9 %all_to_all.60.refs_1_ = bf16[16,80,128]{2,1,0:T(8,128)(2,1)S(1)} all-to-all(bf16[16,80,128]{2,1,0:T(8,128)(2,1)S(1)} %get-tuple-element.37), channel_id=1, replica_groups={{0,16,32,48,64,80,96,112,128,144,160,176,192,208,224,240},{8,24,40,56,7..., dimensions={0} | all-to-all | bytes 655360 | tf_op jit(solution)/shard_map/all_to_all | solution.py:333
  117.0 0.0 copy-done.5
  117.0 0.6 shard_map.85
  117.7 19.6 %all_to_all.61.got = bf16[16,112,128]{2,1,0:T(8,128)(2,1)S(1)} all-to-all(bf16[16,112,128]{2,1,0:T(8,128)(2,1)S(1)} %shard_map.85), channel_id=1, replica_groups={{0,1,2,3,4,5,6,7,8,9,10,11,12,13,14,15},{16,17,18,19,20,21,22,23,24,25,..., dimensions={0} | all-to-all | bytes 917504 | tf_op jit(solution)/shard_map/all_to_all | solution.py:329
  137.3 2.3 %shard_map.86 = (bf16[16,32,128]{2,1,0:T(8,128)(2,1)S(1)}, f32[4,128,128]{2,1,0:T(8,128)S(1)}, f32[64,128]{1,0:T(8,128)S(1)}, f32[8,128]{1,0:T(8,128)S(1)}) custom-call(s32[4,2]{1,0:T(4,128)S(1)} %copy.15.dims, bf16[16,112,128]{2,1,0:T(8,128)(2,1)S(1)} %all_to_all.61.got, bf16[4,16,128,128]{3,2,1,0:T(8,128)(2,1)S(1)} %copy-done, ...), custom_call_target="tpu_custom_call" | custom-call | flops 536870912 | bytes 6291456 | tf_op jit(solution)/shard_map/pallas_call | solution.py:388
  139.6 12.3 %all_to_all.62.got = bf16[16,32,128]{2,1,0:T(8,128)(2,1)S(1)} all-to-all(bf16[16,32,128]{2,1,0:T(8,128)(2,1)S(1)} %get-tuple-element.40), channel_id=1, replica_groups={{0,1,2,3,4,5,6,7,8,9,10,11,12,13,14,15},{16,17,18,19,20,21,22,23,24,25,..., dimensions={0} | all-to-all | bytes 262144 | tf_op jit(solution)/shard_map/all_to_all | solution.py:329
  151.9 0.1 shard_map.87
  152.0 15.0 %all_to_all.63.got = f32[16,40,128]{2,1,0:T(8,128)S(1)} all-to-all(f32[16,40,128]{2,1,0:T(8,128)S(1)} %shard_map.87), channel_id=1, replica_groups={{0,1,2,3,4,5,6,7,8,9,10,11,12,13,14,15},{16,17,18,19,20,21,22,23,24,25,..., dimensions={0} | all-to-all | bytes 655360 | tf_op jit(solution)/shard_map/all_to_all | solution.py:329
  167.0 9.7 %all_to_all.64.sums = f32[16,8,128]{2,1,0:T(8,128)S(1)} all-to-all(f32[16,8,128]{2,1,0:T(8,128)S(1)} %shard_map.88), channel_id=1, replica_groups={{0,16,32,48,64,80,96,112,128,144,160,176,192,208,224,240},{8,24,40,56,7..., dimensions={0} | all-to-all | bytes 131072 | tf_op jit(solution)/shard_map/all_to_all | solution.py:333
  176.7 1.5 shard_map.89
  178.2 0.6 slice_reduce_fusion
  (2 shorter events, 0.1 us)
Async XLA Ops:
  0.6 43.8 %copy-start = (bf16[4,16,128,128]{3,2,1,0:T(8,128)(2,1)S(1)}, bf16[4,16,128,128]{3,2,1,0:T(8,128)(2,1)}, u32[]{:S(2)}) copy-start(bf16[4,16,128,128]{3,2,1,0:T(8,128)(2,1)} %left.5) | copy-start | bytes 6291460
  1.6 0.9 copy-start.3
  3.1 4.2 %collective-permute-start = (f32[32,128]{1,0:T(8,128)S(1)}, f32[32,128]{1,0:T(8,128)S(1)}, u32[]{:S(2)}, u32[]{:S(2)}) collective-permute-start(f32[32,128]{1,0:T(8,128)S(1)} %get-tuple-element.26), channel_id=1, source_target_pairs={{0,8},{8,0},{16,24},{24,16},{32,40},{40,32},{48,56},{56,48},{64,72... | collective-permute-start | bytes 49160 | tf_op jit(solution)/shard_map/ppermute | solution.py:366
  8.0 12.6 %all-to-all-start = ((bf16[16,64,128]{2,1,0:T(8,128)(2,1)}), bf16[16,64,128]{2,1,0:T(8,128)(2,1)S(1)}, u32[]{:S(2)}, u32[]{:S(2)}) async-start(bf16[16,64,128]{2,1,0:T(8,128)(2,1)} %get-tuple-element.27), calls=%async_computation | async-start | bytes 524288 | tf_op jit(solution)/shard_map/all_to_all | solution.py:333
  20.6 0.7 copy-start.4
  44.5 1.6 copy-start.1
  48.1 43.4 %copy-start.2 = (bf16[4,16,128,128]{3,2,1,0:T(8,128)(2,1)S(1)}, bf16[4,16,128,128]{3,2,1,0:T(8,128)(2,1)}, u32[]{:S(2)}) copy-start(bf16[4,16,128,128]{3,2,1,0:T(8,128)(2,1)} %right.5) | copy-start | bytes 6291460
  91.5 25.5 %copy-start.5 = (s32[24]{0:T(128)S(1)}, s32[24]{0:T(128)}, u32[]{:S(2)}) copy-start(s32[24]{0:T(128)} %shard_map.76.refs_0_) | copy-start | bytes 292

commit v2 on v1

--- a/solution.py
+++ b/solution.py
@@ -33,14 +33,14 @@
     return lax.rem(lax.axis_index("sector"), 2), lax.axis_index("op")
 
 
-def call(body, outs, specs, scratch=(), flops=0, nbytes=1 << 18):
+def call(body, outs, specs, scratch=(), flops=0, nbytes=1 << 18, out_specs=None, limit=8):
     return pl.pallas_call(
         body,
         out_shape=[jax.ShapeDtypeStruct(s, d) for s, d in outs],
         in_specs=specs,
-        out_specs=[VMEM] * len(outs),
+        out_specs=out_specs or [VMEM] * len(outs),
         scratch_shapes=list(scratch),
-        compiler_params=pltpu.CompilerParams(vmem_limit_bytes=32 * 1024 * 1024),
+        compiler_params=pltpu.CompilerParams(vmem_limit_bytes=limit << 20),
         cost_estimate=pl.CostEstimate(flops=flops, bytes_accessed=nbytes, transcendentals=0),
     )
 
@@ -73,34 +73,80 @@
     return jnp.sum(row, axis=1, keepdims=True)
 
 
-def start_kernel(dims, theta, keep, send):
+def low_high(low, high):
+    first = iota((SLAB, W), 0) < 4
+    return (
+        jnp.where(first, low, pltpu.roll(high, 4, 0)),
+        jnp.where(first, pltpu.roll(low, 4, 0), high),
+    )
+
+
+def start_kernel(theta, dims, msg, keep, send, held, sizes, sems):
+    size_copy = pltpu.make_async_copy(dims, sizes, sems.at[SEC])
+    copies = [pltpu.make_async_copy(theta.at[i], held.at[i], sems.at[i]) for i in range(SEC)]
+    size_copy.start()
+    for copy in copies:
+        copy.start()
+    size_copy.wait()
+    rows = iota((W, W), 0)
+    cols = iota((W, W), 1)
+    for i in range(SEC):
+        copies[i].wait()
+        inside = (rows < sizes[0, i]) & (cols < sizes[1, i])
+        held[i] = jnp.where(inside, held[i], 0.0)
+    for t in range(GRP):
+        tiles = [held[i, SLAB * t : SLAB * (t + 1), :] for i in range(SEC)]
+        even0, odd0 = low_high(tiles[0], tiles[1])
+        even1, odd1 = low_high(tiles[2], tiles[3])
+        msg[2 * t] = jnp.concatenate([even0, even1], axis=0).astype(BF16)
+        msg[2 * t + 1] = jnp.concatenate([odd0, odd1], axis=0).astype(BF16)
     c, z = core_and_z()
     for slot, out in ((c * NZ + z, keep), ((1 - c) * NZ + z, send)):
         first = pl.multiple_of(slot * SLAB, SLAB)
-        rows = iota((SLAB, W), 0) + first
-        cols = iota((SLAB, W), 1)
         for i in range(SEC):
-            inside = (rows < dims[i, 0]) & (cols < dims[i, 1])
-            out[SLAB * i : SLAB * (i + 1), :] = jnp.where(inside, theta[i, pl.ds(first, SLAB), :], 0.0)
-
-
-def spread_start_kernel(keep, came, msg, slab):
-    c, _ = core_and_z()
-    half = SEC * SLAB
-
-    @pl.when(c == 0)
-    def _():
-        slab[:half] = keep[...]
-        slab[half:] = came[...]
-
-    @pl.when(c == 1)
-    def _():
-        slab[:half] = came[...]
-        slab[half:] = keep[...]
-
-    rounded = slab[...].astype(BF16)
-    for n in range(CHIPS):
-        msg[n] = rounded
+            out[SLAB * i : SLAB * (i + 1), :] = held[i, pl.ds(first, SLAB), :]
+
+
+def load_kernel(array, held, sems):
+    copies = [pltpu.make_async_copy(array.at[i], held.at[i], sems.at[i]) for i in range(SEC)]
+    for copy in copies:
+        copy.start()
+    for copy in copies:
+        copy.wait()
+
+
+def hits_kernel(perm, hits):
+    shape = (3 * W, W)
+    row = iota(shape, 0)
+    at = lax.shift_right_logical(row * 21846, 16)
+    q = row - 3 * at
+    held = jnp.broadcast_to(perm[...], shape)
+    mine = jnp.sum(jnp.where(iota(shape, 1) == at, held, 0.0), axis=1, keepdims=True)
+    want = mine + q.astype(F32) - 1.0
+    want = jnp.where(want < 0.0, want + 128.0, want)
+    want = jnp.where(want > 127.0, want - 128.0, want)
+    hits[...] = (held == want).astype(F32).astype(BF16)
+
+
+def pick_kernel(got, hits, src, came, held, msg, pieces, picked):
+    for g in range(2 * CHIPS):
+        pieces[16 * g : 16 * (g + 1)] = got[g].astype(F32)
+    for r in range(4):
+        part = pieces[pl.ds(r, W, stride=4), :].astype(BF16)
+        picked[pl.ds(r, 3 * W, stride=4), :] = jnp.dot(hits[...], part, preferred_element_type=F32)
+    for g in range(2 * CHIPS):
+        msg[g] = picked[48 * g : 48 * (g + 1)].astype(BF16)
+
+
+def assemble_pieces(got, out):
+    for t in range(GRP):
+        low = got[2 * t].astype(F32)
+        high = got[2 * t + 1].astype(F32)
+        for m in range(NBLK // 2):
+            at = slice(SLAB * m, SLAB * (m + 1))
+            two = low_high(low[at], high[at])
+            for k in range(2):
+                out[2 * m + k, SLAB * t : SLAB * (t + 1), :] = two[k]
 
 
 def source_kernel(perm, src, pos):
@@ -117,15 +163,16 @@
             src[3 * n + q] = pos[lax.rem(mine + (q + 127), 128)]
 
 
-def select_kernel(rows, src, got, msg, blocks):
-    for n in range(CHIPS):
-        blocks[2 * SEC * SLAB * n : 2 * SEC * SLAB * (n + 1)] = got[n, : 2 * SEC * SLAB].astype(F32)
+def select_kernel(rows, src, got, msg):
     for c in range(2):
         for pair in range(NBLK // 2):
-            two = [
-                blocks[pl.ds(pl.multiple_of(src[NBLK * c + 2 * pair + k] * SLAB, SLAB), SLAB), :]
-                for k in range(2)
-            ]
+            two = []
+            for k in range(2):
+                at = src[NBLK * c + 2 * pair + k]
+                inner = lax.bitwise_and(at, 7)
+                first = pl.multiple_of(lax.shift_right_logical(inner, 1) * 16, 16)
+                tile = got[lax.shift_right_logical(at, 3), pl.ds(first, 16), :].astype(F32)
+                two.append(jnp.where(lax.bitwise_and(inner, 1) == 1, tile[SLAB:], tile[:SLAB]))
             tile = jnp.concatenate(two, axis=0).astype(BF16)
             for z in range(NZ):
                 msg[c * NZ + z, 16 * pair : 16 * (pair + 1)] = tile
@@ -170,7 +217,7 @@
         lhs = jnp.concatenate(inner, axis=1)
         rhs = jnp.concatenate([right[i, w] for w in order], axis=0)
         out = jnp.dot(lhs, rhs, preferred_element_type=F32)
-        inside = (rows < dims[i, 0]) & (cols < dims[i, 1])
+        inside = (rows < dims[0, i]) & (cols < dims[1, i])
         acc[i] = jnp.where(inside, out * SCALE, 0.0)
     for s in range(GRP):
         at = slice(SLAB * s, SLAB * (s + 1))
@@ -192,7 +239,7 @@
 
 
 def ham0_kernel(dims, got, left, right, msg, blk, acc):
-    assemble(got, blk)
+    assemble_pieces(got, blk)
     products(dims, blk, left, right, msg, acc)
 
 
@@ -255,9 +302,13 @@
         msg[n, msg_rows:] = tile
 
 
-def reduce0_kernel(got, slab0, msg, image0):
+def reduce0_kernel(got, keep, came, msg, image0, slab0):
+    c, _ = core_and_z()
     image = reduced(got)
     image0[...] = image
+    half = SEC * SLAB
+    slab0[:half] = jnp.where(c == 0, keep[...], came[...])
+    slab0[half:] = jnp.where(c == 0, came[...], keep[...])
     vec = slab0[...]
     spread(msg, image, [row_sum(vec * vec), row_sum(vec * image), row_sum(image * image)])
 
@@ -279,27 +330,28 @@
     vec = v2[...]
     rest = image - coef(coefs, 3) * v1[...] - coef(coefs, 1) * vec
     half = SEC * SLAB
-    rows = inner_rows(vec, image, rest)
+    tile = split_rows(inner_rows(vec, image, rest))
+    for c in range(2):
+        rounded = rest[half * c : half * (c + 1)].astype(BF16)
+        for z in range(NZ):
+            msg[c * NZ + z, :half] = rounded
+            msg[c * NZ + z, half:] = tile
+
+
+def sums_kernel(got, msg):
+    half = SEC * SLAB
+    acc = got[0, half:].astype(F32)
+    for s in range(1, GRP):
+        acc = acc + got[s, half:].astype(F32)
     at = iota((8, W), 0)
     tile = jnp.zeros((8, W), F32)
-    for k, row in enumerate(rows):
+    for k, row in enumerate(join_rows(acc, 4)):
         tile = jnp.where(at == k, jnp.broadcast_to(row, (8, W)), tile)
-    for c in range(2):
-        for z in range(NZ):
-            msg[c * NZ + z, :half] = rest[half * c : half * (c + 1)]
-            msg[c * NZ + z, half:] = tile
-
-
-def sums_kernel(got, msg):
-    half = SEC * SLAB
-    acc = got[0, half:]
-    for s in range(1, GRP):
-        acc = acc + got[s, half:]
     for n in range(CHIPS):
-        msg[n] = acc
-
-
-def finish_kernel(got, sums, own, coefs, vec_out, coef_out, dens_out):
+        msg[n] = tile
+
+
+def finish_kernel(got, sums, own, coefs, vec_out, coef_out, dens_out, rest2):
     acc = sums[0]
     for n in range(1, CHIPS):
         acc = acc + sums[n]
@@ -309,14 +361,18 @@
     d = a2 - a1
     rest = rr - 2.0 * d * vr + d * d * vv
     b3 = jnp.sqrt(jnp.maximum(rest, 0.0) / COUNT + EPS)
-    put_coefs(coef_out, (a0, a1, a2, b1, b2, b3))
+    for k, v in enumerate((a0, a1, a2, b1, b2, b3)):
+        coef_out[k] = v[0, 0]
     wc = 1.0 / b3
     vc = d * wc
+    for s in range(GRP):
+        for pair in range(SEC // 2):
+            tile = got[s, 16 * pair : 16 * (pair + 1)].astype(F32)
+            for k in range(2):
+                rest2[2 * pair + k, SLAB * s : SLAB * (s + 1), :] = tile[SLAB * k : SLAB * (k + 1)]
     for i in range(SEC):
-        for s in range(GRP):
-            at = slice(SLAB * s, SLAB * (s + 1))
-            vec_out[i, at, :] = got[s, SLAB * i : SLAB * (i + 1)] * wc - own[i, at, :] * vc
-        v = vec_out[i]
+        v = rest2[i] * wc - own[i] * vc
+        vec_out[i] = v
         dens_out[i] = (
             lax.dot_general(
                 v, v, (((1,), (1,)), ((), ())), precision=lax.Precision.HIGHEST, preferred_element_type=F32
@@ -339,7 +395,6 @@
         lambda *refs: select_kernel(rows, *refs),
         [((GRP, NBLK * SLAB + extra, W), BF16)],
         [SMEM, VMEM],
-        [pltpu.VMEM((8 * SEC * GRP * 2, W), F32)],
     )(src, got)[0]
 
 
@@ -354,24 +409,49 @@
     flops = 2 * 2 * SEC * TERMS_DEV * W**3
     nbytes = 6 << 20
 
-    src = pl.pallas_call(
+    dims = dims.T
+    any_space = pl.BlockSpec(memory_space=pl.ANY)
+    pieces = 2 * CHIPS
+    sems = pltpu.SemaphoreType.DMA((SEC + 1,))
+
+    msg, keep, send = call(
+        start_kernel,
+        [((pieces, 16, W), BF16), (half, F32), (half, F32)],
+        [any_space, any_space],
+        [pltpu.VMEM((SEC, W, W), F32), pltpu.SMEM((2, SEC), jnp.int32), sems],
+        limit=60,
+    )(theta, dims)
+    got = lax.all_to_all(msg, "sector", 0, 0)
+    (hits,) = call(hits_kernel, [((3 * W, W), BF16)], [VMEM])(perm.astype(F32).reshape(1, W))
+    (src,) = call(
         source_kernel,
-        out_shape=jax.ShapeDtypeStruct((6 * SEC,), jnp.int32),
-        in_specs=[SMEM],
-        out_specs=SMEM,
-        scratch_shapes=[pltpu.SMEM((128,), jnp.int32)],
+        [((6 * SEC,), jnp.int32)],
+        [SMEM],
+        [pltpu.SMEM((128,), jnp.int32)],
+        out_specs=[SMEM],
+        limit=1,
     )(perm)
-
-    keep, send = call(start_kernel, [(half, F32)] * 2, [SMEM, VMEM])(dims, theta)
+    (right,) = call(load_kernel, [((SEC, TERMS_DEV, W, W), BF16)], [any_space], [sems])(right)
     came = lax.ppermute(send, "sector", SWAP)
-    msg, slab0 = call(
-        spread_start_kernel, [((CHIPS, 2 * SEC * SLAB, W), BF16), (slab, F32)], [VMEM, VMEM]
-    )(keep, came)
-    got = over_cz(select(0, over_xy(msg), src))
+    (msg,) = call(
+        pick_kernel,
+        [((pieces, 4 * NBLK, W), BF16)],
+        [VMEM, VMEM, SMEM, any_space, any_space],
+        [pltpu.VMEM((pieces * 16, W), F32), pltpu.VMEM((pieces * 4 * NBLK, W), F32)],
+    )(got, hits, src, came, right)
+    got = lax.all_to_all(msg, "sector", 0, 0)
     msg, blk0 = call(
-        ham0_kernel, [scatter, blocks], [SMEM, VMEM, VMEM, VMEM], acc, flops, nbytes
+        ham0_kernel,
+        [scatter, blocks],
+        [SMEM, VMEM, VMEM, VMEM],
+        acc,
+        flops,
+        nbytes,
+        limit=16,
     )(dims, got, left, right)
-    msg, image0 = call(reduce0_kernel, [plane, (slab, F32)], [VMEM] * 2)(over_cz(msg), slab0)
+    msg, image0, slab0 = call(reduce0_kernel, [plane, (slab, F32), (slab, F32)], [VMEM] * 3)(
+        over_cz(msg), keep, came
+    )
 
     got = over_cz(select(3, over_xy(msg), src))
     msg, blk1, v0, v1, co = call(
@@ -381,6 +461,7 @@
         acc,
         flops,
         nbytes,
+        limit=16,
     )(dims, got, left, right, blk0, slab0, image0)
     msg, rest1 = call(reduce1_kernel, [plane, (slab, F32)], [VMEM] * 4)(over_cz(msg), v1, v0, co)
 
@@ -392,17 +473,21 @@
         [pltpu.VMEM((NBLK, W, W), F32)] + acc,
         flops,
         nbytes,
+        limit=16,
     )(dims, got, left, right, blk1, blk0, v1, rest1, co)
-    (msg,) = call(reduce2_kernel, [((GRP, SEC * SLAB + 8, W), F32)], [VMEM] * 4)(
+    (msg,) = call(reduce2_kernel, [((GRP, SEC * SLAB + 16, W), BF16)], [VMEM] * 4)(
         over_cz(msg), v2, v1, co
     )
 
     got = over_cz(msg)
     (msg,) = call(sums_kernel, [((CHIPS, 8, W), F32)], [VMEM])(got)
-    vec, coef_tile, dens = call(
-        finish_kernel, [((SEC, W, W), F32), coefs, ((SEC, W, W), F32)], [VMEM] * 4
+    return call(
+        finish_kernel,
+        [((SEC, W, W), F32), ((6,), F32), ((SEC, W, W), F32)],
+        [VMEM] * 4,
+        acc,
+        out_specs=[VMEM, SMEM, VMEM],
     )(got, over_xy(msg), own, co)
-    return vec, coef_tile[:6, 0], dens
 
 
 def solution(mesh):

time: 181 us -> 170 us (0.939)
  blocking collectives: 145 us -> 139 us
  waiting for transfers between devices: 5.94 us -> 1.66 us
  local copies, waits for them, and re-layouts: 4.75 us -> 2.25 us
    all_to_all x7 -> x6, blocking collectives: 114 us -> 92.1 us  [over_cz(): return lax.all_to_all(x, BOTH, 0, 0, axis_index_groups=CZ_GROUPS)]
    all_to_all x0 -> x1, blocking collectives: none -> 15.8 us  [per_device(): got = lax.all_to_all(msg, 'sector', 0, 0)]
    all_to_all x1, starting transfers between devices: 5.02 us -> 8.6 us  [per_device(): got = lax.all_to_all(msg, 'sector', 0, 0)]
    all_to_all x1, waiting for transfers between devices: 5.1 us -> 1.66 us  [per_device(): got = lax.all_to_all(msg, 'sector', 0, 0)]
    ppermute x1, starting transfers between devices: 3.33 us -> 0.32 us  [per_device(): came = lax.ppermute(send, 'sector', SWAP)]
    unnamed x13 -> x10, local copies, waits for them, and re-layouts: 4.12 us -> 2.25 us
    pallas_call x6 -> x8, Pallas kernels: 5.41 us -> 6.94 us  [the longest x1 2.42 us: per_device(): call(source_kernel, [((6 * SEC,), jnp.int32)], [SMEM], [pltpu.SMEM((128,)...]
  transfers between devices with their start and end apart: 2 -> 2, of which waited for: 2 -> 1; matrix products, arithmetic and copies ran while one was open for 0% -> 0% of each run, Pallas kernels for 1% -> 2%
where the time goes in v2:
time: 170 us; the launch traced here: 168 us
  blocking collectives  139 us (82%)
  Pallas kernels  14.8 us (9%)
  starting transfers between devices  8.92 us (5%)
  local copies, waits for them, and re-layouts  2.25 us (1%)
    all_to_all x6, blocking collectives, over_cz(): return lax.all_to_all(x, BOTH, 0, 0, axis_index_groups=CZ_GROUPS)  92.1 us
    all_to_all x3, blocking collectives, over_xy(): return lax.all_to_all(x, 'sector', 0, 0, axis_index_groups=XY_GROUPS)  31.3 us
    all_to_all x1, blocking collectives, per_device(): got = lax.all_to_all(msg, 'sector', 0, 0)  15.8 us
    all_to_all x1, starting transfers between devices, per_device(): got = lax.all_to_all(msg, 'sector', 0, 0)  8.6 us
  transfers between devices with their start and end apart: 2, of which 1 were waited for; matrix products, arithmetic and copies ran while one was open for 0% of the time, Pallas kernels for 2%

profile of v2, /device:TPU:1, one launch (start us, length us, event | category | flops | bytes accessed | tf_op | source)
XLA Modules:
  0.0 168.2 jit_solution(14407414109088235246)
XLA Ops:
  0.6 1.7 %shard_map.77 = (bf16[32,16,128]{2,1,0:T(8,128)(2,1)}, f32[32,128]{1,0:T(8,128)}, f32[32,128]{1,0:T(8,128)}) custom-call(f32[4,128,128]{2,1,0:T(8,128)} %theta.1, s32[2,4]{1,0:T(2,128)} %bitcast.3), custom_call_target="tpu_custom_call" | custom-call | bytes 262144 | tf_op jit(solution)/shard_map/pallas_call | solution.py:417
  2.3 8.6 %all-to-all-start = ((bf16[32,16,128]{2,1,0:T(8,128)(2,1)}), bf16[32,16,128]{2,1,0:T(8,128)(2,1)S(1)}, u32[]{:S(2)}, u32[]{:S(2)}) async-start(bf16[32,16,128]{2,1,0:T(8,128)(2,1)} %get-tuple-element.22), calls=%async_computation | async-start | bytes 262144 | tf_op jit(solution)/shard_map/all_to_all | solution.py:424
  10.9 0.3 collective-permute-start
  11.3 0.7 convert_bitcast_fusion.perm
  11.9 0.0 copy-start.4
  11.9 0.7 copy-done.4
  12.6 2.4 %shard_map.76.src.refs_0_ = s32[24]{0:T(128)S(1)} custom-call(s32[128]{0:T(128)S(1)} %copy-done.4), custom_call_target="tpu_custom_call" | custom-call | bytes 262144 | tf_op jit(solution)/shard_map/pallas_call | solution.py:426
  15.0 0.2 shard_map.78.hits
  15.2 0.0 copy-start.1
  15.2 1.6 copy-done.1
  16.8 0.2 shard_map.79.held.right
  17.0 0.0 copy-start.2
  17.0 0.0 collective-permute-done.came
  17.0 1.7 all-to-all-done.got
  18.6 0.0 copy-start
  18.6 0.8 shard_map.80
  19.5 15.8 %all_to_all.55.got = bf16[32,48,128]{2,1,0:T(8,128)(2,1)S(1)} all-to-all(bf16[32,48,128]{2,1,0:T(8,128)(2,1)S(1)} %shard_map.80), channel_id=1, replica_groups=mesh['sector'=32,'op'=8] {'sector'}, dimensions={0} | all-to-all | bytes 786432 | tf_op jit(solution)/shard_map/all_to_all | solution.py:442
  35.3 0.0 copy-done.2
  35.3 0.0 copy-done
  35.3 0.0 copy-start.3
  35.3 2.1 %shard_map.81 = (bf16[16,32,128]{2,1,0:T(8,128)(2,1)S(1)}, f32[12,128,128]{2,1,0:T(8,128)S(1)}) custom-call(s32[2,4]{1,0:T(2,128)S(1)} %bitcast.4, bf16[32,48,128]{2,1,0:T(8,128)(2,1)S(1)} %all_to_all.55.got, bf16[4,16,128,128]{3,2,1,0:T(8,128)(2,1)S(1)} %copy-done, bf16[4,16,128,128]{3,2,1,0:T(8,128)(2,1)S(1)} %shard_map.79.held.right), custom_call_target="tpu_custom_call" | custom-call | flops 536870912 | bytes 6291456 | tf_op jit(solution)/shard_map/pallas_call | solution.py:443
  37.3 15.7 %all_to_all.56.got = bf16[16,32,128]{2,1,0:T(8,128)(2,1)S(1)} all-to-all(bf16[16,32,128]{2,1,0:T(8,128)(2,1)S(1)} %get-tuple-element.24), channel_id=1, replica_groups={{0,1,2,3,4,5,6,7,8,9,10,11,12,13,14,15},{16,17,18,19,20,21,22,23,24,25,..., dimensions={0} | all-to-all | bytes 262144 | tf_op jit(solution)/shard_map/all_to_all | solution.py:385
  53.0 0.0 copy-done.3
  53.1 10.6 %all_to_all.57.refs_1_ = bf16[16,80,128]{2,1,0:T(8,128)(2,1)S(1)} all-to-all(bf16[16,80,128]{2,1,0:T(8,128)(2,1)S(1)} %get-tuple-element.26), channel_id=1, replica_groups={{0,16,32,48,64,80,96,112,128,144,160,176,192,208,224,240},{8,24,40,56,7..., dimensions={0} | all-to-all | bytes 655360 | tf_op jit(solution)/shard_map/all_to_all | solution.py:389
  63.7 0.6 shard_map.83
  64.3 19.6 %all_to_all.58.got = bf16[16,112,128]{2,1,0:T(8,128)(2,1)S(1)} all-to-all(bf16[16,112,128]{2,1,0:T(8,128)(2,1)S(1)} %shard_map.83), channel_id=1, replica_groups={{0,1,2,3,4,5,6,7,8,9,10,11,12,13,14,15},{16,17,18,19,20,21,22,23,24,25,..., dimensions={0} | all-to-all | bytes 917504 | tf_op jit(solution)/shard_map/all_to_all | solution.py:385
  84.0 2.2 %shard_map.84 = (bf16[16,32,128]{2,1,0:T(8,128)(2,1)S(1)}, f32[12,128,128]{2,1,0:T(8,128)S(1)}, f32[64,128]{1,0:T(8,128)S(1)}, f32[64,128]{1,0:T(8,128)S(1)}, f32[8,128]{1,0:T(8,128)S(1)}) custom-call(s32[2,4]{1,0:T(2,128)S(1)} %bitcast.5, bf16[16,112,128]{2,1,0:T(8,128)(2,1)S(1)} %all_to_all.58.got, bf16[4,16,128,128]{3,2,1,0:T(8,128)(2,1)S(1)} %copy-done, ...), custom_call_target="tpu_custom_call" | custom-call | flops 536870912 | bytes 6291456 | tf_op jit(solution)/shard_map/pallas_call | solution.py:457
  86.2 12.3 %all_to_all.59.got = bf16[16,32,128]{2,1,0:T(8,128)(2,1)S(1)} all-to-all(bf16[16,32,128]{2,1,0:T(8,128)(2,1)S(1)} %get-tuple-element.30), channel_id=1, replica_groups={{0,1,2,3,4,5,6,7,8,9,10,11,12,13,14,15},{16,17,18,19,20,21,22,23,24,25,..., dimensions={0} | all-to-all | bytes 262144 | tf_op jit(solution)/shard_map/all_to_all | solution.py:385
  98.4 0.1 shard_map.85
  98.5 10.9 %all_to_all.60.refs_1_ = bf16[16,80,128]{2,1,0:T(8,128)(2,1)S(1)} all-to-all(bf16[16,80,128]{2,1,0:T(8,128)(2,1)S(1)} %get-tuple-element.34), channel_id=1, replica_groups={{0,16,32,48,64,80,96,112,128,144,160,176,192,208,224,240},{8,24,40,56,7..., dimensions={0} | all-to-all | bytes 655360 | tf_op jit(solution)/shard_map/all_to_all | solution.py:389
  109.4 0.6 shard_map.86
  110.1 19.6 %all_to_all.61.got = bf16[16,112,128]{2,1,0:T(8,128)(2,1)S(1)} all-to-all(bf16[16,112,128]{2,1,0:T(8,128)(2,1)S(1)} %shard_map.86), channel_id=1, replica_groups={{0,1,2,3,4,5,6,7,8,9,10,11,12,13,14,15},{16,17,18,19,20,21,22,23,24,25,..., dimensions={0} | all-to-all | bytes 917504 | tf_op jit(solution)/shard_map/all_to_all | solution.py:385
  129.7 2.3 %shard_map.87 = (bf16[16,32,128]{2,1,0:T(8,128)(2,1)S(1)}, f32[4,128,128]{2,1,0:T(8,128)S(1)}, f32[64,128]{1,0:T(8,128)S(1)}, f32[8,128]{1,0:T(8,128)S(1)}) custom-call(s32[2,4]{1,0:T(2,128)S(1)} %bitcast.6, bf16[16,112,128]{2,1,0:T(8,128)(2,1)S(1)} %all_to_all.61.got, bf16[4,16,128,128]{3,2,1,0:T(8,128)(2,1)S(1)} %copy-done, ...), custom_call_target="tpu_custom_call" | custom-call | flops 536870912 | bytes 6291456 | tf_op jit(solution)/shard_map/pallas_call | solution.py:469
  132.0 12.3 %all_to_all.62.got = bf16[16,32,128]{2,1,0:T(8,128)(2,1)S(1)} all-to-all(bf16[16,32,128]{2,1,0:T(8,128)(2,1)S(1)} %get-tuple-element.37), channel_id=1, replica_groups={{0,1,2,3,4,5,6,7,8,9,10,11,12,13,14,15},{16,17,18,19,20,21,22,23,24,25,..., dimensions={0} | all-to-all | bytes 262144 | tf_op jit(solution)/shard_map/all_to_all | solution.py:385
  144.3 0.1 shard_map.88
  144.4 12.6 %all_to_all.63.got = bf16[16,48,128]{2,1,0:T(8,128)(2,1)S(1)} all-to-all(bf16[16,48,128]{2,1,0:T(8,128)(2,1)S(1)} %shard_map.88), channel_id=1, replica_groups={{0,1,2,3,4,5,6,7,8,9,10,11,12,13,14,15},{16,17,18,19,20,21,22,23,24,25,..., dimensions={0} | all-to-all | bytes 393216 | tf_op jit(solution)/shard_map/all_to_all | solution.py:385
  157.0 9.7 %all_to_all.64.sums = f32[16,8,128]{2,1,0:T(8,128)S(1)} all-to-all(f32[16,8,128]{2,1,0:T(8,128)S(1)} %shard_map.89), channel_id=1, replica_groups={{0,16,32,48,64,80,96,112,128,144,160,176,192,208,224,240},{8,24,40,56,7..., dimensions={0} | all-to-all | bytes 131072 | tf_op jit(solution)/shard_map/all_to_all | solution.py:389
  166.7 1.5 shard_map.90
  (2 shorter events, 0.1 us)
Async XLA Ops:
  2.3 16.3 %all-to-all-start = ((bf16[32,16,128]{2,1,0:T(8,128)(2,1)}), bf16[32,16,128]{2,1,0:T(8,128)(2,1)S(1)}, u32[]{:S(2)}, u32[]{:S(2)}) async-start(bf16[32,16,128]{2,1,0:T(8,128)(2,1)} %get-tuple-element.22), calls=%async_computation | async-start | bytes 262144 | tf_op jit(solution)/shard_map/all_to_all | solution.py:424
  10.9 6.0 %collective-permute-start = (f32[32,128]{1,0:T(8,128)}, f32[32,128]{1,0:T(8,128)S(1)}, u32[]{:S(2)}, u32[]{:S(2)}) collective-permute-start(f32[32,128]{1,0:T(8,128)} %get-tuple-element.23), channel_id=1, source_target_pairs={{0,8},{8,0},{16,24},{24,16},{32,40},{40,32},{48,56},{56,48},{64,72... | collective-permute-start | bytes 49160 | tf_op jit(solution)/shard_map/ppermute | solution.py:435
  11.9 0.7 copy-start.4
  15.2 1.6 copy-start.1
  17.0 18.3 %copy-start.2 = (s32[4,2]{0,1:T(2,128)S(1)}, s32[4,2]{0,1:T(2,128)}, u32[]{:S(2)}) copy-start(s32[4,2]{0,1:T(2,128)} %param.9) | copy-start | bytes 100
  18.6 16.6 %copy-start = (bf16[4,16,128,128]{3,2,1,0:T(8,128)(2,1)S(1)}, bf16[4,16,128,128]{3,2,1,0:T(8,128)(2,1)}, u32[]{:S(2)}) copy-start(bf16[4,16,128,128]{3,2,1,0:T(8,128)(2,1)} %left.5) | copy-start | bytes 6291460
  35.3 17.7 %copy-start.3 = (f32[32,128]{1,0:T(8,128)S(1)}, f32[32,128]{1,0:T(8,128)}, u32[]{:S(2)}) copy-start(f32[32,128]{1,0:T(8,128)} %get-tuple-element.25.keep) | copy-start | bytes 49156

commit v3 on v2

--- a/solution.py
+++ b/solution.py
@@ -15,6 +15,7 @@
 CHIPS = 16
 GRP = 16
 NBLK = 3 * SEC
+WIDE = 2 * NBLK * SLAB
 TERMS_DEV = 16
 COUNT = float(128 * W * W)
 EPS = 1e-06
@@ -54,19 +55,35 @@
 
 
 def split_rows(rows):
-    at = iota((16, W), 0)
-    tile = jnp.zeros((16, W), F32)
+    left_half = iota((1, W), 1) < W // 2
+    folded = [row + pltpu.roll(row, W // 2, 1) for row in rows]
+    folded += [jnp.zeros((1, W), F32)] * (4 - len(rows))
+    return split_again([jnp.where(left_half, folded[2 * k], folded[2 * k + 1]) for k in range(2)])
+
+
+def split_again(rows):
+    at = iota((8, W), 0)
+    tile = jnp.zeros((8, W), F32)
     for k, row in enumerate(rows):
         hi = row.astype(BF16).astype(F32)
         mid = (row - hi).astype(BF16).astype(F32)
         low = row - hi - mid
         for n, part in enumerate((hi, mid, low)):
-            tile = jnp.where(at == 3 * k + n, jnp.broadcast_to(part, (16, W)), tile)
+            tile = jnp.where(at == 3 * k + n, jnp.broadcast_to(part, (8, W)), tile)
     return tile.astype(BF16)
 
 
-def join_rows(tile, count):
-    return [row_sum(tile[3 * k : 3 * k + 3]) for k in range(count)]
+def join_rows(tile):
+    return [row_sum(tile[3 * k : 3 * k + 3]) for k in range(2)]
+
+
+def half_totals(rows):
+    left_half = iota((1, W), 1) < W // 2
+    out = []
+    for row in rows:
+        out.append(total(jnp.where(left_half, row, 0.0)))
+        out.append(total(jnp.where(left_half, 0.0, row)))
+    return out
 
 
 def total(row):
@@ -81,13 +98,19 @@
     )
 
 
-def start_kernel(theta, dims, msg, keep, send, held, sizes, sems):
+def start_kernel(theta, dims, msg, keep, send, limits, held, sizes, sems):
     size_copy = pltpu.make_async_copy(dims, sizes, sems.at[SEC])
     copies = [pltpu.make_async_copy(theta.at[i], held.at[i], sems.at[i]) for i in range(SEC)]
     size_copy.start()
     for copy in copies:
         copy.start()
     size_copy.wait()
+    at = iota((8, W), 0)
+    tile = jnp.zeros((8, W), jnp.int32)
+    for i in range(SEC):
+        for k in range(2):
+            tile = jnp.where(at == 2 * i + k, sizes[k, i], tile)
+    limits[...] = tile
     rows = iota((W, W), 0)
     cols = iota((W, W), 1)
     for i in range(SEC):
@@ -115,20 +138,32 @@
         copy.wait()
 
 
-def hits_kernel(perm, hits):
-    shape = (3 * W, W)
-    row = iota(shape, 0)
+def wanted(perm, count, first, shift):
+    shape = (count, W)
+    row = lax.shift_right_logical(iota(shape, 0), shift)
     at = lax.shift_right_logical(row * 21846, 16)
     q = row - 3 * at
-    held = jnp.broadcast_to(perm[...], shape)
-    mine = jnp.sum(jnp.where(iota(shape, 1) == at, held, 0.0), axis=1, keepdims=True)
+    held = jnp.broadcast_to(perm[...].astype(F32), shape)
+    mine = jnp.sum(jnp.where(iota(shape, 1) == at + first, held, 0.0), axis=1, keepdims=True)
     want = mine + q.astype(F32) - 1.0
     want = jnp.where(want < 0.0, want + 128.0, want)
     want = jnp.where(want > 127.0, want - 128.0, want)
-    hits[...] = (held == want).astype(F32).astype(BF16)
-
-
-def pick_kernel(got, hits, src, came, held, msg, pieces, picked):
+    return (held == want).astype(F32).astype(BF16)
+
+
+def hits_kernel(perm, hits, wide):
+    hits[...] = wanted(perm, 3 * W, 0, 0)
+    chip = lax.axis_index("sector") // 2
+    near = wanted(perm, WIDE, chip * 2 * SEC, 3)
+    cols = (W, SLAB * W)
+    spread_out = (lax.shift_right_logical(iota(cols, 1), 3) == iota(cols, 0)).astype(F32).astype(BF16)
+    both = jnp.dot(near, spread_out, preferred_element_type=F32)
+    shape = (WIDE, SLAB * W)
+    same = lax.bitwise_and(iota(shape, 0), 7) == lax.bitwise_and(iota(shape, 1), 7)
+    wide[...] = jnp.where(same, both, 0.0).astype(BF16)
+
+
+def pick_kernel(got, hits, came, held, msg, pieces, picked):
     for g in range(2 * CHIPS):
         pieces[16 * g : 16 * (g + 1)] = got[g].astype(F32)
     for r in range(4):
@@ -149,47 +184,26 @@
                 out[2 * m + k, SLAB * t : SLAB * (t + 1), :] = two[k]
 
 
-def source_kernel(perm, src, pos):
-    chip = lax.axis_index("sector") // 2
-
-    def put(p, carry):
-        pos[perm[p]] = p
-        return carry
-
-    lax.fori_loop(0, 128, put, 0)
-    for n in range(2 * SEC):
-        mine = perm[chip * 2 * SEC + n]
-        for q in range(3):
-            src[3 * n + q] = pos[lax.rem(mine + (q + 127), 128)]
-
-
-def select_kernel(rows, src, got, msg):
+def select_kernel(got, wide, msg):
+    data = 2 * SEC * SLAB
+    slabs = jnp.concatenate([got[n, :data] for n in range(CHIPS)], axis=0)
+    picked = jnp.dot(wide[...], slabs, preferred_element_type=F32).astype(BF16)
+    acc = got[0, data:].astype(F32)
+    for n in range(1, CHIPS):
+        acc = acc + got[n, data:].astype(F32)
+    tile = split_again(join_rows(acc))
     for c in range(2):
-        for pair in range(NBLK // 2):
-            two = []
-            for k in range(2):
-                at = src[NBLK * c + 2 * pair + k]
-                inner = lax.bitwise_and(at, 7)
-                first = pl.multiple_of(lax.shift_right_logical(inner, 1) * 16, 16)
-                tile = got[lax.shift_right_logical(at, 3), pl.ds(first, 16), :].astype(F32)
-                two.append(jnp.where(lax.bitwise_and(inner, 1) == 1, tile[SLAB:], tile[:SLAB]))
-            tile = jnp.concatenate(two, axis=0).astype(BF16)
-            for z in range(NZ):
-                msg[c * NZ + z, 16 * pair : 16 * (pair + 1)] = tile
-    if rows:
-        acc = got[0, 2 * SEC * SLAB :].astype(F32)
-        for n in range(1, CHIPS):
-            acc = acc + got[n, 2 * SEC * SLAB :].astype(F32)
-        tile = split_rows(join_rows(acc, rows))
-        for s in range(GRP):
-            msg[s, NBLK * SLAB :] = tile
-
-
-def gathered_totals(got, rows):
+        half = picked[NBLK * SLAB * c : NBLK * SLAB * (c + 1)]
+        for z in range(NZ):
+            msg[c * NZ + z, : NBLK * SLAB] = half
+            msg[c * NZ + z, NBLK * SLAB :] = tile
+
+
+def gathered_totals(got):
     acc = got[0, NBLK * SLAB :].astype(F32)
     for s in range(1, GRP):
         acc = acc + got[s, NBLK * SLAB :].astype(F32)
-    return [total(r) for r in join_rows(acc, rows)]
+    return half_totals(join_rows(acc))
 
 
 def assemble(got, out):
@@ -200,7 +214,7 @@
                 out[2 * pair + k, SLAB * s : SLAB * (s + 1), :] = tile[SLAB * k : SLAB * (k + 1)]
 
 
-def products(dims, blocks, left, right, msg, acc):
+def products(limits, blocks, left, right, msg, acc):
     _, z = core_and_z()
     rows = iota((W, W), 0)
     cols = iota((W, W), 1)
@@ -217,7 +231,7 @@
         lhs = jnp.concatenate(inner, axis=1)
         rhs = jnp.concatenate([right[i, w] for w in order], axis=0)
         out = jnp.dot(lhs, rhs, preferred_element_type=F32)
-        inside = (rows < dims[0, i]) & (cols < dims[1, i])
+        inside = (rows < coef(limits, 2 * i)) & (cols < coef(limits, 2 * i + 1))
         acc[i] = jnp.where(inside, out * SCALE, 0.0)
     for s in range(GRP):
         at = slice(SLAB * s, SLAB * (s + 1))
@@ -238,13 +252,13 @@
     return ref[k : k + 1, 0:1]
 
 
-def ham0_kernel(dims, got, left, right, msg, blk, acc):
+def ham0_kernel(limits, got, left, right, msg, blk, acc):
     assemble_pieces(got, blk)
-    products(dims, blk, left, right, msg, acc)
-
-
-def ham1_kernel(dims, got, left, right, blk0, slab0, image0, msg, blk, v0, v1, coefs, acc):
-    uu, uw, ww = gathered_totals(got, 3)
+    products(limits, blk, left, right, msg, acc)
+
+
+def ham1_kernel(limits, got, left, right, blk0, slab0, image0, msg, blk, v0, v1, coefs, acc):
+    uu, uw, ww, _ = gathered_totals(got)
     assemble(got, blk)
     n2 = uu / COUNT + EPS
     inv = 1.0 / jnp.sqrt(n2)
@@ -258,13 +272,13 @@
     v0[...] = slab0[...] * inv
     v1[...] = image0[...] * wc - slab0[...] * vc
     put_coefs(coefs, (a0, b1, inv))
-    products(dims, blk, left, right, msg, acc)
+    products(limits, blk, left, right, msg, acc)
 
 
 def ham2_kernel(
-    dims, got, left, right, blk1, blk0, slab1, rest1, old, msg, own, v2, coefs, blk, acc
+    limits, got, left, right, blk1, blk0, slab1, rest1, old, msg, own, v2, coefs, blk, acc
 ):
-    vw, vr, rr, vv = gathered_totals(got, 4)
+    vw, vr, rr, vv = gathered_totals(got)
     assemble(got, blk)
     a0, b1, inv = coef(old, 0), coef(old, 1), coef(old, 2)
     a1 = vw / COUNT
@@ -280,7 +294,7 @@
         own[i] = blk[3 * i + 1]
     v2[...] = (rest1[...] - d * slab1[...]) * wc
     put_coefs(coefs, (a0, a1, b1, b2))
-    products(dims, blk, left, right, msg, acc)
+    products(limits, blk, left, right, msg, acc)
 
 
 def reduced(got):
@@ -345,7 +359,7 @@
         acc = acc + got[s, half:].astype(F32)
     at = iota((8, W), 0)
     tile = jnp.zeros((8, W), F32)
-    for k, row in enumerate(join_rows(acc, 4)):
+    for k, row in enumerate(join_rows(acc)):
         tile = jnp.where(at == k, jnp.broadcast_to(row, (8, W)), tile)
     for n in range(CHIPS):
         msg[n] = tile
@@ -355,7 +369,7 @@
     acc = sums[0]
     for n in range(1, CHIPS):
         acc = acc + sums[n]
-    vw, vr, rr, vv = [total(acc[k : k + 1]) for k in range(4)]
+    vw, vr, rr, vv = half_totals([acc[k : k + 1] for k in range(2)])
     a0, a1, b1, b2 = [coef(coefs, k) for k in range(4)]
     a2 = vw / COUNT
     d = a2 - a1
@@ -389,20 +403,15 @@
     return lax.all_to_all(x, "sector", 0, 0, axis_index_groups=XY_GROUPS)
 
 
-def select(rows, got, src):
-    extra = 16 if rows else 0
-    return call(
-        lambda *refs: select_kernel(rows, *refs),
-        [((GRP, NBLK * SLAB + extra, W), BF16)],
-        [SMEM, VMEM],
-    )(src, got)[0]
+def select(got, wide):
+    return call(select_kernel, [((GRP, NBLK * SLAB + 8, W), BF16)], [VMEM, VMEM])(got, wide)[0]
 
 
 def per_device(theta, left, right, perm, dims):
     half = (SEC * SLAB, W)
     slab = (2 * SEC * SLAB, W)
     scatter = ((GRP, SEC * SLAB, W), BF16)
-    plane = ((CHIPS, 2 * SEC * SLAB + 16, W), BF16)
+    plane = ((CHIPS, 2 * SEC * SLAB + 8, W), BF16)
     blocks = ((NBLK, W, W), F32)
     acc = [pltpu.VMEM((SEC, W, W), F32)]
     coefs = ((8, W), F32)
@@ -414,68 +423,62 @@
     pieces = 2 * CHIPS
     sems = pltpu.SemaphoreType.DMA((SEC + 1,))
 
-    msg, keep, send = call(
+    msg, keep, send, limits = call(
         start_kernel,
-        [((pieces, 16, W), BF16), (half, F32), (half, F32)],
+        [((pieces, 16, W), BF16), (half, F32), (half, F32), ((8, W), jnp.int32)],
         [any_space, any_space],
         [pltpu.VMEM((SEC, W, W), F32), pltpu.SMEM((2, SEC), jnp.int32), sems],
         limit=60,
     )(theta, dims)
     got = lax.all_to_all(msg, "sector", 0, 0)
-    (hits,) = call(hits_kernel, [((3 * W, W), BF16)], [VMEM])(perm.astype(F32).reshape(1, W))
-    (src,) = call(
-        source_kernel,
-        [((6 * SEC,), jnp.int32)],
-        [SMEM],
-        [pltpu.SMEM((128,), jnp.int32)],
-        out_specs=[SMEM],
-        limit=1,
-    )(perm)
+    hits, wide = call(
+        hits_kernel, [((3 * W, W), BF16), ((WIDE, SLAB * W), BF16)], [VMEM]
+    )(perm.reshape(1, W))
     (right,) = call(load_kernel, [((SEC, TERMS_DEV, W, W), BF16)], [any_space], [sems])(right)
     came = lax.ppermute(send, "sector", SWAP)
     (msg,) = call(
         pick_kernel,
         [((pieces, 4 * NBLK, W), BF16)],
-        [VMEM, VMEM, SMEM, any_space, any_space],
+        [VMEM, VMEM, any_space, any_space],
         [pltpu.VMEM((pieces * 16, W), F32), pltpu.VMEM((pieces * 4 * NBLK, W), F32)],
-    )(got, hits, src, came, right)
+    )(got, hits, came, right)
     got = lax.all_to_all(msg, "sector", 0, 0)
     msg, blk0 = call(
         ham0_kernel,
         [scatter, blocks],
-        [SMEM, VMEM, VMEM, VMEM],
+        [VMEM] * 4,
         acc,
         flops,
         nbytes,
         limit=16,
-    )(dims, got, left, right)
+    )(limits, got, left, right)
     msg, image0, slab0 = call(reduce0_kernel, [plane, (slab, F32), (slab, F32)], [VMEM] * 3)(
         over_cz(msg), keep, came
     )
 
-    got = over_cz(select(3, over_xy(msg), src))
+    got = over_cz(select(over_xy(msg), wide))
     msg, blk1, v0, v1, co = call(
         ham1_kernel,
         [scatter, blocks, (slab, F32), (slab, F32), coefs],
-        [SMEM] + [VMEM] * 6,
+        [VMEM] * 7,
         acc,
         flops,
         nbytes,
         limit=16,
-    )(dims, got, left, right, blk0, slab0, image0)
+    )(limits, got, left, right, blk0, slab0, image0)
     msg, rest1 = call(reduce1_kernel, [plane, (slab, F32)], [VMEM] * 4)(over_cz(msg), v1, v0, co)
 
-    got = over_cz(select(4, over_xy(msg), src))
+    got = over_cz(select(over_xy(msg), wide))
     msg, own, v2, co = call(
         ham2_kernel,
         [scatter, ((SEC, W, W), F32), (slab, F32), coefs],
-        [SMEM] + [VMEM] * 8,
+        [VMEM] * 9,
         [pltpu.VMEM((NBLK, W, W), F32)] + acc,
         flops,
         nbytes,
         limit=16,
-    )(dims, got, left, right, blk1, blk0, v1, rest1, co)
-    (msg,) = call(reduce2_kernel, [((GRP, SEC * SLAB + 16, W), BF16)], [VMEM] * 4)(
+    )(limits, got, left, right, blk1, blk0, v1, rest1, co)
+    (msg,) = call(reduce2_kernel, [((GRP, SEC * SLAB + 8, W), BF16)], [VMEM] * 4)(
         over_cz(msg), v2, v1, co
     )
 

time: 170 us -> 163 us (0.959)
  Pallas kernels: 14.8 us -> 9.95 us
  blocking collectives: 139 us -> 135 us
  waiting for transfers between devices: 1.66 us -> 4.51 us
    pallas_call x10 -> x9, Pallas kernels: 12.9 us -> 7.94 us  [the longest x1 1.75 us: per_device(): call(ham2_kernel, [scatter, ((SEC, W, W), F32), (slab, F32), coefs], [VME...]
    all_to_all x1, waiting for transfers between devices: 1.66 us -> 4.51 us  [per_device(): got = lax.all_to_all(msg, 'sector', 0, 0)]
    all_to_all x6, blocking collectives: 92.1 us -> 90 us  [over_cz(): return lax.all_to_all(x, BOTH, 0, 0, axis_index_groups=CZ_GROUPS)]
    all_to_all x1, blocking collectives: 15.8 us -> 14 us  [per_device(): got = lax.all_to_all(msg, 'sector', 0, 0)]
  transfers between devices with their start and end apart: 2 -> 2, of which waited for: 1 -> 1; matrix products, arithmetic and copies ran while one was open for 0% -> 0% of each run, Pallas kernels for 2% -> 0%
where the time goes in v3:
time: 163 us; the launch traced here: 161 us
  blocking collectives  135 us (83%)
  Pallas kernels  9.95 us (6%)
  starting transfers between devices  8.92 us (5%)
  waiting for transfers between devices  4.51 us (3%)
  local copies, waits for them, and re-layouts  2.25 us (1%)
    all_to_all x6, blocking collectives, over_cz(): return lax.all_to_all(x, BOTH, 0, 0, axis_index_groups=CZ_GROUPS)  90 us
    all_to_all x3, blocking collectives, over_xy(): return lax.all_to_all(x, 'sector', 0, 0, axis_index_groups=XY_GROUPS)  30.8 us
    all_to_all x1, blocking collectives, per_device(): got = lax.all_to_all(msg, 'sector', 0, 0)  14 us
    all_to_all x1, starting transfers between devices, per_device(): got = lax.all_to_all(msg, 'sector', 0, 0)  8.6 us
    all_to_all x1, waiting for transfers between devices, per_device(): got = lax.all_to_all(msg, 'sector', 0, 0)  4.51 us
  transfers between devices with their start and end apart: 2, of which 1 were waited for; matrix products, arithmetic and copies ran while one was open for 0% of the time, Pallas kernels for 0%

profile of v3, /device:TPU:1, one launch (start us, length us, event | category | flops | bytes accessed | tf_op | source)
XLA Modules:
  0.0 161.2 jit_solution(118633752945853931)
XLA Ops:
  0.6 1.7 %shard_map.76 = (bf16[32,16,128]{2,1,0:T(8,128)(2,1)}, f32[32,128]{1,0:T(8,128)}, f32[32,128]{1,0:T(8,128)}, s32[8,128]{1,0:T(8,128)}) custom-call(f32[4,128,128]{2,1,0:T(8,128)} %theta.1, s32[2,4]{1,0:T(2,128)} %bitcast.3), custom_call_target="tpu_custom_call" | custom-call | bytes 262144 | tf_op jit(solution)/shard_map/pallas_call | solution.py:426
  2.3 8.6 %all-to-all-start = ((bf16[32,16,128]{2,1,0:T(8,128)(2,1)}), bf16[32,16,128]{2,1,0:T(8,128)(2,1)S(1)}, u32[]{:S(2)}, u32[]{:S(2)}) async-start(bf16[32,16,128]{2,1,0:T(8,128)(2,1)} %get-tuple-element.26), calls=%async_computation | async-start | bytes 262144 | tf_op jit(solution)/shard_map/all_to_all | solution.py:433
  10.9 0.3 collective-permute-start
  11.3 0.0 copy-start.4
  11.3 0.7 copy-done.4
  11.9 0.4 shard_map.77
  12.3 0.0 copy-start.1
  12.3 1.6 copy-done.1
  13.9 0.2 shard_map.78.held.right
  14.1 0.0 copy-start.2
  14.1 0.0 collective-permute-done.came
  14.1 4.5 %all-to-all-done.got = bf16[32,16,128]{2,1,0:T(8,128)(2,1)S(1)} async-done(((bf16[32,16,128]{2,1,0:T(8,128)(2,1)}), bf16[32,16,128]{2,1,0:T(8,128)(2,1)S(1)}, u32[]{:S(2)}, u32[]{:S(2)}) %all-to-all-start) | async-done | bytes 131104 | tf_op jit(solution)/shard_map/all_to_all | solution.py:433
  18.6 0.0 copy-start
  18.6 0.3 shard_map.79
  18.9 14.0 %all_to_all.55.got = bf16[32,48,128]{2,1,0:T(8,128)(2,1)S(1)} all-to-all(bf16[32,48,128]{2,1,0:T(8,128)(2,1)S(1)} %shard_map.79), channel_id=1, replica_groups=mesh['sector'=32,'op'=8] {'sector'}, dimensions={0} | all-to-all | bytes 786432 | tf_op jit(solution)/shard_map/all_to_all | solution.py:445
  32.9 0.0 copy-done.2
  32.9 0.0 copy-done
  32.9 0.0 copy-start.3
  33.0 1.5 shard_map.80
  34.5 15.7 %all_to_all.56.got = bf16[16,32,128]{2,1,0:T(8,128)(2,1)S(1)} all-to-all(bf16[16,32,128]{2,1,0:T(8,128)(2,1)S(1)} %get-tuple-element.29), channel_id=1, replica_groups={{0,1,2,3,4,5,6,7,8,9,10,11,12,13,14,15},{16,17,18,19,20,21,22,23,24,25,..., dimensions={0} | all-to-all | bytes 262144 | tf_op jit(solution)/shard_map/all_to_all | solution.py:399
  50.2 0.0 copy-done.3
  50.2 0.1 shard_map.81
  50.3 10.4 %all_to_all.57.got = bf16[16,72,128]{2,1,0:T(8,128)(2,1)S(1)} all-to-all(bf16[16,72,128]{2,1,0:T(8,128)(2,1)S(1)} %get-tuple-element.31), channel_id=1, replica_groups={{0,16,32,48,64,80,96,112,128,144,160,176,192,208,224,240},{8,24,40,56,7..., dimensions={0} | all-to-all | bytes 589824 | tf_op jit(solution)/shard_map/all_to_all | solution.py:403
  60.7 0.2 shard_map.82
  60.9 19.0 %all_to_all.58.got = bf16[16,104,128]{2,1,0:T(8,128)(2,1)S(1)} all-to-all(bf16[16,104,128]{2,1,0:T(8,128)(2,1)S(1)} %shard_map.82), channel_id=1, replica_groups={{0,1,2,3,4,5,6,7,8,9,10,11,12,13,14,15},{16,17,18,19,20,21,22,23,24,25,..., dimensions={0} | all-to-all | bytes 851968 | tf_op jit(solution)/shard_map/all_to_all | solution.py:399
  79.9 1.7 %shard_map.83 = (bf16[16,32,128]{2,1,0:T(8,128)(2,1)S(1)}, f32[12,128,128]{2,1,0:T(8,128)S(1)}, f32[64,128]{1,0:T(8,128)S(1)}, f32[64,128]{1,0:T(8,128)S(1)}, f32[8,128]{1,0:T(8,128)S(1)}) custom-call(s32[8,128]{1,0:T(8,128)S(1)} %copy-done.2, bf16[16,104,128]{2,1,0:T(8,128)(2,1)S(1)} %all_to_all.58.got, bf16[4,16,128,128]{3,2,1,0:T(8,128)(2,1)S(1)} %copy-done, ...), custom_call_target="tpu_custom_call" | custom-call | flops 536870912 | bytes 6291456 | tf_op jit(solution)/shard_map/pallas_call | solution.py:460
  81.6 12.1 %all_to_all.59.got = bf16[16,32,128]{2,1,0:T(8,128)(2,1)S(1)} all-to-all(bf16[16,32,128]{2,1,0:T(8,128)(2,1)S(1)} %get-tuple-element.36), channel_id=1, replica_groups={{0,1,2,3,4,5,6,7,8,9,10,11,12,13,14,15},{16,17,18,19,20,21,22,23,24,25,..., dimensions={0} | all-to-all | bytes 262144 | tf_op jit(solution)/shard_map/all_to_all | solution.py:399
  93.7 0.1 shard_map.84
  93.9 10.7 %all_to_all.60.got = bf16[16,72,128]{2,1,0:T(8,128)(2,1)S(1)} all-to-all(bf16[16,72,128]{2,1,0:T(8,128)(2,1)S(1)} %get-tuple-element.40), channel_id=1, replica_groups={{0,16,32,48,64,80,96,112,128,144,160,176,192,208,224,240},{8,24,40,56,7..., dimensions={0} | all-to-all | bytes 589824 | tf_op jit(solution)/shard_map/all_to_all | solution.py:403
  104.5 0.3 shard_map.85
  104.8 19.0 %all_to_all.61.got = bf16[16,104,128]{2,1,0:T(8,128)(2,1)S(1)} all-to-all(bf16[16,104,128]{2,1,0:T(8,128)(2,1)S(1)} %shard_map.85), channel_id=1, replica_groups={{0,1,2,3,4,5,6,7,8,9,10,11,12,13,14,15},{16,17,18,19,20,21,22,23,24,25,..., dimensions={0} | all-to-all | bytes 851968 | tf_op jit(solution)/shard_map/all_to_all | solution.py:399
  123.8 1.7 %shard_map.86 = (bf16[16,32,128]{2,1,0:T(8,128)(2,1)S(1)}, f32[4,128,128]{2,1,0:T(8,128)S(1)}, f32[64,128]{1,0:T(8,128)S(1)}, f32[8,128]{1,0:T(8,128)S(1)}) custom-call(s32[8,128]{1,0:T(8,128)S(1)} %copy-done.2, bf16[16,104,128]{2,1,0:T(8,128)(2,1)S(1)} %all_to_all.61.got, bf16[4,16,128,128]{3,2,1,0:T(8,128)(2,1)S(1)} %copy-done, ...), custom_call_target="tpu_custom_call" | custom-call | flops 536870912 | bytes 6291456 | tf_op jit(solution)/shard_map/pallas_call | solution.py:472
  125.5 12.1 %all_to_all.62.got = bf16[16,32,128]{2,1,0:T(8,128)(2,1)S(1)} all-to-all(bf16[16,32,128]{2,1,0:T(8,128)(2,1)S(1)} %get-tuple-element.43), channel_id=1, replica_groups={{0,1,2,3,4,5,6,7,8,9,10,11,12,13,14,15},{16,17,18,19,20,21,22,23,24,25,..., dimensions={0} | all-to-all | bytes 262144 | tf_op jit(solution)/shard_map/all_to_all | solution.py:399
  137.7 0.1 shard_map.87
  137.8 12.1 %all_to_all.63.got = bf16[16,40,128]{2,1,0:T(8,128)(2,1)S(1)} all-to-all(bf16[16,40,128]{2,1,0:T(8,128)(2,1)S(1)} %shard_map.87), channel_id=1, replica_groups={{0,1,2,3,4,5,6,7,8,9,10,11,12,13,14,15},{16,17,18,19,20,21,22,23,24,25,..., dimensions={0} | all-to-all | bytes 327680 | tf_op jit(solution)/shard_map/all_to_all | solution.py:399
  150.0 9.7 %all_to_all.64.sums = f32[16,8,128]{2,1,0:T(8,128)S(1)} all-to-all(f32[16,8,128]{2,1,0:T(8,128)S(1)} %shard_map.88), channel_id=1, replica_groups={{0,16,32,48,64,80,96,112,128,144,160,176,192,208,224,240},{8,24,40,56,7..., dimensions={0} | all-to-all | bytes 131072 | tf_op jit(solution)/shard_map/all_to_all | solution.py:403
  159.7 1.5 shard_map.89
  (1 shorter events, 0.0 us)
Async XLA Ops:
  2.3 16.3 %all-to-all-start = ((bf16[32,16,128]{2,1,0:T(8,128)(2,1)}), bf16[32,16,128]{2,1,0:T(8,128)(2,1)S(1)}, u32[]{:S(2)}, u32[]{:S(2)}) async-start(bf16[32,16,128]{2,1,0:T(8,128)(2,1)} %get-tuple-element.26), calls=%async_computation | async-start | bytes 262144 | tf_op jit(solution)/shard_map/all_to_all | solution.py:433
  10.9 3.2 %collective-permute-start = (f32[32,128]{1,0:T(8,128)}, f32[32,128]{1,0:T(8,128)S(1)}, u32[]{:S(2)}, u32[]{:S(2)}) collective-permute-start(f32[32,128]{1,0:T(8,128)} %get-tuple-element.28), channel_id=1, source_target_pairs={{0,8},{8,0},{16,24},{24,16},{32,40},{40,32},{48,56},{56,48},{64,72... | collective-permute-start | bytes 49160 | tf_op jit(solution)/shard_map/ppermute | solution.py:438
  11.3 0.7 copy-start.4
  12.3 1.6 copy-start.1
  14.1 18.8 %copy-start.2 = (s32[8,128]{1,0:T(8,128)S(1)}, s32[8,128]{1,0:T(8,128)}, u32[]{:S(2)}) copy-start(s32[8,128]{1,0:T(8,128)} %get-tuple-element.25.limits) | copy-start | bytes 12292
  18.6 14.3 %copy-start = (bf16[4,16,128,128]{3,2,1,0:T(8,128)(2,1)S(1)}, bf16[4,16,128,128]{3,2,1,0:T(8,128)(2,1)}, u32[]{:S(2)}) copy-start(bf16[4,16,128,128]{3,2,1,0:T(8,128)(2,1)} %left.5) | copy-start | bytes 6291460
  32.9 17.2 %copy-start.3 = (f32[32,128]{1,0:T(8,128)S(1)}, f32[32,128]{1,0:T(8,128)}, u32[]{:S(2)}) copy-start(f32[32,128]{1,0:T(8,128)} %get-tuple-element.30.keep) | copy-start | bytes 49156

commit v4 on v3

--- a/solution.py
+++ b/solution.py
@@ -15,6 +15,8 @@
 CHIPS = 16
 GRP = 16
 NBLK = 3 * SEC
+HELD = SEC // 2
+NEAR = 3 * HELD
 WIDE = 2 * NBLK * SLAB
 TERMS_DEV = 16
 COUNT = float(128 * W * W)
@@ -25,6 +27,8 @@
 CZ_GROUPS = [[(2 * chip + c) * NZ + z for c in range(2) for z in range(NZ)] for chip in range(CHIPS)]
 XY_GROUPS = [[2 * chip + c for chip in range(CHIPS)] for c in range(2)]
 SWAP = [(i, i ^ 1) for i in range(2 * CHIPS)]
+DOWN = [(i, (i - 1) % NZ) for i in range(NZ)]
+UP = [(i, (i + 1) % NZ) for i in range(NZ)]
 
 VMEM = pl.BlockSpec(memory_space=pltpu.VMEM)
 SMEM = pl.BlockSpec(memory_space=pltpu.SMEM)
@@ -98,11 +102,27 @@
     )
 
 
-def start_kernel(theta, dims, msg, keep, send, limits, held, sizes, sems):
+def start_kernel(
+    theta, dims, left, right, msg, keep, send, limits, down, up, held, sizes, stage, sems, out_sems
+):
     size_copy = pltpu.make_async_copy(dims, sizes, sems.at[SEC])
     copies = [pltpu.make_async_copy(theta.at[i], held.at[i], sems.at[i]) for i in range(SEC)]
+    c, z = core_and_z()
+    other = HELD * (1 - lax.rem(z, 2))
     size_copy.start()
     for copy in copies:
+        copy.start()
+    away = (down, up)
+    halves = []
+    for m in range(HELD):
+        for k, array in enumerate((left, right)):
+            halves.append(
+                (
+                    pltpu.make_async_copy(array.at[other + m], stage.at[m, k], sems.at[SEC + 1 + 2 * m + k]),
+                    pltpu.make_async_copy(stage.at[m, k], away[m].at[k], out_sems.at[2 * m + k]),
+                )
+            )
+    for copy, _ in halves:
         copy.start()
     size_copy.wait()
     at = iota((8, W), 0)
@@ -115,6 +135,10 @@
     cols = iota((W, W), 1)
     for i in range(SEC):
         copies[i].wait()
+        if i == SEC - 1:
+            for copy, out in halves:
+                copy.wait()
+                out.start()
         inside = (rows < sizes[0, i]) & (cols < sizes[1, i])
         held[i] = jnp.where(inside, held[i], 0.0)
     for t in range(GRP):
@@ -123,19 +147,12 @@
         even1, odd1 = low_high(tiles[2], tiles[3])
         msg[2 * t] = jnp.concatenate([even0, even1], axis=0).astype(BF16)
         msg[2 * t + 1] = jnp.concatenate([odd0, odd1], axis=0).astype(BF16)
-    c, z = core_and_z()
     for slot, out in ((c * NZ + z, keep), ((1 - c) * NZ + z, send)):
         first = pl.multiple_of(slot * SLAB, SLAB)
         for i in range(SEC):
             out[SLAB * i : SLAB * (i + 1), :] = held[i, pl.ds(first, SLAB), :]
-
-
-def load_kernel(array, held, sems):
-    copies = [pltpu.make_async_copy(array.at[i], held.at[i], sems.at[i]) for i in range(SEC)]
-    for copy in copies:
-        copy.start()
-    for copy in copies:
-        copy.wait()
+    for _, out in halves:
+        out.wait()
 
 
 def wanted(perm, count, first, shift):
@@ -151,8 +168,11 @@
     return (held == want).astype(F32).astype(BF16)
 
 
-def hits_kernel(perm, hits, wide):
-    hits[...] = wanted(perm, 3 * W, 0, 0)
+def hits_kernel(perm, ones):
+    hits = wanted(perm, 3 * W, 0, 0)
+    part = 3 * W // SLAB
+    for k in range(SLAB):
+        ones[WIDE:, W * k : W * (k + 1)] = hits[part * k : part * (k + 1)]
     chip = lax.axis_index("sector") // 2
     near = wanted(perm, WIDE, chip * 2 * SEC, 3)
     cols = (W, SLAB * W)
@@ -160,15 +180,16 @@
     both = jnp.dot(near, spread_out, preferred_element_type=F32)
     shape = (WIDE, SLAB * W)
     same = lax.bitwise_and(iota(shape, 0), 7) == lax.bitwise_and(iota(shape, 1), 7)
-    wide[...] = jnp.where(same, both, 0.0).astype(BF16)
-
-
-def pick_kernel(got, hits, came, held, msg, pieces, picked):
+    ones[:WIDE] = jnp.where(same, both, 0.0).astype(BF16)
+
+
+def pick_kernel(got, ones, came, held, msg, pieces, picked):
     for g in range(2 * CHIPS):
         pieces[16 * g : 16 * (g + 1)] = got[g].astype(F32)
+    hits = jnp.concatenate([ones[WIDE:, W * k : W * (k + 1)] for k in range(SLAB)], axis=0)
     for r in range(4):
         part = pieces[pl.ds(r, W, stride=4), :].astype(BF16)
-        picked[pl.ds(r, 3 * W, stride=4), :] = jnp.dot(hits[...], part, preferred_element_type=F32)
+        picked[pl.ds(r, 3 * W, stride=4), :] = jnp.dot(hits, part, preferred_element_type=F32)
     for g in range(2 * CHIPS):
         msg[g] = picked[48 * g : 48 * (g + 1)].astype(BF16)
 
@@ -184,31 +205,32 @@
                 out[2 * m + k, SLAB * t : SLAB * (t + 1), :] = two[k]
 
 
-def select_kernel(got, wide, msg):
+def select_kernel(got, ones, msg):
     data = 2 * SEC * SLAB
     slabs = jnp.concatenate([got[n, :data] for n in range(CHIPS)], axis=0)
-    picked = jnp.dot(wide[...], slabs, preferred_element_type=F32).astype(BF16)
+    picked = jnp.dot(ones[:WIDE], slabs, preferred_element_type=F32).astype(BF16)
     acc = got[0, data:].astype(F32)
     for n in range(1, CHIPS):
         acc = acc + got[n, data:].astype(F32)
     tile = split_again(join_rows(acc))
+    rows = NEAR * SLAB
     for c in range(2):
-        half = picked[NBLK * SLAB * c : NBLK * SLAB * (c + 1)]
         for z in range(NZ):
-            msg[c * NZ + z, : NBLK * SLAB] = half
-            msg[c * NZ + z, NBLK * SLAB :] = tile
-
-
-def gathered_totals(got):
-    acc = got[0, NBLK * SLAB :].astype(F32)
+            first = rows * (2 * c + z % 2)
+            msg[c * NZ + z, :rows] = picked[first : first + rows]
+            msg[c * NZ + z, rows:] = tile
+
+
+def summed_tile(got, first):
+    acc = got[0, first:].astype(F32)
     for s in range(1, GRP):
-        acc = acc + got[s, NBLK * SLAB :].astype(F32)
-    return half_totals(join_rows(acc))
+        acc = acc + got[s, first:].astype(F32)
+    return join_rows(acc)
 
 
 def assemble(got, out):
     for s in range(GRP):
-        for pair in range(NBLK // 2):
+        for pair in range(NEAR // 2):
             tile = got[s, 16 * pair : 16 * (pair + 1)].astype(F32)
             for k in range(2):
                 out[2 * pair + k, SLAB * s : SLAB * (s + 1), :] = tile[SLAB * k : SLAB * (k + 1)]
@@ -240,6 +262,45 @@
             msg[s, 16 * pair : 16 * (pair + 1)] = tile.astype(BF16)
 
 
+def start_copies(above, below, near, sems):
+    copies = []
+    for m, array in enumerate((above, below)):
+        for k in range(2):
+            copy = pltpu.make_async_copy(array.at[k], near.at[m, k], sems.at[2 * m + k])
+            copy.start()
+            copies.append(copy)
+    return copies
+
+
+def products_held(limits, blocks, left, right, extra, msg, acc):
+    _, z = core_and_z()
+    odd = lax.rem(z, 2)
+    rows = iota((W, W), 0)
+    cols = iota((W, W), 1)
+    inner = [[], []]
+    rhs = [[], []]
+    for mine in (True, False):
+        for m in range(HELD):
+            i = HELD * odd + m
+            start = z if mine else lax.rem(z + (NZ + 1 - 2 * m), NZ)
+            for r in range(3):
+                terms = range(r, TERMS_DEV, 3)
+                vec = blocks[3 * m + lax.rem(start + r, 3)].astype(BF16)
+                lhs = jnp.concatenate([left[i, w] if mine else extra[m, 0, w] for w in terms], axis=0)
+                got = jnp.dot(lhs, vec, preferred_element_type=F32).astype(BF16)
+                inner[m] += [got[W * n : W * (n + 1)] for n in range(len(terms))]
+                rhs[m] += [right[i, w] if mine else extra[m, 1, w] for w in terms]
+    for m in range(HELD):
+        i = HELD * odd + m
+        lhs = jnp.concatenate(inner[m], axis=1)
+        out = jnp.dot(lhs, jnp.concatenate(rhs[m], axis=0), preferred_element_type=F32)
+        size = limits[pl.ds(2 * i, 1), 0:1], limits[pl.ds(2 * i + 1, 1), 0:1]
+        acc[m] = jnp.where((rows < size[0]) & (cols < size[1]), out * SCALE, 0.0)
+    for s in range(GRP):
+        at = slice(SLAB * s, SLAB * (s + 1))
+        msg[s, :16] = jnp.concatenate([acc[0, at, :], acc[1, at, :]], axis=0).astype(BF16)
+
+
 def put_coefs(out, values):
     at = iota((8, W), 0)
     tile = jnp.zeros((8, W), F32)
@@ -252,13 +313,19 @@
     return ref[k : k + 1, 0:1]
 
 
-def ham0_kernel(limits, got, left, right, msg, blk, acc):
+def ham0_kernel(limits, got, left, right, above, below, msg, blk, near, acc, sems):
+    copies = start_copies(above, below, near, sems)
     assemble_pieces(got, blk)
     products(limits, blk, left, right, msg, acc)
-
-
-def ham1_kernel(limits, got, left, right, blk0, slab0, image0, msg, blk, v0, v1, coefs, acc):
-    uu, uw, ww, _ = gathered_totals(got)
+    for copy in copies:
+        copy.wait()
+
+
+def ham1_kernel(
+    limits, got, left, right, near, blk0, slab0, image0, msg, blk, v0, v1, coefs, acc
+):
+    first = NEAR * lax.rem(core_and_z()[1], 2)
+    uu, uw, ww, _ = half_totals(summed_tile(got, NEAR * SLAB))
     assemble(got, blk)
     n2 = uu / COUNT + EPS
     inv = 1.0 / jnp.sqrt(n2)
@@ -267,18 +334,19 @@
     b1 = jnp.sqrt(jnp.maximum(rr, 0.0) / COUNT + EPS)
     wc = inv / b1
     vc = a0 * wc
-    for n in range(NBLK):
-        blk[n] = blk[n] * wc - blk0[n] * vc
+    for n in range(NEAR):
+        blk[n] = blk[n] * wc - blk0[first + n] * vc
     v0[...] = slab0[...] * inv
     v1[...] = image0[...] * wc - slab0[...] * vc
     put_coefs(coefs, (a0, b1, inv))
-    products(limits, blk, left, right, msg, acc)
+    products_held(limits, blk, left, right, near, msg, acc)
 
 
 def ham2_kernel(
-    limits, got, left, right, blk1, blk0, slab1, rest1, old, msg, own, v2, coefs, blk, acc
+    limits, got, left, right, near, blk1, blk0, slab1, rest1, old, msg, v2, coefs, blk, acc
 ):
-    vw, vr, rr, vv = gathered_totals(got)
+    first = NEAR * lax.rem(core_and_z()[1], 2)
+    vw, vr, rr, vv = half_totals(summed_tile(got, NEAR * SLAB))
     assemble(got, blk)
     a0, b1, inv = coef(old, 0), coef(old, 1), coef(old, 2)
     a1 = vw / COUNT
@@ -288,13 +356,15 @@
     wc = 1.0 / b2
     vc = a1 * wc
     pc = b1 * inv * wc
-    for n in range(NBLK):
-        blk[n] = blk[n] * wc - blk1[n] * vc - blk0[n] * pc
-    for i in range(SEC):
-        own[i] = blk[3 * i + 1]
+    for n in range(NEAR):
+        blk[n] = blk[n] * wc - blk1[n] * vc - blk0[first + n] * pc
     v2[...] = (rest1[...] - d * slab1[...]) * wc
     put_coefs(coefs, (a0, a1, b1, b2))
-    products(limits, blk, left, right, msg, acc)
+    products_held(limits, blk, left, right, near, msg, acc)
+    dots = row_sum(sum(blk[3 * m + 1] * acc[m] for m in range(HELD)))
+    tile = split_rows([dots])
+    for s in range(GRP):
+        msg[s, 16:] = tile
 
 
 def reduced(got):
@@ -304,6 +374,17 @@
         for z in range(1, NZ):
             acc = acc + got[c * NZ + z].astype(F32)
         parts.append(acc)
+    return jnp.concatenate(parts, axis=0)
+
+
+def reduced_halves(got):
+    parts = []
+    for c in range(2):
+        for odd in range(2):
+            acc = got[c * NZ + odd, :16].astype(F32)
+            for z in range(odd + 2, NZ, 2):
+                acc = acc + got[c * NZ + z, :16].astype(F32)
+            parts.append(acc)
     return jnp.concatenate(parts, axis=0)
 
 
@@ -332,60 +413,59 @@
 
 
 def reduce1_kernel(got, v1, v0, coefs, msg, rest1):
-    image = reduced(got)
+    image = reduced_halves(got)
     vec = v1[...]
     rest = image - coef(coefs, 1) * v0[...] - coef(coefs, 0) * vec
     rest1[...] = rest
     spread(msg, image, inner_rows(vec, image, rest))
 
 
-def reduce2_kernel(got, v2, v1, coefs, msg):
-    image = reduced(got)
+def reduce2_kernel(got, v2, v1, coefs, msg, rest2):
+    image = reduced_halves(got)
     vec = v2[...]
     rest = image - coef(coefs, 3) * v1[...] - coef(coefs, 1) * vec
-    half = SEC * SLAB
-    tile = split_rows(inner_rows(vec, image, rest))
-    for c in range(2):
-        rounded = rest[half * c : half * (c + 1)].astype(BF16)
-        for z in range(NZ):
-            msg[c * NZ + z, :half] = rounded
-            msg[c * NZ + z, half:] = tile
-
-
-def sums_kernel(got, msg):
-    half = SEC * SLAB
-    acc = got[0, half:].astype(F32)
-    for s in range(1, GRP):
-        acc = acc + got[s, half:].astype(F32)
+    rest2[...] = rest
+    rows = [summed_tile(got, 16)[0]] + inner_rows(vec, image, rest)[1:]
     at = iota((8, W), 0)
     tile = jnp.zeros((8, W), F32)
-    for k, row in enumerate(join_rows(acc)):
+    for k, row in enumerate(rows):
         tile = jnp.where(at == k, jnp.broadcast_to(row, (8, W)), tile)
     for n in range(CHIPS):
         msg[n] = tile
 
 
-def finish_kernel(got, sums, own, coefs, vec_out, coef_out, dens_out, rest2):
-    acc = sums[0]
+def residual_kernel(got, rest2, v2, coefs, msg, last):
+    acc = got[0]
     for n in range(1, CHIPS):
-        acc = acc + sums[n]
-    vw, vr, rr, vv = half_totals([acc[k : k + 1] for k in range(2)])
+        acc = acc + got[n]
+    a2 = total(acc[0:1]) / COUNT
+    d = a2 - coef(coefs, 1)
+    put_coefs(last, (a2, d))
+    rounded = (rest2[...] - d * v2[...]).astype(BF16)
+    tile = split_rows([acc[k : k + 1] for k in range(1, 4)])
+    half = SEC * SLAB
+    for c in range(2):
+        for z in range(NZ):
+            msg[c * NZ + z, :half] = rounded[half * c : half * (c + 1)]
+            msg[c * NZ + z, half:] = tile
+
+
+def finish_kernel(got, coefs, last, vec_out, coef_out, dens_out, rest):
+    vr, rr, vv, _ = half_totals(summed_tile(got, SEC * SLAB))
     a0, a1, b1, b2 = [coef(coefs, k) for k in range(4)]
-    a2 = vw / COUNT
-    d = a2 - a1
-    rest = rr - 2.0 * d * vr + d * d * vv
-    b3 = jnp.sqrt(jnp.maximum(rest, 0.0) / COUNT + EPS)
+    a2, d = coef(last, 0), coef(last, 1)
+    norm = rr - 2.0 * d * vr + d * d * vv
+    b3 = jnp.sqrt(jnp.maximum(norm, 0.0) / COUNT + EPS)
     for k, v in enumerate((a0, a1, a2, b1, b2, b3)):
         coef_out[k] = v[0, 0]
     wc = 1.0 / b3
-    vc = d * wc
     for s in range(GRP):
         for pair in range(SEC // 2):
             tile = got[s, 16 * pair : 16 * (pair + 1)].astype(F32)
             for k in range(2):
-                rest2[2 * pair + k, SLAB * s : SLAB * (s + 1), :] = tile[SLAB * k : SLAB * (k + 1)]
+                rest[2 * pair + k, SLAB * s : SLAB * (s + 1), :] = tile[SLAB * k : SLAB * (k + 1)]
     for i in range(SEC):
-        v = rest2[i] * wc - own[i] * vc
+        v = rest[i] * wc
         vec_out[i] = v
         dens_out[i] = (
             lax.dot_general(
@@ -403,8 +483,8 @@
     return lax.all_to_all(x, "sector", 0, 0, axis_index_groups=XY_GROUPS)
 
 
-def select(got, wide):
-    return call(select_kernel, [((GRP, NBLK * SLAB + 8, W), BF16)], [VMEM, VMEM])(got, wide)[0]
+def select(got, ones):
+    return call(select_kernel, [((GRP, NEAR * SLAB + 8, W), BF16)], [VMEM, VMEM])(got, ones)[0]
 
 
 def per_device(theta, left, right, perm, dims):
@@ -421,76 +501,87 @@
     dims = dims.T
     any_space = pl.BlockSpec(memory_space=pl.ANY)
     pieces = 2 * CHIPS
-    sems = pltpu.SemaphoreType.DMA((SEC + 1,))
-
-    msg, keep, send, limits = call(
+    away_type = ((2, TERMS_DEV, W, W), BF16)
+    near_type = ((HELD, 2, TERMS_DEV, W, W), BF16)
+    sems = pltpu.SemaphoreType.DMA((SEC + 1 + 2 * HELD,))
+
+    msg, keep, send, limits, down, up = call(
         start_kernel,
-        [((pieces, 16, W), BF16), (half, F32), (half, F32), ((8, W), jnp.int32)],
-        [any_space, any_space],
-        [pltpu.VMEM((SEC, W, W), F32), pltpu.SMEM((2, SEC), jnp.int32), sems],
+        [((pieces, 16, W), BF16), (half, F32), (half, F32), ((8, W), jnp.int32), away_type, away_type],
+        [any_space] * 4,
+        [
+            pltpu.VMEM((SEC, W, W), F32),
+            pltpu.SMEM((2, SEC), jnp.int32),
+            pltpu.VMEM(*near_type),
+            sems,
+            pltpu.SemaphoreType.DMA((2 * HELD,)),
+        ],
+        out_specs=[VMEM] * 4 + [any_space] * 2,
         limit=60,
-    )(theta, dims)
+    )(theta, dims, left, right)
+    above = lax.ppermute(down, "op", DOWN)
+    below = lax.ppermute(up, "op", UP)
     got = lax.all_to_all(msg, "sector", 0, 0)
-    hits, wide = call(
-        hits_kernel, [((3 * W, W), BF16), ((WIDE, SLAB * W), BF16)], [VMEM]
-    )(perm.reshape(1, W))
-    (right,) = call(load_kernel, [((SEC, TERMS_DEV, W, W), BF16)], [any_space], [sems])(right)
+    (ones,) = call(hits_kernel, [((WIDE + 3 * W // SLAB, SLAB * W), BF16)], [VMEM])(perm.reshape(1, W))
     came = lax.ppermute(send, "sector", SWAP)
     (msg,) = call(
         pick_kernel,
         [((pieces, 4 * NBLK, W), BF16)],
         [VMEM, VMEM, any_space, any_space],
         [pltpu.VMEM((pieces * 16, W), F32), pltpu.VMEM((pieces * 4 * NBLK, W), F32)],
-    )(got, hits, came, right)
+    )(got, ones, came, right)
     got = lax.all_to_all(msg, "sector", 0, 0)
-    msg, blk0 = call(
+    msg, blk0, near = call(
         ham0_kernel,
-        [scatter, blocks],
-        [VMEM] * 4,
+        [scatter, blocks, near_type],
+        [VMEM] * 4 + [any_space] * 2,
+        acc + [pltpu.SemaphoreType.DMA((2 * HELD,))],
+        flops,
+        nbytes,
+        limit=20,
+    )(limits, got, left, right, above, below)
+    msg, image0, slab0 = call(reduce0_kernel, [plane, (slab, F32), (slab, F32)], [VMEM] * 3)(
+        over_cz(msg), keep, came
+    )
+
+    held = ((NEAR, W, W), F32)
+    acc = [pltpu.VMEM((HELD, W, W), F32)]
+    got = over_cz(select(over_xy(msg), ones))
+    msg, blk1, v0, v1, co = call(
+        ham1_kernel,
+        [((GRP, 16, W), BF16), held, (slab, F32), (slab, F32), coefs],
+        [VMEM] * 8,
         acc,
         flops,
         nbytes,
-        limit=16,
-    )(limits, got, left, right)
-    msg, image0, slab0 = call(reduce0_kernel, [plane, (slab, F32), (slab, F32)], [VMEM] * 3)(
-        over_cz(msg), keep, came
-    )
-
-    got = over_cz(select(over_xy(msg), wide))
-    msg, blk1, v0, v1, co = call(
-        ham1_kernel,
-        [scatter, blocks, (slab, F32), (slab, F32), coefs],
-        [VMEM] * 7,
-        acc,
+        limit=20,
+    )(limits, got, left, right, near, blk0, slab0, image0)
+    msg, rest1 = call(reduce1_kernel, [plane, (slab, F32)], [VMEM] * 4)(over_cz(msg), v1, v0, co)
+
+    got = over_cz(select(over_xy(msg), ones))
+    msg, v2, co = call(
+        ham2_kernel,
+        [((GRP, 24, W), BF16), (slab, F32), coefs],
+        [VMEM] * 10,
+        [pltpu.VMEM((NEAR, W, W), F32)] + acc,
         flops,
         nbytes,
-        limit=16,
-    )(limits, got, left, right, blk0, slab0, image0)
-    msg, rest1 = call(reduce1_kernel, [plane, (slab, F32)], [VMEM] * 4)(over_cz(msg), v1, v0, co)
-
-    got = over_cz(select(over_xy(msg), wide))
-    msg, own, v2, co = call(
-        ham2_kernel,
-        [scatter, ((SEC, W, W), F32), (slab, F32), coefs],
-        [VMEM] * 9,
-        [pltpu.VMEM((NBLK, W, W), F32)] + acc,
-        flops,
-        nbytes,
-        limit=16,
-    )(limits, got, left, right, blk1, blk0, v1, rest1, co)
-    (msg,) = call(reduce2_kernel, [((GRP, SEC * SLAB + 8, W), BF16)], [VMEM] * 4)(
+        limit=20,
+    )(limits, got, left, right, near, blk1, blk0, v1, rest1, co)
+    msg, rest2 = call(reduce2_kernel, [((CHIPS, 8, W), F32), (slab, F32)], [VMEM] * 4)(
         over_cz(msg), v2, v1, co
     )
 
-    got = over_cz(msg)
-    (msg,) = call(sums_kernel, [((CHIPS, 8, W), F32)], [VMEM])(got)
+    msg, last = call(residual_kernel, [((GRP, SEC * SLAB + 8, W), BF16), coefs], [VMEM] * 4)(
+        over_xy(msg), rest2, v2, co
+    )
     return call(
         finish_kernel,
         [((SEC, W, W), F32), ((6,), F32), ((SEC, W, W), F32)],
-        [VMEM] * 4,
-        acc,
+        [VMEM] * 3,
+        [pltpu.VMEM((SEC, W, W), F32)],
         out_specs=[VMEM, SMEM, VMEM],
-    )(got, over_xy(msg), own, co)
+    )(over_cz(msg), co, last)
 
 
 def solution(mesh):

time: 163 us -> 157 us (0.963); the launches traced: 161 us -> 157 us
  blocking collectives: 135 us -> 122 us
  starting transfers between devices: 8.92 us -> 14.8 us
  waiting for transfers between devices: 4.51 us -> 6.98 us
  Pallas kernels: 9.95 us -> 12.2 us
  local copies, waits for them, and re-layouts: 2.25 us -> 0.02 us
    all_to_all x6, blocking collectives: 90 us -> 77.3 us  [over_cz(): return lax.all_to_all(x, BOTH, 0, 0, axis_index_groups=CZ_GROUPS)]
    ppermute x0 -> x2, starting transfers between devices: none -> 6.48 us  [the longest x1 6.48 us: per_device(): above = lax.ppermute(down, 'op', DOWN)]
    unnamed x10, local copies, waits for them, and re-layouts: 2.25 us -> 0.02 us
    pallas_call x1, Pallas kernels: 1.68 us -> 3.44 us  [per_device(): call(start_kernel, [((pieces, 16, W), BF16), (half, F32), (half, F32), ((...]
    all_to_all x1, waiting for transfers between devices: 4.51 us -> 6.22 us  [per_device(): got = lax.all_to_all(msg, 'sector', 0, 0)]
    pallas_call x9 -> x8, Pallas kernels: 6.18 us -> 6.66 us  [the longest x1 2.46 us: per_device(): call(ham0_kernel, [scatter, blocks, near_type], [VMEM] * 4 + [any_space]...]
  transfers between devices with their start and end apart: 2 -> 4, of which waited for: 1 -> 2; matrix products, arithmetic and copies ran while one was open for 0% -> 0% of each run, Pallas kernels for 0% -> 0%
where the time goes in v4:
time: 157 us
  blocking collectives  122 us (78%)
  starting transfers between devices  14.8 us (9%)
  Pallas kernels  12.2 us (8%)
  waiting for transfers between devices  6.98 us (4%)
    all_to_all x6, blocking collectives, over_cz(): return lax.all_to_all(x, BOTH, 0, 0, axis_index_groups=CZ_GROUPS)  77.3 us
    all_to_all x3, blocking collectives, over_xy(): return lax.all_to_all(x, 'sector', 0, 0, axis_index_groups=XY_GROUPS)  30.8 us
    all_to_all x1, blocking collectives, per_device(): got = lax.all_to_all(msg, 'sector', 0, 0)  14 us
    all_to_all x1, starting transfers between devices, per_device(): got = lax.all_to_all(msg, 'sector', 0, 0)  8.04 us
    ppermute x1, starting transfers between devices, per_device(): above = lax.ppermute(down, 'op', DOWN)  6.48 us
    all_to_all x1, waiting for transfers between devices, per_device(): got = lax.all_to_all(msg, 'sector', 0, 0)  6.22 us
    pallas_call x1, Pallas kernels, per_device(): call(start_kernel, [((pieces, 16, W), BF16), (half, F32), (half, F32), ((...  3.44 us
  transfers between devices with their start and end apart: 4, of which 2 were waited for; matrix products, arithmetic and copies ran while one was open for 0% of the time, Pallas kernels for 0%

profile of v4, /device:TPU:1, one launch (start us, length us, event | category | flops | bytes accessed | tf_op | source)
XLA Modules:
  0.0 156.8 jit_solution(11321700287374193705)
XLA Ops:
  0.6 0.0 copy-start.4
  0.6 0.0 copy-start
  0.7 3.4 %shard_map.76 = (bf16[32,16,128]{2,1,0:T(8,128)(2,1)}, f32[32,128]{1,0:T(8,128)}, f32[32,128]{1,0:T(8,128)}, s32[8,128]{1,0:T(8,128)}, bf16[2,16,128,128]{3,2,1,...) custom-call(f32[4,128,128]{2,1,0:T(8,128)} %theta.1, s32[2,4]{1,0:T(2,128)} %bitcast.3, bf16[4,16,128,128]{3,2,1,0:T(8,128)(2,1)} %left.7, ...), custom_call_target="tpu_custom_call" | custom-call | bytes 262144 | tf_op jit(solution)/shard_map/pallas_call | solution.py:508
  4.1 6.5 %collective-permute-start.1 = (bf16[2,16,128,128]{3,2,1,0:T(8,128)(2,1)}, bf16[2,16,128,128]{3,2,1,0:T(8,128)(2,1)}, u32[]{:S(2)}, u32[]{:S(2)}) collective-permute-start(bf16[2,16,128,128]{3,2,1,0:T(8,128)(2,1)} %get-tuple-element.32), channel_id=1, source_target_pairs={{0,7},{1,0},{2,1},{3,2},{4,3},{5,4},{6,5},{7,6},{8,15},{9,8},{10,9... | collective-permute-start | bytes 3145736 | tf_op jit(solution)/shard_map/ppermute | solution.py:522
  10.6 0.0 collective-permute-start.2
  10.6 8.0 %all-to-all-start = ((bf16[32,16,128]{2,1,0:T(8,128)(2,1)}), bf16[32,16,128]{2,1,0:T(8,128)(2,1)S(1)}, u32[]{:S(2)}, u32[]{:S(2)}) async-start(bf16[32,16,128]{2,1,0:T(8,128)(2,1)} %get-tuple-element.30), calls=%async_computation | async-start | bytes 262144 | tf_op jit(solution)/shard_map/all_to_all | solution.py:524
  18.6 0.3 collective-permute-start
  19.0 0.0 copy-done.4
  19.0 0.0 copy-start.2
  19.0 0.4 shard_map.77.ones
  19.4 0.8 collective-permute-done.came
  20.1 6.2 %all-to-all-done.got = bf16[32,16,128]{2,1,0:T(8,128)(2,1)S(1)} async-done(((bf16[32,16,128]{2,1,0:T(8,128)(2,1)}), bf16[32,16,128]{2,1,0:T(8,128)(2,1)S(1)}, u32[]{:S(2)}, u32[]{:S(2)}) %all-to-all-start) | async-done | bytes 131104 | tf_op jit(solution)/shard_map/all_to_all | solution.py:524
  26.3 0.0 copy-done
  26.3 0.0 copy-start.1
  26.3 0.3 shard_map.78
  26.6 14.0 %all_to_all.55.got = bf16[32,48,128]{2,1,0:T(8,128)(2,1)S(1)} all-to-all(bf16[32,48,128]{2,1,0:T(8,128)(2,1)S(1)} %shard_map.78), channel_id=1, replica_groups=mesh['sector'=32,'op'=8] {'sector'}, dimensions={0} | all-to-all | bytes 786432 | tf_op jit(solution)/shard_map/all_to_all | solution.py:533
  40.6 0.0 collective-permute-done.1.above
  40.7 0.0 collective-permute-done.2.below
  40.7 0.0 copy-done.2
  40.7 0.0 copy-done.1
  40.7 0.0 copy-start.3
  40.7 2.5 %shard_map.79 = (bf16[16,32,128]{2,1,0:T(8,128)(2,1)S(1)}, f32[12,128,128]{2,1,0:T(8,128)S(1)}, bf16[2,2,16,128,128]{4,3,2,1,0:T(8,128)(2,1)S(1)}) custom-call(s32[8,128]{1,0:T(8,128)S(1)} %copy-done.2, bf16[32,48,128]{2,1,0:T(8,128)(2,1)S(1)} %all_to_all.55.got, bf16[4,16,128,128]{3,2,1,0:T(8,128)(2,1)S(1)} %copy-done.1, ...), custom_call_target="tpu_custom_call" | custom-call | flops 536870912 | bytes 6291456 | tf_op jit(solution)/shard_map/pallas_call | solution.py:534
  43.2 11.8 %all_to_all.56.got = bf16[16,32,128]{2,1,0:T(8,128)(2,1)S(1)} all-to-all(bf16[16,32,128]{2,1,0:T(8,128)(2,1)S(1)} %get-tuple-element.34), channel_id=1, replica_groups={{0,1,2,3,4,5,6,7,8,9,10,11,12,13,14,15},{16,17,18,19,20,21,22,23,24,25,..., dimensions={0} | all-to-all | bytes 262144 | tf_op jit(solution)/shard_map/all_to_all | solution.py:479
  55.0 0.0 copy-done.3
  55.0 0.1 shard_map.80
  55.1 10.4 %all_to_all.57.got = bf16[16,72,128]{2,1,0:T(8,128)(2,1)S(1)} all-to-all(bf16[16,72,128]{2,1,0:T(8,128)(2,1)S(1)} %get-tuple-element.36), channel_id=1, replica_groups={{0,16,32,48,64,80,96,112,128,144,160,176,192,208,224,240},{8,24,40,56,7..., dimensions={0} | all-to-all | bytes 589824 | tf_op jit(solution)/shard_map/all_to_all | solution.py:483
  65.5 0.2 shard_map.81
  65.8 15.0 %all_to_all.58.got = bf16[16,56,128]{2,1,0:T(8,128)(2,1)S(1)} all-to-all(bf16[16,56,128]{2,1,0:T(8,128)(2,1)S(1)} %shard_map.81), channel_id=1, replica_groups={{0,1,2,3,4,5,6,7,8,9,10,11,12,13,14,15},{16,17,18,19,20,21,22,23,24,25,..., dimensions={0} | all-to-all | bytes 458752 | tf_op jit(solution)/shard_map/all_to_all | solution.py:479
  80.8 1.5 shard_map.82
  82.3 11.8 %all_to_all.59.got = bf16[16,16,128]{2,1,0:T(8,128)(2,1)S(1)} all-to-all(bf16[16,16,128]{2,1,0:T(8,128)(2,1)S(1)} %get-tuple-element.41), channel_id=1, replica_groups={{0,1,2,3,4,5,6,7,8,9,10,11,12,13,14,15},{16,17,18,19,20,21,22,23,24,25,..., dimensions={0} | all-to-all | bytes 131072 | tf_op jit(solution)/shard_map/all_to_all | solution.py:479
  94.1 0.1 shard_map.83
  94.2 10.7 %all_to_all.60.got = bf16[16,72,128]{2,1,0:T(8,128)(2,1)S(1)} all-to-all(bf16[16,72,128]{2,1,0:T(8,128)(2,1)S(1)} %get-tuple-element.45), channel_id=1, replica_groups={{0,16,32,48,64,80,96,112,128,144,160,176,192,208,224,240},{8,24,40,56,7..., dimensions={0} | all-to-all | bytes 589824 | tf_op jit(solution)/shard_map/all_to_all | solution.py:483
  104.9 0.2 shard_map.84
  105.2 13.9 %all_to_all.61.got = bf16[16,56,128]{2,1,0:T(8,128)(2,1)S(1)} all-to-all(bf16[16,56,128]{2,1,0:T(8,128)(2,1)S(1)} %shard_map.84), channel_id=1, replica_groups={{0,1,2,3,4,5,6,7,8,9,10,11,12,13,14,15},{16,17,18,19,20,21,22,23,24,25,..., dimensions={0} | all-to-all | bytes 458752 | tf_op jit(solution)/shard_map/all_to_all | solution.py:479
  119.0 1.6 %shard_map.85 = (bf16[16,24,128]{2,1,0:T(8,128)(2,1)S(1)}, f32[64,128]{1,0:T(8,128)S(1)}, f32[8,128]{1,0:T(8,128)S(1)}) custom-call(s32[8,128]{1,0:T(8,128)S(1)} %copy-done.2, bf16[16,56,128]{2,1,0:T(8,128)(2,1)S(1)} %all_to_all.61.got, bf16[4,16,128,128]{3,2,1,0:T(8,128)(2,1)S(1)} %copy-done.1, bf16[4,16,128,128]{3,2,1,0:T(8,128)(2,1)S(1)} %copy-done, ...), custom_call_target="tpu_custom_call" | custom-call | flops 536870912 | bytes 6291456 | tf_op jit(solution)/shard_map/pallas_call | solution.py:562
  120.7 12.0 %all_to_all.62.got = bf16[16,24,128]{2,1,0:T(8,128)(2,1)S(1)} all-to-all(bf16[16,24,128]{2,1,0:T(8,128)(2,1)S(1)} %get-tuple-element.48), channel_id=1, replica_groups={{0,1,2,3,4,5,6,7,8,9,10,11,12,13,14,15},{16,17,18,19,20,21,22,23,24,25,..., dimensions={0} | all-to-all | bytes 196608 | tf_op jit(solution)/shard_map/all_to_all | solution.py:479
  132.6 0.1 shard_map.86
  132.7 9.7 %all_to_all.63.got = f32[16,8,128]{2,1,0:T(8,128)S(1)} all-to-all(f32[16,8,128]{2,1,0:T(8,128)S(1)} %get-tuple-element.51), channel_id=1, replica_groups={{0,16,32,48,64,80,96,112,128,144,160,176,192,208,224,240},{8,24,40,56,7..., dimensions={0} | all-to-all | bytes 131072 | tf_op jit(solution)/shard_map/all_to_all | solution.py:483
  142.4 0.1 shard_map.87
  142.5 12.8 %all_to_all.64.got = bf16[16,40,128]{2,1,0:T(8,128)(2,1)S(1)} all-to-all(bf16[16,40,128]{2,1,0:T(8,128)(2,1)S(1)} %get-tuple-element.53), channel_id=1, replica_groups={{0,1,2,3,4,5,6,7,8,9,10,11,12,13,14,15},{16,17,18,19,20,21,22,23,24,25,..., dimensions={0} | all-to-all | bytes 327680 | tf_op jit(solution)/shard_map/all_to_all | solution.py:479
  155.3 1.5 shard_map.88
Async XLA Ops:
  0.6 18.3 %copy-start.4 = (s32[128]{0:T(128)S(1)}, s32[128]{0:T(128)}, u32[]{:S(2)}) copy-start(s32[128]{0:T(128)} %param.8) | copy-start | bytes 1540
  0.6 25.7 %copy-start = (bf16[4,16,128,128]{3,2,1,0:T(8,128)(2,1)S(1)}, bf16[4,16,128,128]{3,2,1,0:T(8,128)(2,1)}, u32[]{:S(2)}) copy-start(bf16[4,16,128,128]{3,2,1,0:T(8,128)(2,1)} %right.7) | copy-start | bytes 6291460
  4.1 36.6 %collective-permute-start.1 = (bf16[2,16,128,128]{3,2,1,0:T(8,128)(2,1)}, bf16[2,16,128,128]{3,2,1,0:T(8,128)(2,1)}, u32[]{:S(2)}, u32[]{:S(2)}) collective-permute-start(bf16[2,16,128,128]{3,2,1,0:T(8,128)(2,1)} %get-tuple-element.32), channel_id=1, source_target_pairs={{0,7},{1,0},{2,1},{3,2},{4,3},{5,4},{6,5},{7,6},{8,15},{9,8},{10,9... | collective-permute-start | bytes 3145736 | tf_op jit(solution)/shard_map/ppermute | solution.py:522
  10.6 30.1 %collective-permute-start.2 = (bf16[2,16,128,128]{3,2,1,0:T(8,128)(2,1)}, bf16[2,16,128,128]{3,2,1,0:T(8,128)(2,1)}, u32[]{:S(2)}, u32[]{:S(2)}) collective-permute-start(bf16[2,16,128,128]{3,2,1,0:T(8,128)(2,1)} %get-tuple-element.33), channel_id=1, source_target_pairs={{0,1},{1,2},{2,3},{3,4},{4,5},{5,6},{6,7},{7,0},{8,9},{9,10},{10,1... | collective-permute-start | bytes 3145736 | tf_op jit(solution)/shard_map/ppermute | solution.py:523
  10.6 15.8 %all-to-all-start = ((bf16[32,16,128]{2,1,0:T(8,128)(2,1)}), bf16[32,16,128]{2,1,0:T(8,128)(2,1)S(1)}, u32[]{:S(2)}, u32[]{:S(2)}) async-start(bf16[32,16,128]{2,1,0:T(8,128)(2,1)} %get-tuple-element.30), calls=%async_computation | async-start | bytes 262144 | tf_op jit(solution)/shard_map/all_to_all | solution.py:524
  18.6 1.5 collective-permute-start
  19.0 21.7 %copy-start.2 = (s32[8,128]{1,0:T(8,128)S(1)}, s32[8,128]{1,0:T(8,128)}, u32[]{:S(2)}) copy-start(s32[8,128]{1,0:T(8,128)} %get-tuple-element.29.limits) | copy-start | bytes 12292
  26.3 14.3 %copy-start.1 = (bf16[4,16,128,128]{3,2,1,0:T(8,128)(2,1)S(1)}, bf16[4,16,128,128]{3,2,1,0:T(8,128)(2,1)}, u32[]{:S(2)}) copy-start(bf16[4,16,128,128]{3,2,1,0:T(8,128)(2,1)} %left.7) | copy-start | bytes 6291460
  40.7 14.3 %copy-start.3 = (f32[32,128]{1,0:T(8,128)S(1)}, f32[32,128]{1,0:T(8,128)}, u32[]{:S(2)}) copy-start(f32[32,128]{1,0:T(8,128)} %get-tuple-element.35.keep) | copy-start | bytes 49156

commit v5 on v4

--- a/solution.py
+++ b/solution.py
@@ -155,11 +155,15 @@
         out.wait()
 
 
-def wanted(perm, count, first, shift):
+def wanted(perm, count, first, shift, sides):
     shape = (count, W)
     row = lax.shift_right_logical(iota(shape, 0), shift)
-    at = lax.shift_right_logical(row * 21846, 16)
-    q = row - 3 * at
+    if sides:
+        at = lax.shift_right_logical(row, 1)
+        q = 2 * lax.bitwise_and(row, 1)
+    else:
+        at = lax.shift_right_logical(row * 21846, 16)
+        q = row - 3 * at
     held = jnp.broadcast_to(perm[...].astype(F32), shape)
     mine = jnp.sum(jnp.where(iota(shape, 1) == at + first, held, 0.0), axis=1, keepdims=True)
     want = mine + q.astype(F32) - 1.0
@@ -169,12 +173,12 @@
 
 
 def hits_kernel(perm, ones):
-    hits = wanted(perm, 3 * W, 0, 0)
-    part = 3 * W // SLAB
+    hits = wanted(perm, 2 * W, 0, 0, True)
+    part = 2 * W // SLAB
     for k in range(SLAB):
         ones[WIDE:, W * k : W * (k + 1)] = hits[part * k : part * (k + 1)]
     chip = lax.axis_index("sector") // 2
-    near = wanted(perm, WIDE, chip * 2 * SEC, 3)
+    near = wanted(perm, WIDE, chip * 2 * SEC, 3, False)
     cols = (W, SLAB * W)
     spread_out = (lax.shift_right_logical(iota(cols, 1), 3) == iota(cols, 0)).astype(F32).astype(BF16)
     both = jnp.dot(near, spread_out, preferred_element_type=F32)
@@ -189,20 +193,25 @@
     hits = jnp.concatenate([ones[WIDE:, W * k : W * (k + 1)] for k in range(SLAB)], axis=0)
     for r in range(4):
         part = pieces[pl.ds(r, W, stride=4), :].astype(BF16)
-        picked[pl.ds(r, 3 * W, stride=4), :] = jnp.dot(hits, part, preferred_element_type=F32)
+        picked[pl.ds(r, 2 * W, stride=4), :] = jnp.dot(hits, part, preferred_element_type=F32)
     for g in range(2 * CHIPS):
-        msg[g] = picked[48 * g : 48 * (g + 1)].astype(BF16)
-
-
-def assemble_pieces(got, out):
+        msg[g] = picked[32 * g : 32 * (g + 1)].astype(BF16)
+
+
+def assemble_pieces(got, theta, limits, out):
     for t in range(GRP):
         low = got[2 * t].astype(F32)
         high = got[2 * t + 1].astype(F32)
-        for m in range(NBLK // 2):
-            at = slice(SLAB * m, SLAB * (m + 1))
+        for i in range(SEC):
+            at = slice(SLAB * i, SLAB * (i + 1))
             two = low_high(low[at], high[at])
             for k in range(2):
-                out[2 * m + k, SLAB * t : SLAB * (t + 1), :] = two[k]
+                out[3 * i + 2 * k, SLAB * t : SLAB * (t + 1), :] = two[k]
+    rows = iota((W, W), 0)
+    cols = iota((W, W), 1)
+    for i in range(SEC):
+        inside = (rows < coef(limits, 2 * i)) & (cols < coef(limits, 2 * i + 1))
+        out[3 * i + 1] = jnp.where(inside, theta[i], 0.0)
 
 
 def select_kernel(got, ones, msg):
@@ -313,9 +322,9 @@
     return ref[k : k + 1, 0:1]
 
 
-def ham0_kernel(limits, got, left, right, above, below, msg, blk, near, acc, sems):
+def ham0_kernel(limits, theta, got, left, right, above, below, msg, blk, near, acc, sems):
     copies = start_copies(above, below, near, sems)
-    assemble_pieces(got, blk)
+    assemble_pieces(got, theta, limits, blk)
     products(limits, blk, left, right, msg, acc)
     for copy in copies:
         copy.wait()
@@ -467,12 +476,14 @@
     for i in range(SEC):
         v = rest[i] * wc
         vec_out[i] = v
-        dens_out[i] = (
-            lax.dot_general(
-                v, v, (((1,), (1,)), ((), ())), precision=lax.Precision.HIGHEST, preferred_element_type=F32
-            )
-            / W
-        )
+        high = v.astype(BF16)
+        low = (v - high.astype(F32)).astype(BF16)
+        dens_out[i] = lax.dot_general(
+            jnp.concatenate([high, high, low], axis=1),
+            jnp.concatenate([high, low, high], axis=1),
+            (((1,), (1,)), ((), ())),
+            preferred_element_type=F32,
+        ) * (1.0 / W)
 
 
 def over_cz(x):
@@ -522,24 +533,24 @@
     above = lax.ppermute(down, "op", DOWN)
     below = lax.ppermute(up, "op", UP)
     got = lax.all_to_all(msg, "sector", 0, 0)
-    (ones,) = call(hits_kernel, [((WIDE + 3 * W // SLAB, SLAB * W), BF16)], [VMEM])(perm.reshape(1, W))
+    (ones,) = call(hits_kernel, [((WIDE + 2 * W // SLAB, SLAB * W), BF16)], [VMEM])(perm.reshape(1, W))
     came = lax.ppermute(send, "sector", SWAP)
     (msg,) = call(
         pick_kernel,
-        [((pieces, 4 * NBLK, W), BF16)],
+        [((pieces, 8 * SEC, W), BF16)],
         [VMEM, VMEM, any_space, any_space],
-        [pltpu.VMEM((pieces * 16, W), F32), pltpu.VMEM((pieces * 4 * NBLK, W), F32)],
+        [pltpu.VMEM((pieces * 16, W), F32), pltpu.VMEM((pieces * 8 * SEC, W), F32)],
     )(got, ones, came, right)
     got = lax.all_to_all(msg, "sector", 0, 0)
     msg, blk0, near = call(
         ham0_kernel,
         [scatter, blocks, near_type],
-        [VMEM] * 4 + [any_space] * 2,
+        [VMEM] * 5 + [any_space] * 2,
         acc + [pltpu.SemaphoreType.DMA((2 * HELD,))],
         flops,
         nbytes,
         limit=20,
-    )(limits, got, left, right, above, below)
+    )(limits, theta, got, left, right, above, below)
     msg, image0, slab0 = call(reduce0_kernel, [plane, (slab, F32), (slab, F32)], [VMEM] * 3)(
         over_cz(msg), keep, came
     )

time: 157 us -> 156 us (level)
  no operation moved by 1% of the time
where the time goes in v5:
time: 156 us; the launch traced here: 155 us
  blocking collectives  121 us (78%)
  starting transfers between devices  15 us (10%)
  Pallas kernels  11.7 us (8%)
  waiting for transfers between devices  7.03 us (5%)
    all_to_all x6, blocking collectives, over_cz(): return lax.all_to_all(x, BOTH, 0, 0, axis_index_groups=CZ_GROUPS)  77.3 us
    all_to_all x3, blocking collectives, over_xy(): return lax.all_to_all(x, 'sector', 0, 0, axis_index_groups=XY_GROUPS)  30.9 us
    all_to_all x1, blocking collectives, per_device(): got = lax.all_to_all(msg, 'sector', 0, 0)  12.7 us
    all_to_all x1, starting transfers between devices, per_device(): got = lax.all_to_all(msg, 'sector', 0, 0)  8.17 us
    ppermute x1, starting transfers between devices, per_device(): above = lax.ppermute(down, 'op', DOWN)  6.48 us
    all_to_all x1, waiting for transfers between devices, per_device(): got = lax.all_to_all(msg, 'sector', 0, 0)  6.22 us
    pallas_call x1, Pallas kernels, per_device(): call(start_kernel, [((pieces, 16, W), BF16), (half, F32), (half, F32), ((...  3.44 us
  transfers between devices with their start and end apart: 4, of which 2 were waited for; matrix products, arithmetic and copies ran while one was open for 0% of the time, Pallas kernels for 0%

profile of v5, /device:TPU:1, one launch (start us, length us, event | category | flops | bytes accessed | tf_op | source)
XLA Modules:
  0.0 155.4 jit_solution(7002542505190085388)
XLA Ops:
  0.6 0.0 copy-start.5
  0.6 0.0 copy-start
  0.7 3.4 %shard_map.76 = (bf16[32,16,128]{2,1,0:T(8,128)(2,1)}, f32[32,128]{1,0:T(8,128)}, f32[32,128]{1,0:T(8,128)}, s32[8,128]{1,0:T(8,128)}, bf16[2,16,128,128]{3,2,1,...) custom-call(f32[4,128,128]{2,1,0:T(8,128)} %theta.3, s32[2,4]{1,0:T(2,128)} %bitcast.3, bf16[4,16,128,128]{3,2,1,0:T(8,128)(2,1)} %left.7, ...), custom_call_target="tpu_custom_call" | custom-call | bytes 262144 | tf_op jit(solution)/shard_map/pallas_call | solution.py:519
  4.1 6.5 %collective-permute-start.1 = (bf16[2,16,128,128]{3,2,1,0:T(8,128)(2,1)}, bf16[2,16,128,128]{3,2,1,0:T(8,128)(2,1)}, u32[]{:S(2)}, u32[]{:S(2)}) collective-permute-start(bf16[2,16,128,128]{3,2,1,0:T(8,128)(2,1)} %get-tuple-element.32), channel_id=1, source_target_pairs={{0,7},{1,0},{2,1},{3,2},{4,3},{5,4},{6,5},{7,6},{8,15},{9,8},{10,9... | collective-permute-start | bytes 3145736 | tf_op jit(solution)/shard_map/ppermute | solution.py:533
  10.6 0.0 collective-permute-start.2
  10.6 0.0 copy-start.2
  10.6 0.0 copy-start.3
  10.6 8.2 %all-to-all-start = ((bf16[32,16,128]{2,1,0:T(8,128)(2,1)}), bf16[32,16,128]{2,1,0:T(8,128)(2,1)S(1)}, u32[]{:S(2)}, u32[]{:S(2)}) async-start(bf16[32,16,128]{2,1,0:T(8,128)(2,1)} %get-tuple-element.30), calls=%async_computation | async-start | bytes 262144 | tf_op jit(solution)/shard_map/all_to_all | solution.py:535
  18.8 0.3 collective-permute-start
  19.1 0.0 copy-done.5
  19.1 0.3 shard_map.77.ones
  19.4 0.8 collective-permute-done.came
  20.2 6.2 %all-to-all-done.got = bf16[32,16,128]{2,1,0:T(8,128)(2,1)S(1)} async-done(((bf16[32,16,128]{2,1,0:T(8,128)(2,1)}), bf16[32,16,128]{2,1,0:T(8,128)(2,1)S(1)}, u32[]{:S(2)}, u32[]{:S(2)}) %all-to-all-start) | async-done | bytes 131104 | tf_op jit(solution)/shard_map/all_to_all | solution.py:535
  26.5 0.0 copy-done
  26.5 0.0 copy-start.1
  26.5 0.2 shard_map.78
  26.7 12.7 %all_to_all.55.got = bf16[32,32,128]{2,1,0:T(8,128)(2,1)S(1)} all-to-all(bf16[32,32,128]{2,1,0:T(8,128)(2,1)S(1)} %shard_map.78), channel_id=1, replica_groups=mesh['sector'=32,'op'=8] {'sector'}, dimensions={0} | all-to-all | bytes 524288 | tf_op jit(solution)/shard_map/all_to_all | solution.py:544
  39.4 0.0 collective-permute-done.1.above
  39.4 0.0 collective-permute-done.2.below
  39.4 0.0 copy-done.2
  39.4 0.0 copy-done.3
  39.4 0.0 copy-done.1
  39.4 0.0 copy-start.4
  39.5 2.5 %shard_map.79 = (bf16[16,32,128]{2,1,0:T(8,128)(2,1)S(1)}, f32[12,128,128]{2,1,0:T(8,128)S(1)}, bf16[2,2,16,128,128]{4,3,2,1,0:T(8,128)(2,1)S(1)}) custom-call(s32[8,128]{1,0:T(8,128)S(1)} %copy-done.3, f32[4,128,128]{2,1,0:T(8,128)S(1)} %copy-done.2, bf16[32,32,128]{2,1,0:T(8,128)(2,1)S(1)} %all_to_all.55.got, bf16[4,16,128,128]{3,2,1,0:T(8,128)(2,1)S(1)} %copy-done.1, ...), custom_call_target="tpu_custom_call" | custom-call | flops 536870912 | bytes 6291456 | tf_op jit(solution)/shard_map/pallas_call | solution.py:545
  41.9 11.9 %all_to_all.56.got = bf16[16,32,128]{2,1,0:T(8,128)(2,1)S(1)} all-to-all(bf16[16,32,128]{2,1,0:T(8,128)(2,1)S(1)} %get-tuple-element.34), channel_id=1, replica_groups={{0,1,2,3,4,5,6,7,8,9,10,11,12,13,14,15},{16,17,18,19,20,21,22,23,24,25,..., dimensions={0} | all-to-all | bytes 262144 | tf_op jit(solution)/shard_map/all_to_all | solution.py:490
  53.8 0.0 copy-done.4
  53.9 0.1 shard_map.80
  54.0 10.5 %all_to_all.57.got = bf16[16,72,128]{2,1,0:T(8,128)(2,1)S(1)} all-to-all(bf16[16,72,128]{2,1,0:T(8,128)(2,1)S(1)} %get-tuple-element.36), channel_id=1, replica_groups={{0,16,32,48,64,80,96,112,128,144,160,176,192,208,224,240},{8,24,40,56,7..., dimensions={0} | all-to-all | bytes 589824 | tf_op jit(solution)/shard_map/all_to_all | solution.py:494
  64.4 0.2 shard_map.81
  64.7 15.0 %all_to_all.58.got = bf16[16,56,128]{2,1,0:T(8,128)(2,1)S(1)} all-to-all(bf16[16,56,128]{2,1,0:T(8,128)(2,1)S(1)} %shard_map.81), channel_id=1, replica_groups={{0,1,2,3,4,5,6,7,8,9,10,11,12,13,14,15},{16,17,18,19,20,21,22,23,24,25,..., dimensions={0} | all-to-all | bytes 458752 | tf_op jit(solution)/shard_map/all_to_all | solution.py:490
  79.7 1.5 shard_map.82
  81.2 11.8 %all_to_all.59.got = bf16[16,16,128]{2,1,0:T(8,128)(2,1)S(1)} all-to-all(bf16[16,16,128]{2,1,0:T(8,128)(2,1)S(1)} %get-tuple-element.41), channel_id=1, replica_groups={{0,1,2,3,4,5,6,7,8,9,10,11,12,13,14,15},{16,17,18,19,20,21,22,23,24,25,..., dimensions={0} | all-to-all | bytes 131072 | tf_op jit(solution)/shard_map/all_to_all | solution.py:490
  93.0 0.1 shard_map.83
  93.1 10.7 %all_to_all.60.got = bf16[16,72,128]{2,1,0:T(8,128)(2,1)S(1)} all-to-all(bf16[16,72,128]{2,1,0:T(8,128)(2,1)S(1)} %get-tuple-element.45), channel_id=1, replica_groups={{0,16,32,48,64,80,96,112,128,144,160,176,192,208,224,240},{8,24,40,56,7..., dimensions={0} | all-to-all | bytes 589824 | tf_op jit(solution)/shard_map/all_to_all | solution.py:494
  103.8 0.2 shard_map.84
  104.1 13.9 %all_to_all.61.got = bf16[16,56,128]{2,1,0:T(8,128)(2,1)S(1)} all-to-all(bf16[16,56,128]{2,1,0:T(8,128)(2,1)S(1)} %shard_map.84), channel_id=1, replica_groups={{0,1,2,3,4,5,6,7,8,9,10,11,12,13,14,15},{16,17,18,19,20,21,22,23,24,25,..., dimensions={0} | all-to-all | bytes 458752 | tf_op jit(solution)/shard_map/all_to_all | solution.py:490
  117.9 1.6 %shard_map.85 = (bf16[16,24,128]{2,1,0:T(8,128)(2,1)S(1)}, f32[64,128]{1,0:T(8,128)S(1)}, f32[8,128]{1,0:T(8,128)S(1)}) custom-call(s32[8,128]{1,0:T(8,128)S(1)} %copy-done.3, bf16[16,56,128]{2,1,0:T(8,128)(2,1)S(1)} %all_to_all.61.got, bf16[4,16,128,128]{3,2,1,0:T(8,128)(2,1)S(1)} %copy-done.1, bf16[4,16,128,128]{3,2,1,0:T(8,128)(2,1)S(1)} %copy-done, ...), custom_call_target="tpu_custom_call" | custom-call | flops 536870912 | bytes 6291456 | tf_op jit(solution)/shard_map/pallas_call | solution.py:573
  119.6 12.0 %all_to_all.62.got = bf16[16,24,128]{2,1,0:T(8,128)(2,1)S(1)} all-to-all(bf16[16,24,128]{2,1,0:T(8,128)(2,1)S(1)} %get-tuple-element.48), channel_id=1, replica_groups={{0,1,2,3,4,5,6,7,8,9,10,11,12,13,14,15},{16,17,18,19,20,21,22,23,24,25,..., dimensions={0} | all-to-all | bytes 196608 | tf_op jit(solution)/shard_map/all_to_all | solution.py:490
  131.5 0.1 shard_map.86
  131.6 9.7 %all_to_all.63.got = f32[16,8,128]{2,1,0:T(8,128)S(1)} all-to-all(f32[16,8,128]{2,1,0:T(8,128)S(1)} %get-tuple-element.51), channel_id=1, replica_groups={{0,16,32,48,64,80,96,112,128,144,160,176,192,208,224,240},{8,24,40,56,7..., dimensions={0} | all-to-all | bytes 131072 | tf_op jit(solution)/shard_map/all_to_all | solution.py:494
  141.3 0.1 shard_map.87
  141.4 12.8 %all_to_all.64.got = bf16[16,40,128]{2,1,0:T(8,128)(2,1)S(1)} all-to-all(bf16[16,40,128]{2,1,0:T(8,128)(2,1)S(1)} %get-tuple-element.53), channel_id=1, replica_groups={{0,1,2,3,4,5,6,7,8,9,10,11,12,13,14,15},{16,17,18,19,20,21,22,23,24,25,..., dimensions={0} | all-to-all | bytes 327680 | tf_op jit(solution)/shard_map/all_to_all | solution.py:490
  154.2 1.2 shard_map.88
Async XLA Ops:
  0.6 18.5 %copy-start.5 = (s32[128]{0:T(128)S(1)}, s32[128]{0:T(128)}, u32[]{:S(2)}) copy-start(s32[128]{0:T(128)} %param.8) | copy-start | bytes 1540
  0.6 25.8 %copy-start = (bf16[4,16,128,128]{3,2,1,0:T(8,128)(2,1)S(1)}, bf16[4,16,128,128]{3,2,1,0:T(8,128)(2,1)}, u32[]{:S(2)}) copy-start(bf16[4,16,128,128]{3,2,1,0:T(8,128)(2,1)} %right.7) | copy-start | bytes 6291460
  4.1 35.3 %collective-permute-start.1 = (bf16[2,16,128,128]{3,2,1,0:T(8,128)(2,1)}, bf16[2,16,128,128]{3,2,1,0:T(8,128)(2,1)}, u32[]{:S(2)}, u32[]{:S(2)}) collective-permute-start(bf16[2,16,128,128]{3,2,1,0:T(8,128)(2,1)} %get-tuple-element.32), channel_id=1, source_target_pairs={{0,7},{1,0},{2,1},{3,2},{4,3},{5,4},{6,5},{7,6},{8,15},{9,8},{10,9... | collective-permute-start | bytes 3145736 | tf_op jit(solution)/shard_map/ppermute | solution.py:533
  10.6 28.8 %collective-permute-start.2 = (bf16[2,16,128,128]{3,2,1,0:T(8,128)(2,1)}, bf16[2,16,128,128]{3,2,1,0:T(8,128)(2,1)}, u32[]{:S(2)}, u32[]{:S(2)}) collective-permute-start(bf16[2,16,128,128]{3,2,1,0:T(8,128)(2,1)} %get-tuple-element.33), channel_id=1, source_target_pairs={{0,1},{1,2},{2,3},{3,4},{4,5},{5,6},{6,7},{7,0},{8,9},{9,10},{10,1... | collective-permute-start | bytes 3145736 | tf_op jit(solution)/shard_map/ppermute | solution.py:534
  10.6 28.8 %copy-start.2 = (f32[4,128,128]{2,1,0:T(8,128)S(1)}, f32[4,128,128]{2,1,0:T(8,128)}, u32[]{:S(2)}) copy-start(f32[4,128,128]{2,1,0:T(8,128)} %theta.3) | copy-start | bytes 786436
  10.6 28.8 %copy-start.3 = (s32[8,128]{1,0:T(8,128)S(1)}, s32[8,128]{1,0:T(8,128)}, u32[]{:S(2)}) copy-start(s32[8,128]{1,0:T(8,128)} %get-tuple-element.29.limits) | copy-start | bytes 12292
  10.6 15.9 %all-to-all-start = ((bf16[32,16,128]{2,1,0:T(8,128)(2,1)}), bf16[32,16,128]{2,1,0:T(8,128)(2,1)S(1)}, u32[]{:S(2)}, u32[]{:S(2)}) async-start(bf16[32,16,128]{2,1,0:T(8,128)(2,1)} %get-tuple-element.30), calls=%async_computation | async-start | bytes 262144 | tf_op jit(solution)/shard_map/all_to_all | solution.py:535
  18.8 1.5 collective-permute-start
  26.5 13.0 %copy-start.1 = (bf16[4,16,128,128]{3,2,1,0:T(8,128)(2,1)S(1)}, bf16[4,16,128,128]{3,2,1,0:T(8,128)(2,1)}, u32[]{:S(2)}) copy-start(bf16[4,16,128,128]{3,2,1,0:T(8,128)(2,1)} %left.7) | copy-start | bytes 6291460
  39.4 14.4 %copy-start.4 = (f32[32,128]{1,0:T(8,128)S(1)}, f32[32,128]{1,0:T(8,128)}, u32[]{:S(2)}) copy-start(f32[32,128]{1,0:T(8,128)} %get-tuple-element.35.keep) | copy-start | bytes 49156

commit v6 on v5

--- a/solution.py
+++ b/solution.py
@@ -1,3 +1,5 @@
+import functools
+
 import jax
 import jax.numpy as jnp
 from jax import lax
@@ -214,7 +216,7 @@
         out[3 * i + 1] = jnp.where(inside, theta[i], 0.0)
 
 
-def select_kernel(got, ones, msg):
+def select_kernel(shifted, got, ones, msg):
     data = 2 * SEC * SLAB
     slabs = jnp.concatenate([got[n, :data] for n in range(CHIPS)], axis=0)
     picked = jnp.dot(ones[:WIDE], slabs, preferred_element_type=F32).astype(BF16)
@@ -222,12 +224,27 @@
     for n in range(1, CHIPS):
         acc = acc + got[n, data:].astype(F32)
     tile = split_again(join_rows(acc))
+    shifts = []
+    if shifted:
+        parts = []
+        for n in range(CHIPS):
+            row = got[n, data:].astype(F32)[6:7]
+            parts += [jnp.broadcast_to(row[:, W // 2 * c : W // 2 * c + 1], (SEC * SLAB, W)) for c in range(2)]
+        column = jnp.concatenate(parts, axis=0).astype(BF16)
+        needed = jnp.dot(ones[:WIDE], column, preferred_element_type=F32)
+        group = lax.shift_right_logical(iota((1, W), 1), 4)
+        for k in range(4):
+            row = jnp.zeros((1, W), F32)
+            for b in range(NEAR):
+                at = (NEAR * k + b) * SLAB
+                row = jnp.where(group == b, needed[at : at + 1], row)
+            shifts.append(jnp.where(iota((8, W), 0) == 6, row, tile.astype(F32)).astype(BF16))
     rows = NEAR * SLAB
     for c in range(2):
         for z in range(NZ):
             first = rows * (2 * c + z % 2)
             msg[c * NZ + z, :rows] = picked[first : first + rows]
-            msg[c * NZ + z, rows:] = tile
+            msg[c * NZ + z, rows:] = shifts[2 * c + z % 2] if shifted else tile
 
 
 def summed_tile(got, first):
@@ -245,7 +262,7 @@
                 out[2 * pair + k, SLAB * s : SLAB * (s + 1), :] = tile[SLAB * k : SLAB * (k + 1)]
 
 
-def products(limits, blocks, left, right, msg, acc):
+def products(limits, blocks, left, right, acc):
     _, z = core_and_z()
     rows = iota((W, W), 0)
     cols = iota((W, W), 1)
@@ -264,9 +281,12 @@
         out = jnp.dot(lhs, rhs, preferred_element_type=F32)
         inside = (rows < coef(limits, 2 * i)) & (cols < coef(limits, 2 * i + 1))
         acc[i] = jnp.where(inside, out * SCALE, 0.0)
+
+
+def pack(acc, msg):
     for s in range(GRP):
         at = slice(SLAB * s, SLAB * (s + 1))
-        for pair in range(SEC // 2):
+        for pair in range(acc.shape[0] // 2):
             tile = jnp.concatenate([acc[2 * pair, at, :], acc[2 * pair + 1, at, :]], axis=0)
             msg[s, 16 * pair : 16 * (pair + 1)] = tile.astype(BF16)
 
@@ -281,7 +301,7 @@
     return copies
 
 
-def products_held(limits, blocks, left, right, extra, msg, acc):
+def products_held(limits, blocks, left, right, extra, acc):
     _, z = core_and_z()
     odd = lax.rem(z, 2)
     rows = iota((W, W), 0)
@@ -305,9 +325,6 @@
         out = jnp.dot(lhs, jnp.concatenate(rhs[m], axis=0), preferred_element_type=F32)
         size = limits[pl.ds(2 * i, 1), 0:1], limits[pl.ds(2 * i + 1, 1), 0:1]
         acc[m] = jnp.where((rows < size[0]) & (cols < size[1]), out * SCALE, 0.0)
-    for s in range(GRP):
-        at = slice(SLAB * s, SLAB * (s + 1))
-        msg[s, :16] = jnp.concatenate([acc[0, at, :], acc[1, at, :]], axis=0).astype(BF16)
 
 
 def put_coefs(out, values):
@@ -325,13 +342,22 @@
 def ham0_kernel(limits, theta, got, left, right, above, below, msg, blk, near, acc, sems):
     copies = start_copies(above, below, near, sems)
     assemble_pieces(got, theta, limits, blk)
-    products(limits, blk, left, right, msg, acc)
+    products(limits, blk, left, right, acc)
+    uu = total(row_sum(sum(blk[3 * i + 1] * blk[3 * i + 1] for i in range(SEC))))
+    up = total(row_sum(sum(blk[3 * i + 1] * acc[i] for i in range(SEC))))
+    shift = jnp.where(uu > 0.0, up / jnp.where(uu > 0.0, uu, 1.0), 0.0)
+    for i in range(SEC):
+        acc[i] = acc[i] - shift * blk[3 * i + 1]
+    pack(acc, msg)
+    tile = split_again([jnp.broadcast_to(shift, (1, W))])
+    for s in range(GRP):
+        msg[s, SEC * SLAB :] = tile
     for copy in copies:
         copy.wait()
 
 
 def ham1_kernel(
-    limits, got, left, right, near, blk0, slab0, image0, msg, blk, v0, v1, coefs, acc
+    limits, got, left, right, near, blk0, slab0, rest0, shift0, msg, blk, v0, v1, coefs, acc
 ):
     first = NEAR * lax.rem(core_and_z()[1], 2)
     uu, uw, ww, _ = half_totals(summed_tile(got, NEAR * SLAB))
@@ -342,48 +368,56 @@
     rr = (ww - 2.0 * a0 * uw + a0 * a0 * uu) / n2
     b1 = jnp.sqrt(jnp.maximum(rr, 0.0) / COUNT + EPS)
     wc = inv / b1
-    vc = a0 * wc
+    shifts = got[0, NEAR * SLAB :].astype(F32)[6:7]
     for n in range(NEAR):
+        vc = (a0 - shifts[:, 16 * n : 16 * n + 1]) * wc
         blk[n] = blk[n] * wc - blk0[first + n] * vc
     v0[...] = slab0[...] * inv
-    v1[...] = image0[...] * wc - slab0[...] * vc
+    half = SEC * SLAB
+    for c in range(2):
+        at = slice(half * c, half * (c + 1))
+        v1[at] = rest0[at] * wc - slab0[at] * ((a0 - coef(shift0, c)) * wc)
     put_coefs(coefs, (a0, b1, inv))
-    products_held(limits, blk, left, right, near, msg, acc)
+    products_held(limits, blk, left, right, near, acc)
+    for m in range(HELD):
+        acc[m] = acc[m] - (0.25 * a0) * blk[3 * m + 1] - (0.25 * b1 * inv) * blk0[first + 3 * m + 1]
+    pack(acc, msg)
 
 
 def ham2_kernel(
-    limits, got, left, right, near, blk1, blk0, slab1, rest1, old, msg, v2, coefs, blk, acc
+    limits, got, left, right, near, blk1, slab1, rest1, old, msg, v2, coefs, blk, acc
 ):
-    first = NEAR * lax.rem(core_and_z()[1], 2)
     vw, vr, rr, vv = half_totals(summed_tile(got, NEAR * SLAB))
     assemble(got, blk)
-    a0, b1, inv = coef(old, 0), coef(old, 1), coef(old, 2)
+    a0, b1 = coef(old, 0), coef(old, 1)
     a1 = vw / COUNT
     d = a1 - a0
     rest = rr - 2.0 * d * vr + d * d * vv
     b2 = jnp.sqrt(jnp.maximum(rest, 0.0) / COUNT + EPS)
     wc = 1.0 / b2
-    vc = a1 * wc
-    pc = b1 * inv * wc
     for n in range(NEAR):
-        blk[n] = blk[n] * wc - blk1[n] * vc - blk0[first + n] * pc
+        blk[n] = blk[n] * wc - blk1[n] * (d * wc)
     v2[...] = (rest1[...] - d * slab1[...]) * wc
     put_coefs(coefs, (a0, a1, b1, b2))
-    products_held(limits, blk, left, right, near, msg, acc)
+    products_held(limits, blk, left, right, near, acc)
     dots = row_sum(sum(blk[3 * m + 1] * acc[m] for m in range(HELD)))
+    for m in range(HELD):
+        acc[m] = acc[m] - (0.25 * a1) * blk[3 * m + 1] - (0.25 * b2) * blk1[3 * m + 1]
+    pack(acc, msg)
     tile = split_rows([dots])
     for s in range(GRP):
         msg[s, 16:] = tile
 
 
 def reduced(got):
-    parts = []
+    data = SEC * SLAB
+    out = []
     for c in range(2):
         acc = got[c * NZ].astype(F32)
         for z in range(1, NZ):
             acc = acc + got[c * NZ + z].astype(F32)
-        parts.append(acc)
-    return jnp.concatenate(parts, axis=0)
+        out.append((acc[:data], row_sum(acc[data : data + 3])))
+    return out
 
 
 def reduced_halves(got):
@@ -397,24 +431,35 @@
     return jnp.concatenate(parts, axis=0)
 
 
-def spread(msg, image, rows):
-    msg_rows = 2 * SEC * SLAB
+def spread(msg, image, rows, extra=None):
+    data = 2 * SEC * SLAB
     rounded = image.astype(BF16)
     tile = split_rows(rows)
+    if extra is not None:
+        tile = jnp.where(iota((8, W), 0) == 6, extra, tile.astype(F32)).astype(BF16)
     for n in range(CHIPS):
-        msg[n, :msg_rows] = rounded
-        msg[n, msg_rows:] = tile
-
-
-def reduce0_kernel(got, keep, came, msg, image0, slab0):
+        msg[n, :data] = rounded
+        msg[n, data:] = tile
+
+
+def reduce0_kernel(got, keep, came, msg, rest0, slab0, shift0):
     c, _ = core_and_z()
-    image = reduced(got)
-    image0[...] = image
     half = SEC * SLAB
     slab0[:half] = jnp.where(c == 0, keep[...], came[...])
     slab0[half:] = jnp.where(c == 0, came[...], keep[...])
+    image = []
+    shifts = []
+    for k, (acc, shift) in enumerate(reduced(got)):
+        at = slice(half * k, half * (k + 1))
+        sent = shift.astype(BF16).astype(F32)
+        rest0[at] = acc + (shift - sent) * slab0[at]
+        image.append(acc + shift * slab0[at])
+        shifts.append(sent)
+    put_coefs(shift0, [row[:, 0:1] for row in shifts])
     vec = slab0[...]
-    spread(msg, image, [row_sum(vec * vec), row_sum(vec * image), row_sum(image * image)])
+    image = jnp.concatenate(image, axis=0)
+    rows = [row_sum(vec * vec), row_sum(vec * image), row_sum(image * image)]
+    spread(msg, rest0[...], rows, jnp.where(iota((1, W), 1) < W // 2, shifts[0], shifts[1]))
 
 
 def inner_rows(vec, image, rest):
@@ -422,19 +467,18 @@
 
 
 def reduce1_kernel(got, v1, v0, coefs, msg, rest1):
-    image = reduced_halves(got)
+    rest = reduced_halves(got)
     vec = v1[...]
-    rest = image - coef(coefs, 1) * v0[...] - coef(coefs, 0) * vec
+    image = rest + coef(coefs, 1) * v0[...] + coef(coefs, 0) * vec
     rest1[...] = rest
-    spread(msg, image, inner_rows(vec, image, rest))
-
-
-def reduce2_kernel(got, v2, v1, coefs, msg, rest2):
-    image = reduced_halves(got)
+    spread(msg, rest, inner_rows(vec, image, rest))
+
+
+def reduce2_kernel(got, v2, msg, rest2):
+    rest = reduced_halves(got)
     vec = v2[...]
-    rest = image - coef(coefs, 3) * v1[...] - coef(coefs, 1) * vec
     rest2[...] = rest
-    rows = [summed_tile(got, 16)[0]] + inner_rows(vec, image, rest)[1:]
+    rows = [summed_tile(got, 16)[0], row_sum(vec * rest), row_sum(rest * rest), row_sum(vec * vec)]
     at = iota((8, W), 0)
     tile = jnp.zeros((8, W), F32)
     for k, row in enumerate(rows):
@@ -494,14 +538,15 @@
     return lax.all_to_all(x, "sector", 0, 0, axis_index_groups=XY_GROUPS)
 
 
-def select(got, ones):
-    return call(select_kernel, [((GRP, NEAR * SLAB + 8, W), BF16)], [VMEM, VMEM])(got, ones)[0]
+def select(shifted, got, ones):
+    return call(
+        functools.partial(select_kernel, shifted), [((GRP, NEAR * SLAB + 8, W), BF16)], [VMEM, VMEM])(got, ones)[0]
 
 
 def per_device(theta, left, right, perm, dims):
     half = (SEC * SLAB, W)
     slab = (2 * SEC * SLAB, W)
-    scatter = ((GRP, SEC * SLAB, W), BF16)
+    scatter = ((GRP, SEC * SLAB + 8, W), BF16)
     plane = ((CHIPS, 2 * SEC * SLAB + 8, W), BF16)
     blocks = ((NBLK, W, W), F32)
     acc = [pltpu.VMEM((SEC, W, W), F32)]
@@ -551,36 +596,38 @@
         nbytes,
         limit=20,
     )(limits, theta, got, left, right, above, below)
-    msg, image0, slab0 = call(reduce0_kernel, [plane, (slab, F32), (slab, F32)], [VMEM] * 3)(
+    msg, rest0, slab0, shift0 = call(
+        reduce0_kernel, [plane, (slab, F32), (slab, F32), coefs], [VMEM] * 3
+    )(
         over_cz(msg), keep, came
     )
 
     held = ((NEAR, W, W), F32)
     acc = [pltpu.VMEM((HELD, W, W), F32)]
-    got = over_cz(select(over_xy(msg), ones))
+    got = over_cz(select(True, over_xy(msg), ones))
     msg, blk1, v0, v1, co = call(
         ham1_kernel,
         [((GRP, 16, W), BF16), held, (slab, F32), (slab, F32), coefs],
-        [VMEM] * 8,
+        [VMEM] * 9,
         acc,
         flops,
         nbytes,
         limit=20,
-    )(limits, got, left, right, near, blk0, slab0, image0)
+    )(limits, got, left, right, near, blk0, slab0, rest0, shift0)
     msg, rest1 = call(reduce1_kernel, [plane, (slab, F32)], [VMEM] * 4)(over_cz(msg), v1, v0, co)
 
-    got = over_cz(select(over_xy(msg), ones))
+    got = over_cz(select(False, over_xy(msg), ones))
     msg, v2, co = call(
         ham2_kernel,
         [((GRP, 24, W), BF16), (slab, F32), coefs],
-        [VMEM] * 10,
+        [VMEM] * 9,
         [pltpu.VMEM((NEAR, W, W), F32)] + acc,
         flops,
         nbytes,
         limit=20,
-    )(limits, got, left, right, near, blk1, blk0, v1, rest1, co)
-    msg, rest2 = call(reduce2_kernel, [((CHIPS, 8, W), F32), (slab, F32)], [VMEM] * 4)(
-        over_cz(msg), v2, v1, co
+    )(limits, got, left, right, near, blk1, v1, rest1, co)
+    msg, rest2 = call(reduce2_kernel, [((CHIPS, 8, W), F32), (slab, F32)], [VMEM] * 2)(
+        over_cz(msg), v2
     )
 
     msg, last = call(residual_kernel, [((GRP, SEC * SLAB + 8, W), BF16), coefs], [VMEM] * 4)(

time: 156 us -> 157 us (level)
  no operation moved by 1% of the time
where the time goes in v6:
time: 157 us
  blocking collectives  122 us (78%)
  starting transfers between devices  15 us (10%)
  Pallas kernels  12.3 us (8%)
  waiting for transfers between devices  7.03 us (4%)
    all_to_all x6, blocking collectives, over_cz(): return lax.all_to_all(x, BOTH, 0, 0, axis_index_groups=CZ_GROUPS)  77.9 us
    all_to_all x3, blocking collectives, over_xy(): return lax.all_to_all(x, 'sector', 0, 0, axis_index_groups=XY_GROUPS)  31 us
    all_to_all x1, blocking collectives, per_device(): got = lax.all_to_all(msg, 'sector', 0, 0)  12.7 us
    all_to_all x1, starting transfers between devices, per_device(): got = lax.all_to_all(msg, 'sector', 0, 0)  8.17 us
    ppermute x1, starting transfers between devices, per_device(): above = lax.ppermute(down, 'op', DOWN)  6.48 us
    all_to_all x1, waiting for transfers between devices, per_device(): got = lax.all_to_all(msg, 'sector', 0, 0)  6.22 us
    pallas_call x1, Pallas kernels, per_device(): call(start_kernel, [((pieces, 16, W), BF16), (half, F32), (half, F32), ((...  3.44 us
  transfers between devices with their start and end apart: 4, of which 2 were waited for; matrix products, arithmetic and copies ran while one was open for 0% of the time, Pallas kernels for 0%

profile of v6, /device:TPU:1, one launch (start us, length us, event | category | flops | bytes accessed | tf_op | source)
XLA Modules:
  0.0 156.6 jit_solution(4288226321199936364)
XLA Ops:
  0.6 0.0 copy-start.5
  0.6 0.0 copy-start
  0.7 3.4 %shard_map.76 = (bf16[32,16,128]{2,1,0:T(8,128)(2,1)}, f32[32,128]{1,0:T(8,128)}, f32[32,128]{1,0:T(8,128)}, s32[8,128]{1,0:T(8,128)}, bf16[2,16,128,128]{3,2,1,...) custom-call(f32[4,128,128]{2,1,0:T(8,128)} %theta.3, s32[2,4]{1,0:T(2,128)} %bitcast.3, bf16[4,16,128,128]{3,2,1,0:T(8,128)(2,1)} %left.7, ...), custom_call_target="tpu_custom_call" | custom-call | bytes 262144 | tf_op jit(solution)/shard_map/pallas_call | solution.py:564
  4.1 6.5 %collective-permute-start.1 = (bf16[2,16,128,128]{3,2,1,0:T(8,128)(2,1)}, bf16[2,16,128,128]{3,2,1,0:T(8,128)(2,1)}, u32[]{:S(2)}, u32[]{:S(2)}) collective-permute-start(bf16[2,16,128,128]{3,2,1,0:T(8,128)(2,1)} %get-tuple-element.33), channel_id=1, source_target_pairs={{0,7},{1,0},{2,1},{3,2},{4,3},{5,4},{6,5},{7,6},{8,15},{9,8},{10,9... | collective-permute-start | bytes 3145736 | tf_op jit(solution)/shard_map/ppermute | solution.py:578
  10.6 0.0 collective-permute-start.2
  10.6 0.0 copy-start.2
  10.6 0.0 copy-start.3
  10.6 8.2 %all-to-all-start = ((bf16[32,16,128]{2,1,0:T(8,128)(2,1)}), bf16[32,16,128]{2,1,0:T(8,128)(2,1)S(1)}, u32[]{:S(2)}, u32[]{:S(2)}) async-start(bf16[32,16,128]{2,1,0:T(8,128)(2,1)} %get-tuple-element.31), calls=%async_computation | async-start | bytes 262144 | tf_op jit(solution)/shard_map/all_to_all | solution.py:580
  18.8 0.3 collective-permute-start
  19.1 0.0 copy-done.5
  19.1 0.3 shard_map.77.ones
  19.4 0.8 collective-permute-done.came
  20.2 6.2 %all-to-all-done.got = bf16[32,16,128]{2,1,0:T(8,128)(2,1)S(1)} async-done(((bf16[32,16,128]{2,1,0:T(8,128)(2,1)}), bf16[32,16,128]{2,1,0:T(8,128)(2,1)S(1)}, u32[]{:S(2)}, u32[]{:S(2)}) %all-to-all-start) | async-done | bytes 131104 | tf_op jit(solution)/shard_map/all_to_all | solution.py:580
  26.5 0.0 copy-done
  26.5 0.0 copy-start.1
  26.5 0.2 shard_map.78
  26.7 12.7 %all_to_all.55.got = bf16[32,32,128]{2,1,0:T(8,128)(2,1)S(1)} all-to-all(bf16[32,32,128]{2,1,0:T(8,128)(2,1)S(1)} %shard_map.78), channel_id=1, replica_groups=mesh['sector'=32,'op'=8] {'sector'}, dimensions={0} | all-to-all | bytes 524288 | tf_op jit(solution)/shard_map/all_to_all | solution.py:589
  39.4 0.0 collective-permute-done.1.above
  39.4 0.0 collective-permute-done.2.below
  39.4 0.0 copy-done.2
  39.4 0.0 copy-done.3
  39.4 0.0 copy-done.1
  39.4 0.0 copy-start.4
  39.5 2.9 %shard_map.79 = (bf16[16,40,128]{2,1,0:T(8,128)(2,1)S(1)}, f32[12,128,128]{2,1,0:T(8,128)S(1)}, bf16[2,2,16,128,128]{4,3,2,1,0:T(8,128)(2,1)S(1)}) custom-call(s32[8,128]{1,0:T(8,128)S(1)} %copy-done.3, f32[4,128,128]{2,1,0:T(8,128)S(1)} %copy-done.2, bf16[32,32,128]{2,1,0:T(8,128)(2,1)S(1)} %all_to_all.55.got, bf16[4,16,128,128]{3,2,1,0:T(8,128)(2,1)S(1)} %copy-done.1, ...), custom_call_target="tpu_custom_call" | custom-call | flops 536870912 | bytes 6291456 | tf_op jit(solution)/shard_map/pallas_call | solution.py:590
  42.3 12.5 %all_to_all.56.got = bf16[16,40,128]{2,1,0:T(8,128)(2,1)S(1)} all-to-all(bf16[16,40,128]{2,1,0:T(8,128)(2,1)S(1)} %get-tuple-element.35), channel_id=1, replica_groups={{0,1,2,3,4,5,6,7,8,9,10,11,12,13,14,15},{16,17,18,19,20,21,22,23,24,25,..., dimensions={0} | all-to-all | bytes 327680 | tf_op jit(solution)/shard_map/all_to_all | solution.py:534
  54.8 0.0 copy-done.4
  54.8 0.1 shard_map.80
  54.9 10.6 %all_to_all.57.got = bf16[16,72,128]{2,1,0:T(8,128)(2,1)S(1)} all-to-all(bf16[16,72,128]{2,1,0:T(8,128)(2,1)S(1)} %get-tuple-element.37), channel_id=1, replica_groups={{0,16,32,48,64,80,96,112,128,144,160,176,192,208,224,240},{8,24,40,56,7..., dimensions={0} | all-to-all | bytes 589824 | tf_op jit(solution)/shard_map/all_to_all | solution.py:538
  65.5 0.4 shard_map.81
  65.9 15.0 %all_to_all.58.got = bf16[16,56,128]{2,1,0:T(8,128)(2,1)S(1)} all-to-all(bf16[16,56,128]{2,1,0:T(8,128)(2,1)S(1)} %shard_map.81), channel_id=1, replica_groups={{0,1,2,3,4,5,6,7,8,9,10,11,12,13,14,15},{16,17,18,19,20,21,22,23,24,25,..., dimensions={0} | all-to-all | bytes 458752 | tf_op jit(solution)/shard_map/all_to_all | solution.py:534
  80.9 1.6 %shard_map.82 = (bf16[16,16,128]{2,1,0:T(8,128)(2,1)S(1)}, f32[6,128,128]{2,1,0:T(8,128)S(1)}, f32[64,128]{1,0:T(8,128)S(1)}, f32[64,128]{1,0:T(8,128)S(1)}, f32[8,128]{1,0:T(8,128)S(1)}) custom-call(s32[8,128]{1,0:T(8,128)S(1)} %copy-done.3, bf16[16,56,128]{2,1,0:T(8,128)(2,1)S(1)} %all_to_all.58.got, bf16[4,16,128,128]{3,2,1,0:T(8,128)(2,1)S(1)} %copy-done.1, ...), custom_call_target="tpu_custom_call" | custom-call | flops 536870912 | bytes 6291456 | tf_op jit(solution)/shard_map/pallas_call | solution.py:608
  82.5 11.8 %all_to_all.59.got = bf16[16,16,128]{2,1,0:T(8,128)(2,1)S(1)} all-to-all(bf16[16,16,128]{2,1,0:T(8,128)(2,1)S(1)} %get-tuple-element.43), channel_id=1, replica_groups={{0,1,2,3,4,5,6,7,8,9,10,11,12,13,14,15},{16,17,18,19,20,21,22,23,24,25,..., dimensions={0} | all-to-all | bytes 131072 | tf_op jit(solution)/shard_map/all_to_all | solution.py:534
  94.2 0.1 shard_map.83
  94.4 10.7 %all_to_all.60.got = bf16[16,72,128]{2,1,0:T(8,128)(2,1)S(1)} all-to-all(bf16[16,72,128]{2,1,0:T(8,128)(2,1)S(1)} %get-tuple-element.47), channel_id=1, replica_groups={{0,16,32,48,64,80,96,112,128,144,160,176,192,208,224,240},{8,24,40,56,7..., dimensions={0} | all-to-all | bytes 589824 | tf_op jit(solution)/shard_map/all_to_all | solution.py:538
  105.1 0.2 shard_map.84
  105.3 13.9 %all_to_all.61.got = bf16[16,56,128]{2,1,0:T(8,128)(2,1)S(1)} all-to-all(bf16[16,56,128]{2,1,0:T(8,128)(2,1)S(1)} %shard_map.84), channel_id=1, replica_groups={{0,1,2,3,4,5,6,7,8,9,10,11,12,13,14,15},{16,17,18,19,20,21,22,23,24,25,..., dimensions={0} | all-to-all | bytes 458752 | tf_op jit(solution)/shard_map/all_to_all | solution.py:534
  119.2 1.6 %shard_map.85 = (bf16[16,24,128]{2,1,0:T(8,128)(2,1)S(1)}, f32[64,128]{1,0:T(8,128)S(1)}, f32[8,128]{1,0:T(8,128)S(1)}) custom-call(s32[8,128]{1,0:T(8,128)S(1)} %copy-done.3, bf16[16,56,128]{2,1,0:T(8,128)(2,1)S(1)} %all_to_all.61.got, bf16[4,16,128,128]{3,2,1,0:T(8,128)(2,1)S(1)} %copy-done.1, bf16[4,16,128,128]{3,2,1,0:T(8,128)(2,1)S(1)} %copy-done, ...), custom_call_target="tpu_custom_call" | custom-call | flops 536870912 | bytes 6291456 | tf_op jit(solution)/shard_map/pallas_call | solution.py:620
  120.8 12.0 %all_to_all.62.got = bf16[16,24,128]{2,1,0:T(8,128)(2,1)S(1)} all-to-all(bf16[16,24,128]{2,1,0:T(8,128)(2,1)S(1)} %get-tuple-element.50), channel_id=1, replica_groups={{0,1,2,3,4,5,6,7,8,9,10,11,12,13,14,15},{16,17,18,19,20,21,22,23,24,25,..., dimensions={0} | all-to-all | bytes 196608 | tf_op jit(solution)/shard_map/all_to_all | solution.py:534
  132.8 9.7 %all_to_all.63.got = f32[16,8,128]{2,1,0:T(8,128)S(1)} all-to-all(f32[16,8,128]{2,1,0:T(8,128)S(1)} %get-tuple-element.52), channel_id=1, replica_groups={{0,16,32,48,64,80,96,112,128,144,160,176,192,208,224,240},{8,24,40,56,7..., dimensions={0} | all-to-all | bytes 131072 | tf_op jit(solution)/shard_map/all_to_all | solution.py:538
  142.5 0.1 shard_map.87
  142.6 12.8 %all_to_all.64.got = bf16[16,40,128]{2,1,0:T(8,128)(2,1)S(1)} all-to-all(bf16[16,40,128]{2,1,0:T(8,128)(2,1)S(1)} %get-tuple-element.55), channel_id=1, replica_groups={{0,1,2,3,4,5,6,7,8,9,10,11,12,13,14,15},{16,17,18,19,20,21,22,23,24,25,..., dimensions={0} | all-to-all | bytes 327680 | tf_op jit(solution)/shard_map/all_to_all | solution.py:534
  155.4 1.2 shard_map.88
  (1 shorter events, 0.0 us)
Async XLA Ops:
  0.6 18.5 %copy-start.5 = (s32[128]{0:T(128)S(1)}, s32[128]{0:T(128)}, u32[]{:S(2)}) copy-start(s32[128]{0:T(128)} %param.8) | copy-start | bytes 1540
  0.6 25.8 %copy-start = (bf16[4,16,128,128]{3,2,1,0:T(8,128)(2,1)S(1)}, bf16[4,16,128,128]{3,2,1,0:T(8,128)(2,1)}, u32[]{:S(2)}) copy-start(bf16[4,16,128,128]{3,2,1,0:T(8,128)(2,1)} %right.7) | copy-start | bytes 6291460
  4.1 35.3 %collective-permute-start.1 = (bf16[2,16,128,128]{3,2,1,0:T(8,128)(2,1)}, bf16[2,16,128,128]{3,2,1,0:T(8,128)(2,1)}, u32[]{:S(2)}, u32[]{:S(2)}) collective-permute-start(bf16[2,16,128,128]{3,2,1,0:T(8,128)(2,1)} %get-tuple-element.33), channel_id=1, source_target_pairs={{0,7},{1,0},{2,1},{3,2},{4,3},{5,4},{6,5},{7,6},{8,15},{9,8},{10,9... | collective-permute-start | bytes 3145736 | tf_op jit(solution)/shard_map/ppermute | solution.py:578
  10.6 28.8 %collective-permute-start.2 = (bf16[2,16,128,128]{3,2,1,0:T(8,128)(2,1)}, bf16[2,16,128,128]{3,2,1,0:T(8,128)(2,1)}, u32[]{:S(2)}, u32[]{:S(2)}) collective-permute-start(bf16[2,16,128,128]{3,2,1,0:T(8,128)(2,1)} %get-tuple-element.34), channel_id=1, source_target_pairs={{0,1},{1,2},{2,3},{3,4},{4,5},{5,6},{6,7},{7,0},{8,9},{9,10},{10,1... | collective-permute-start | bytes 3145736 | tf_op jit(solution)/shard_map/ppermute | solution.py:579
  10.6 28.8 %copy-start.2 = (f32[4,128,128]{2,1,0:T(8,128)S(1)}, f32[4,128,128]{2,1,0:T(8,128)}, u32[]{:S(2)}) copy-start(f32[4,128,128]{2,1,0:T(8,128)} %theta.3) | copy-start | bytes 786436
  10.6 28.8 %copy-start.3 = (s32[8,128]{1,0:T(8,128)S(1)}, s32[8,128]{1,0:T(8,128)}, u32[]{:S(2)}) copy-start(s32[8,128]{1,0:T(8,128)} %get-tuple-element.30.limits) | copy-start | bytes 12292
  10.6 15.9 %all-to-all-start = ((bf16[32,16,128]{2,1,0:T(8,128)(2,1)}), bf16[32,16,128]{2,1,0:T(8,128)(2,1)S(1)}, u32[]{:S(2)}, u32[]{:S(2)}) async-start(bf16[32,16,128]{2,1,0:T(8,128)(2,1)} %get-tuple-element.31), calls=%async_computation | async-start | bytes 262144 | tf_op jit(solution)/shard_map/all_to_all | solution.py:580
  18.8 1.5 collective-permute-start
  26.5 13.0 %copy-start.1 = (bf16[4,16,128,128]{3,2,1,0:T(8,128)(2,1)S(1)}, bf16[4,16,128,128]{3,2,1,0:T(8,128)(2,1)}, u32[]{:S(2)}) copy-start(bf16[4,16,128,128]{3,2,1,0:T(8,128)(2,1)} %left.7) | copy-start | bytes 6291460
  39.4 15.3 %copy-start.4 = (f32[32,128]{1,0:T(8,128)S(1)}, f32[32,128]{1,0:T(8,128)}, u32[]{:S(2)}) copy-start(f32[32,128]{1,0:T(8,128)} %get-tuple-element.36.keep) | copy-start | bytes 49156

commit v7 on v6

--- a/solution.py
+++ b/solution.py
@@ -283,11 +283,11 @@
         acc[i] = jnp.where(inside, out * SCALE, 0.0)
 
 
-def pack(acc, msg):
+def pack(count, rows, msg):
     for s in range(GRP):
         at = slice(SLAB * s, SLAB * (s + 1))
-        for pair in range(acc.shape[0] // 2):
-            tile = jnp.concatenate([acc[2 * pair, at, :], acc[2 * pair + 1, at, :]], axis=0)
+        for pair in range(count // 2):
+            tile = jnp.concatenate([rows(2 * pair, at), rows(2 * pair + 1, at)], axis=0)
             msg[s, 16 * pair : 16 * (pair + 1)] = tile.astype(BF16)
 
 
@@ -346,9 +346,7 @@
     uu = total(row_sum(sum(blk[3 * i + 1] * blk[3 * i + 1] for i in range(SEC))))
     up = total(row_sum(sum(blk[3 * i + 1] * acc[i] for i in range(SEC))))
     shift = jnp.where(uu > 0.0, up / jnp.where(uu > 0.0, uu, 1.0), 0.0)
-    for i in range(SEC):
-        acc[i] = acc[i] - shift * blk[3 * i + 1]
-    pack(acc, msg)
+    pack(SEC, lambda i, at: acc[i, at, :] - shift * blk[3 * i + 1, at, :], msg)
     tile = split_again([jnp.broadcast_to(shift, (1, W))])
     for s in range(GRP):
         msg[s, SEC * SLAB :] = tile
@@ -379,9 +377,14 @@
         v1[at] = rest0[at] * wc - slab0[at] * ((a0 - coef(shift0, c)) * wc)
     put_coefs(coefs, (a0, b1, inv))
     products_held(limits, blk, left, right, near, acc)
-    for m in range(HELD):
-        acc[m] = acc[m] - (0.25 * a0) * blk[3 * m + 1] - (0.25 * b1 * inv) * blk0[first + 3 * m + 1]
-    pack(acc, msg)
+    share, before = 0.25 * a0, 0.25 * b1 * inv
+    pack(
+        HELD,
+        lambda m, at: acc[m, at, :]
+        - share * blk[3 * m + 1, at, :]
+        - before * blk0[first + 3 * m + 1, at, :],
+        msg,
+    )
 
 
 def ham2_kernel(
@@ -401,9 +404,12 @@
     put_coefs(coefs, (a0, a1, b1, b2))
     products_held(limits, blk, left, right, near, acc)
     dots = row_sum(sum(blk[3 * m + 1] * acc[m] for m in range(HELD)))
-    for m in range(HELD):
-        acc[m] = acc[m] - (0.25 * a1) * blk[3 * m + 1] - (0.25 * b2) * blk1[3 * m + 1]
-    pack(acc, msg)
+    share, before = 0.25 * a1, 0.25 * b2
+    pack(
+        HELD,
+        lambda m, at: acc[m, at, :] - share * blk[3 * m + 1, at, :] - before * blk1[3 * m + 1, at, :],
+        msg,
+    )
     tile = split_rows([dots])
     for s in range(GRP):
         msg[s, 16:] = tile
@@ -503,7 +509,8 @@
             msg[c * NZ + z, half:] = tile
 
 
-def finish_kernel(got, coefs, last, vec_out, coef_out, dens_out, rest):
+def finish_kernel(got, coefs, last, vec_out, coef_out, dens_out, rest, dens, sems):
+    copies = []
     vr, rr, vv, _ = half_totals(summed_tile(got, SEC * SLAB))
     a0, a1, b1, b2 = [coef(coefs, k) for k in range(4)]
     a2, d = coef(last, 0), coef(last, 1)
@@ -519,15 +526,21 @@
                 rest[2 * pair + k, SLAB * s : SLAB * (s + 1), :] = tile[SLAB * k : SLAB * (k + 1)]
     for i in range(SEC):
         v = rest[i] * wc
-        vec_out[i] = v
+        rest[i] = v
+        copies.append(pltpu.make_async_copy(rest.at[i], vec_out.at[i], sems.at[i]))
+        copies[-1].start()
         high = v.astype(BF16)
         low = (v - high.astype(F32)).astype(BF16)
-        dens_out[i] = lax.dot_general(
+        dens[i] = lax.dot_general(
             jnp.concatenate([high, high, low], axis=1),
             jnp.concatenate([high, low, high], axis=1),
             (((1,), (1,)), ((), ())),
             preferred_element_type=F32,
         ) * (1.0 / W)
+        copies.append(pltpu.make_async_copy(dens.at[i], dens_out.at[i], sems.at[SEC + i]))
+        copies[-1].start()
+    for copy in copies:
+        copy.wait()
 
 
 def over_cz(x):
@@ -637,8 +650,8 @@
         finish_kernel,
         [((SEC, W, W), F32), ((6,), F32), ((SEC, W, W), F32)],
         [VMEM] * 3,
-        [pltpu.VMEM((SEC, W, W), F32)],
-        out_specs=[VMEM, SMEM, VMEM],
+        [pltpu.VMEM((SEC, W, W), F32)] * 2 + [pltpu.SemaphoreType.DMA((2 * SEC,))],
+        out_specs=[any_space, SMEM, any_space],
     )(over_cz(msg), co, last)
 
 

time: 157 us -> 158 us (level)
  no operation moved by 1% of the time
where the time goes in v7:
time: 158 us; the launch traced here: 157 us
  blocking collectives  122 us (77%)
  starting transfers between devices  15 us (9%)
  Pallas kernels  12.8 us (8%)
  waiting for transfers between devices  7.03 us (4%)
    all_to_all x6, blocking collectives, over_cz(): return lax.all_to_all(x, BOTH, 0, 0, axis_index_groups=CZ_GROUPS)  77.8 us
    all_to_all x3, blocking collectives, over_xy(): return lax.all_to_all(x, 'sector', 0, 0, axis_index_groups=XY_GROUPS)  31 us
    all_to_all x1, blocking collectives, per_device(): got = lax.all_to_all(msg, 'sector', 0, 0)  12.7 us
    all_to_all x1, starting transfers between devices, per_device(): got = lax.all_to_all(msg, 'sector', 0, 0)  8.17 us
    ppermute x1, starting transfers between devices, per_device(): above = lax.ppermute(down, 'op', DOWN)  6.48 us
    all_to_all x1, waiting for transfers between devices, per_device(): got = lax.all_to_all(msg, 'sector', 0, 0)  6.22 us
    pallas_call x1, Pallas kernels, per_device(): call(start_kernel, [((pieces, 16, W), BF16), (half, F32), (half, F32), ((...  3.44 us
  transfers between devices with their start and end apart: 4, of which 2 were waited for; matrix products, arithmetic and copies ran while one was open for 0% of the time, Pallas kernels for 0%

profile of v7, /device:TPU:1, one launch (start us, length us, event | category | flops | bytes accessed | tf_op | source)
XLA Modules:
  0.0 157.2 jit_solution(16917188110338954551)
XLA Ops:
  0.6 0.0 copy-start.5
  0.6 0.0 copy-start
  0.7 3.4 %shard_map.76 = (bf16[32,16,128]{2,1,0:T(8,128)(2,1)}, f32[32,128]{1,0:T(8,128)}, f32[32,128]{1,0:T(8,128)}, s32[8,128]{1,0:T(8,128)}, bf16[2,16,128,128]{3,2,1,...) custom-call(f32[4,128,128]{2,1,0:T(8,128)} %theta.3, s32[2,4]{1,0:T(2,128)} %bitcast.3, bf16[4,16,128,128]{3,2,1,0:T(8,128)(2,1)} %left.7, ...), custom_call_target="tpu_custom_call" | custom-call | bytes 262144 | tf_op jit(solution)/shard_map/pallas_call | solution.py:577
  4.1 6.5 %collective-permute-start.1 = (bf16[2,16,128,128]{3,2,1,0:T(8,128)(2,1)}, bf16[2,16,128,128]{3,2,1,0:T(8,128)(2,1)}, u32[]{:S(2)}, u32[]{:S(2)}) collective-permute-start(bf16[2,16,128,128]{3,2,1,0:T(8,128)(2,1)} %get-tuple-element.33), channel_id=1, source_target_pairs={{0,7},{1,0},{2,1},{3,2},{4,3},{5,4},{6,5},{7,6},{8,15},{9,8},{10,9... | collective-permute-start | bytes 3145736 | tf_op jit(solution)/shard_map/ppermute | solution.py:591
  10.6 0.0 collective-permute-start.2
  10.6 0.0 copy-start.2
  10.6 0.0 copy-start.3
  10.6 8.2 %all-to-all-start = ((bf16[32,16,128]{2,1,0:T(8,128)(2,1)}), bf16[32,16,128]{2,1,0:T(8,128)(2,1)S(1)}, u32[]{:S(2)}, u32[]{:S(2)}) async-start(bf16[32,16,128]{2,1,0:T(8,128)(2,1)} %get-tuple-element.31), calls=%async_computation | async-start | bytes 262144 | tf_op jit(solution)/shard_map/all_to_all | solution.py:593
  18.8 0.3 collective-permute-start
  19.1 0.0 copy-done.5
  19.1 0.3 shard_map.77.ones
  19.4 0.8 collective-permute-done.came
  20.2 6.2 %all-to-all-done.got = bf16[32,16,128]{2,1,0:T(8,128)(2,1)S(1)} async-done(((bf16[32,16,128]{2,1,0:T(8,128)(2,1)}), bf16[32,16,128]{2,1,0:T(8,128)(2,1)S(1)}, u32[]{:S(2)}, u32[]{:S(2)}) %all-to-all-start) | async-done | bytes 131104 | tf_op jit(solution)/shard_map/all_to_all | solution.py:593
  26.5 0.0 copy-done
  26.5 0.0 copy-start.1
  26.5 0.2 shard_map.78
  26.7 12.7 %all_to_all.55.got = bf16[32,32,128]{2,1,0:T(8,128)(2,1)S(1)} all-to-all(bf16[32,32,128]{2,1,0:T(8,128)(2,1)S(1)} %shard_map.78), channel_id=1, replica_groups=mesh['sector'=32,'op'=8] {'sector'}, dimensions={0} | all-to-all | bytes 524288 | tf_op jit(solution)/shard_map/all_to_all | solution.py:602
  39.4 0.0 collective-permute-done.1.above
  39.4 0.0 collective-permute-done.2.below
  39.4 0.0 copy-done.2
  39.4 0.0 copy-done.3
  39.4 0.0 copy-done.1
  39.4 0.0 copy-start.4
  39.5 2.9 %shard_map.79 = (bf16[16,40,128]{2,1,0:T(8,128)(2,1)S(1)}, f32[12,128,128]{2,1,0:T(8,128)S(1)}, bf16[2,2,16,128,128]{4,3,2,1,0:T(8,128)(2,1)S(1)}) custom-call(s32[8,128]{1,0:T(8,128)S(1)} %copy-done.3, f32[4,128,128]{2,1,0:T(8,128)S(1)} %copy-done.2, bf16[32,32,128]{2,1,0:T(8,128)(2,1)S(1)} %all_to_all.55.got, bf16[4,16,128,128]{3,2,1,0:T(8,128)(2,1)S(1)} %copy-done.1, ...), custom_call_target="tpu_custom_call" | custom-call | flops 536870912 | bytes 6291456 | tf_op jit(solution)/shard_map/pallas_call | solution.py:603
  42.3 12.5 %all_to_all.56.got = bf16[16,40,128]{2,1,0:T(8,128)(2,1)S(1)} all-to-all(bf16[16,40,128]{2,1,0:T(8,128)(2,1)S(1)} %get-tuple-element.35), channel_id=1, replica_groups={{0,1,2,3,4,5,6,7,8,9,10,11,12,13,14,15},{16,17,18,19,20,21,22,23,24,25,..., dimensions={0} | all-to-all | bytes 327680 | tf_op jit(solution)/shard_map/all_to_all | solution.py:547
  54.8 0.0 copy-done.4
  54.8 0.1 shard_map.80
  54.9 10.6 %all_to_all.57.got = bf16[16,72,128]{2,1,0:T(8,128)(2,1)S(1)} all-to-all(bf16[16,72,128]{2,1,0:T(8,128)(2,1)S(1)} %get-tuple-element.37), channel_id=1, replica_groups={{0,16,32,48,64,80,96,112,128,144,160,176,192,208,224,240},{8,24,40,56,7..., dimensions={0} | all-to-all | bytes 589824 | tf_op jit(solution)/shard_map/all_to_all | solution.py:551
  65.5 0.4 shard_map.81
  65.9 15.0 %all_to_all.58.got = bf16[16,56,128]{2,1,0:T(8,128)(2,1)S(1)} all-to-all(bf16[16,56,128]{2,1,0:T(8,128)(2,1)S(1)} %shard_map.81), channel_id=1, replica_groups={{0,1,2,3,4,5,6,7,8,9,10,11,12,13,14,15},{16,17,18,19,20,21,22,23,24,25,..., dimensions={0} | all-to-all | bytes 458752 | tf_op jit(solution)/shard_map/all_to_all | solution.py:547
  80.9 1.6 shard_map.82
  82.5 11.8 %all_to_all.59.got = bf16[16,16,128]{2,1,0:T(8,128)(2,1)S(1)} all-to-all(bf16[16,16,128]{2,1,0:T(8,128)(2,1)S(1)} %get-tuple-element.43), channel_id=1, replica_groups={{0,1,2,3,4,5,6,7,8,9,10,11,12,13,14,15},{16,17,18,19,20,21,22,23,24,25,..., dimensions={0} | all-to-all | bytes 131072 | tf_op jit(solution)/shard_map/all_to_all | solution.py:547
  94.2 0.1 shard_map.83
  94.4 10.7 %all_to_all.60.got = bf16[16,72,128]{2,1,0:T(8,128)(2,1)S(1)} all-to-all(bf16[16,72,128]{2,1,0:T(8,128)(2,1)S(1)} %get-tuple-element.47), channel_id=1, replica_groups={{0,16,32,48,64,80,96,112,128,144,160,176,192,208,224,240},{8,24,40,56,7..., dimensions={0} | all-to-all | bytes 589824 | tf_op jit(solution)/shard_map/all_to_all | solution.py:551
  105.1 0.2 shard_map.84
  105.3 13.9 %all_to_all.61.got = bf16[16,56,128]{2,1,0:T(8,128)(2,1)S(1)} all-to-all(bf16[16,56,128]{2,1,0:T(8,128)(2,1)S(1)} %shard_map.84), channel_id=1, replica_groups={{0,1,2,3,4,5,6,7,8,9,10,11,12,13,14,15},{16,17,18,19,20,21,22,23,24,25,..., dimensions={0} | all-to-all | bytes 458752 | tf_op jit(solution)/shard_map/all_to_all | solution.py:547
  119.2 1.6 %shard_map.85 = (bf16[16,24,128]{2,1,0:T(8,128)(2,1)S(1)}, f32[64,128]{1,0:T(8,128)S(1)}, f32[8,128]{1,0:T(8,128)S(1)}) custom-call(s32[8,128]{1,0:T(8,128)S(1)} %copy-done.3, bf16[16,56,128]{2,1,0:T(8,128)(2,1)S(1)} %all_to_all.61.got, bf16[4,16,128,128]{3,2,1,0:T(8,128)(2,1)S(1)} %copy-done.1, bf16[4,16,128,128]{3,2,1,0:T(8,128)(2,1)S(1)} %copy-done, ...), custom_call_target="tpu_custom_call" | custom-call | flops 536870912 | bytes 6291456 | tf_op jit(solution)/shard_map/pallas_call | solution.py:633
  120.8 12.0 %all_to_all.62.got = bf16[16,24,128]{2,1,0:T(8,128)(2,1)S(1)} all-to-all(bf16[16,24,128]{2,1,0:T(8,128)(2,1)S(1)} %get-tuple-element.50), channel_id=1, replica_groups={{0,1,2,3,4,5,6,7,8,9,10,11,12,13,14,15},{16,17,18,19,20,21,22,23,24,25,..., dimensions={0} | all-to-all | bytes 196608 | tf_op jit(solution)/shard_map/all_to_all | solution.py:547
  132.8 9.7 %all_to_all.63.got = f32[16,8,128]{2,1,0:T(8,128)S(1)} all-to-all(f32[16,8,128]{2,1,0:T(8,128)S(1)} %get-tuple-element.52), channel_id=1, replica_groups={{0,16,32,48,64,80,96,112,128,144,160,176,192,208,224,240},{8,24,40,56,7..., dimensions={0} | all-to-all | bytes 131072 | tf_op jit(solution)/shard_map/all_to_all | solution.py:551
  142.5 0.1 shard_map.87
  142.6 12.8 %all_to_all.64.got = bf16[16,40,128]{2,1,0:T(8,128)(2,1)S(1)} all-to-all(bf16[16,40,128]{2,1,0:T(8,128)(2,1)S(1)} %get-tuple-element.55), channel_id=1, replica_groups={{0,1,2,3,4,5,6,7,8,9,10,11,12,13,14,15},{16,17,18,19,20,21,22,23,24,25,..., dimensions={0} | all-to-all | bytes 327680 | tf_op jit(solution)/shard_map/all_to_all | solution.py:547
  155.4 1.7 %shard_map.88 = (f32[4,128,128]{2,1,0:T(8,128)}, f32[6]{0:T(128)}, f32[4,128,128]{2,1,0:T(8,128)}) custom-call(bf16[16,40,128]{2,1,0:T(8,128)(2,1)S(1)} %all_to_all.64.got, f32[8,128]{1,0:T(8,128)S(1)} %get-tuple-element.54.coefs, f32[8,128]{1,0:T(8,128)S(1)} %get-tuple-element.56.last), custom_call_target="tpu_custom_call" | custom-call | bytes 262144 | tf_op jit(solution)/shard_map/pallas_call | solution.py:649
  (1 shorter events, 0.0 us)
Async XLA Ops:
  0.6 18.5 %copy-start.5 = (s32[128]{0:T(128)S(1)}, s32[128]{0:T(128)}, u32[]{:S(2)}) copy-start(s32[128]{0:T(128)} %param.8) | copy-start | bytes 1540
  0.6 25.8 %copy-start = (bf16[4,16,128,128]{3,2,1,0:T(8,128)(2,1)S(1)}, bf16[4,16,128,128]{3,2,1,0:T(8,128)(2,1)}, u32[]{:S(2)}) copy-start(bf16[4,16,128,128]{3,2,1,0:T(8,128)(2,1)} %right.7) | copy-start | bytes 6291460
  4.1 35.3 %collective-permute-start.1 = (bf16[2,16,128,128]{3,2,1,0:T(8,128)(2,1)}, bf16[2,16,128,128]{3,2,1,0:T(8,128)(2,1)}, u32[]{:S(2)}, u32[]{:S(2)}) collective-permute-start(bf16[2,16,128,128]{3,2,1,0:T(8,128)(2,1)} %get-tuple-element.33), channel_id=1, source_target_pairs={{0,7},{1,0},{2,1},{3,2},{4,3},{5,4},{6,5},{7,6},{8,15},{9,8},{10,9... | collective-permute-start | bytes 3145736 | tf_op jit(solution)/shard_map/ppermute | solution.py:591
  10.6 28.8 %collective-permute-start.2 = (bf16[2,16,128,128]{3,2,1,0:T(8,128)(2,1)}, bf16[2,16,128,128]{3,2,1,0:T(8,128)(2,1)}, u32[]{:S(2)}, u32[]{:S(2)}) collective-permute-start(bf16[2,16,128,128]{3,2,1,0:T(8,128)(2,1)} %get-tuple-element.34), channel_id=1, source_target_pairs={{0,1},{1,2},{2,3},{3,4},{4,5},{5,6},{6,7},{7,0},{8,9},{9,10},{10,1... | collective-permute-start | bytes 3145736 | tf_op jit(solution)/shard_map/ppermute | solution.py:592
  10.6 28.8 %copy-start.2 = (f32[4,128,128]{2,1,0:T(8,128)S(1)}, f32[4,128,128]{2,1,0:T(8,128)}, u32[]{:S(2)}) copy-start(f32[4,128,128]{2,1,0:T(8,128)} %theta.3) | copy-start | bytes 786436
  10.6 28.8 %copy-start.3 = (s32[8,128]{1,0:T(8,128)S(1)}, s32[8,128]{1,0:T(8,128)}, u32[]{:S(2)}) copy-start(s32[8,128]{1,0:T(8,128)} %get-tuple-element.30.limits) | copy-start | bytes 12292
  10.6 15.9 %all-to-all-start = ((bf16[32,16,128]{2,1,0:T(8,128)(2,1)}), bf16[32,16,128]{2,1,0:T(8,128)(2,1)S(1)}, u32[]{:S(2)}, u32[]{:S(2)}) async-start(bf16[32,16,128]{2,1,0:T(8,128)(2,1)} %get-tuple-element.31), calls=%async_computation | async-start | bytes 262144 | tf_op jit(solution)/shard_map/all_to_all | solution.py:593
  18.8 1.5 collective-permute-start
  26.5 13.0 %copy-start.1 = (bf16[4,16,128,128]{3,2,1,0:T(8,128)(2,1)S(1)}, bf16[4,16,128,128]{3,2,1,0:T(8,128)(2,1)}, u32[]{:S(2)}) copy-start(bf16[4,16,128,128]{3,2,1,0:T(8,128)(2,1)} %left.7) | copy-start | bytes 6291460
  39.4 15.3 %copy-start.4 = (f32[32,128]{1,0:T(8,128)S(1)}, f32[32,128]{1,0:T(8,128)}, u32[]{:S(2)}) copy-start(f32[32,128]{1,0:T(8,128)} %get-tuple-element.36.keep) | copy-start | bytes 49156

commit v8 on v7

--- a/solution.py
+++ b/solution.py
@@ -263,6 +263,7 @@
 
 
 def products(limits, blocks, left, right, acc):
+    own = along = jnp.zeros((1, W), F32)
     _, z = core_and_z()
     rows = iota((W, W), 0)
     cols = iota((W, W), 1)
@@ -280,7 +281,12 @@
         rhs = jnp.concatenate([right[i, w] for w in order], axis=0)
         out = jnp.dot(lhs, rhs, preferred_element_type=F32)
         inside = (rows < coef(limits, 2 * i)) & (cols < coef(limits, 2 * i + 1))
-        acc[i] = jnp.where(inside, out * SCALE, 0.0)
+        out = jnp.where(inside, out * SCALE, 0.0)
+        acc[i] = out
+        vec = blocks[3 * i + 1]
+        own = own + row_sum(vec * vec)
+        along = along + row_sum(vec * out)
+    return total(own), total(along)
 
 
 def pack(count, rows, msg):
@@ -342,9 +348,7 @@
 def ham0_kernel(limits, theta, got, left, right, above, below, msg, blk, near, acc, sems):
     copies = start_copies(above, below, near, sems)
     assemble_pieces(got, theta, limits, blk)
-    products(limits, blk, left, right, acc)
-    uu = total(row_sum(sum(blk[3 * i + 1] * blk[3 * i + 1] for i in range(SEC))))
-    up = total(row_sum(sum(blk[3 * i + 1] * acc[i] for i in range(SEC))))
+    uu, up = products(limits, blk, left, right, acc)
     shift = jnp.where(uu > 0.0, up / jnp.where(uu > 0.0, uu, 1.0), 0.0)
     pack(SEC, lambda i, at: acc[i, at, :] - shift * blk[3 * i + 1, at, :], msg)
     tile = split_again([jnp.broadcast_to(shift, (1, W))])
@@ -509,8 +513,7 @@
             msg[c * NZ + z, half:] = tile
 
 
-def finish_kernel(got, coefs, last, vec_out, coef_out, dens_out, rest, dens, sems):
-    copies = []
+def finish_kernel(got, coefs, last, vec_out, coef_out, dens_out, rest):
     vr, rr, vv, _ = half_totals(summed_tile(got, SEC * SLAB))
     a0, a1, b1, b2 = [coef(coefs, k) for k in range(4)]
     a2, d = coef(last, 0), coef(last, 1)
@@ -526,21 +529,15 @@
                 rest[2 * pair + k, SLAB * s : SLAB * (s + 1), :] = tile[SLAB * k : SLAB * (k + 1)]
     for i in range(SEC):
         v = rest[i] * wc
-        rest[i] = v
-        copies.append(pltpu.make_async_copy(rest.at[i], vec_out.at[i], sems.at[i]))
-        copies[-1].start()
+        vec_out[i] = v
         high = v.astype(BF16)
         low = (v - high.astype(F32)).astype(BF16)
-        dens[i] = lax.dot_general(
+        dens_out[i] = lax.dot_general(
             jnp.concatenate([high, high, low], axis=1),
             jnp.concatenate([high, low, high], axis=1),
             (((1,), (1,)), ((), ())),
             preferred_element_type=F32,
         ) * (1.0 / W)
-        copies.append(pltpu.make_async_copy(dens.at[i], dens_out.at[i], sems.at[SEC + i]))
-        copies[-1].start()
-    for copy in copies:
-        copy.wait()
 
 
 def over_cz(x):
@@ -650,8 +647,8 @@
         finish_kernel,
         [((SEC, W, W), F32), ((6,), F32), ((SEC, W, W), F32)],
         [VMEM] * 3,
-        [pltpu.VMEM((SEC, W, W), F32)] * 2 + [pltpu.SemaphoreType.DMA((2 * SEC,))],
-        out_specs=[any_space, SMEM, any_space],
+        [pltpu.VMEM((SEC, W, W), F32)],
+        out_specs=[VMEM, SMEM, VMEM],
     )(over_cz(msg), co, last)
 
 

time: 158 us -> 157 us (level)
  no operation moved by 1% of the time
where the time goes in v8:
time: 157 us
  blocking collectives  122 us (78%)
  starting transfers between devices  15 us (10%)
  Pallas kernels  12.3 us (8%)
  waiting for transfers between devices  7.03 us (4%)
    all_to_all x6, blocking collectives, over_cz(): return lax.all_to_all(x, BOTH, 0, 0, axis_index_groups=CZ_GROUPS)  77.9 us
    all_to_all x3, blocking collectives, over_xy(): return lax.all_to_all(x, 'sector', 0, 0, axis_index_groups=XY_GROUPS)  31 us
    all_to_all x1, blocking collectives, per_device(): got = lax.all_to_all(msg, 'sector', 0, 0)  12.7 us
    all_to_all x1, starting transfers between devices, per_device(): got = lax.all_to_all(msg, 'sector', 0, 0)  8.17 us
    ppermute x1, starting transfers between devices, per_device(): above = lax.ppermute(down, 'op', DOWN)  6.48 us
    all_to_all x1, waiting for transfers between devices, per_device(): got = lax.all_to_all(msg, 'sector', 0, 0)  6.22 us
    pallas_call x1, Pallas kernels, per_device(): call(start_kernel, [((pieces, 16, W), BF16), (half, F32), (half, F32), ((...  3.44 us
  transfers between devices with their start and end apart: 4, of which 2 were waited for; matrix products, arithmetic and copies ran while one was open for 0% of the time, Pallas kernels for 0%

profile of v8, /device:TPU:1, one launch (start us, length us, event | category | flops | bytes accessed | tf_op | source)
XLA Modules:
  0.0 156.6 jit_solution(1643756500167319161)
XLA Ops:
  0.6 0.0 copy-start.5
  0.6 0.0 copy-start
  0.7 3.4 %shard_map.76 = (bf16[32,16,128]{2,1,0:T(8,128)(2,1)}, f32[32,128]{1,0:T(8,128)}, f32[32,128]{1,0:T(8,128)}, s32[8,128]{1,0:T(8,128)}, bf16[2,16,128,128]{3,2,1,...) custom-call(f32[4,128,128]{2,1,0:T(8,128)} %theta.3, s32[2,4]{1,0:T(2,128)} %bitcast.3, bf16[4,16,128,128]{3,2,1,0:T(8,128)(2,1)} %left.7, ...), custom_call_target="tpu_custom_call" | custom-call | bytes 262144 | tf_op jit(solution)/shard_map/pallas_call | solution.py:574
  4.1 6.5 %collective-permute-start.1 = (bf16[2,16,128,128]{3,2,1,0:T(8,128)(2,1)}, bf16[2,16,128,128]{3,2,1,0:T(8,128)(2,1)}, u32[]{:S(2)}, u32[]{:S(2)}) collective-permute-start(bf16[2,16,128,128]{3,2,1,0:T(8,128)(2,1)} %get-tuple-element.33), channel_id=1, source_target_pairs={{0,7},{1,0},{2,1},{3,2},{4,3},{5,4},{6,5},{7,6},{8,15},{9,8},{10,9... | collective-permute-start | bytes 3145736 | tf_op jit(solution)/shard_map/ppermute | solution.py:588
  10.6 0.0 collective-permute-start.2
  10.6 0.0 copy-start.2
  10.6 0.0 copy-start.3
  10.6 8.2 %all-to-all-start = ((bf16[32,16,128]{2,1,0:T(8,128)(2,1)}), bf16[32,16,128]{2,1,0:T(8,128)(2,1)S(1)}, u32[]{:S(2)}, u32[]{:S(2)}) async-start(bf16[32,16,128]{2,1,0:T(8,128)(2,1)} %get-tuple-element.31), calls=%async_computation | async-start | bytes 262144 | tf_op jit(solution)/shard_map/all_to_all | solution.py:590
  18.8 0.3 collective-permute-start
  19.1 0.0 copy-done.5
  19.1 0.3 shard_map.77.ones
  19.4 0.8 collective-permute-done.came
  20.2 6.2 %all-to-all-done.got = bf16[32,16,128]{2,1,0:T(8,128)(2,1)S(1)} async-done(((bf16[32,16,128]{2,1,0:T(8,128)(2,1)}), bf16[32,16,128]{2,1,0:T(8,128)(2,1)S(1)}, u32[]{:S(2)}, u32[]{:S(2)}) %all-to-all-start) | async-done | bytes 131104 | tf_op jit(solution)/shard_map/all_to_all | solution.py:590
  26.5 0.0 copy-done
  26.5 0.0 copy-start.1
  26.5 0.2 shard_map.78
  26.7 12.7 %all_to_all.55.got = bf16[32,32,128]{2,1,0:T(8,128)(2,1)S(1)} all-to-all(bf16[32,32,128]{2,1,0:T(8,128)(2,1)S(1)} %shard_map.78), channel_id=1, replica_groups=mesh['sector'=32,'op'=8] {'sector'}, dimensions={0} | all-to-all | bytes 524288 | tf_op jit(solution)/shard_map/all_to_all | solution.py:599
  39.4 0.0 collective-permute-done.1.above
  39.4 0.0 collective-permute-done.2.below
  39.4 0.0 copy-done.2
  39.4 0.0 copy-done.3
  39.4 0.0 copy-done.1
  39.4 0.0 copy-start.4
  39.5 2.9 %shard_map.79 = (bf16[16,40,128]{2,1,0:T(8,128)(2,1)S(1)}, f32[12,128,128]{2,1,0:T(8,128)S(1)}, bf16[2,2,16,128,128]{4,3,2,1,0:T(8,128)(2,1)S(1)}) custom-call(s32[8,128]{1,0:T(8,128)S(1)} %copy-done.3, f32[4,128,128]{2,1,0:T(8,128)S(1)} %copy-done.2, bf16[32,32,128]{2,1,0:T(8,128)(2,1)S(1)} %all_to_all.55.got, bf16[4,16,128,128]{3,2,1,0:T(8,128)(2,1)S(1)} %copy-done.1, ...), custom_call_target="tpu_custom_call" | custom-call | flops 536870912 | bytes 6291456 | tf_op jit(solution)/shard_map/pallas_call | solution.py:600
  42.3 12.5 %all_to_all.56.got = bf16[16,40,128]{2,1,0:T(8,128)(2,1)S(1)} all-to-all(bf16[16,40,128]{2,1,0:T(8,128)(2,1)S(1)} %get-tuple-element.35), channel_id=1, replica_groups={{0,1,2,3,4,5,6,7,8,9,10,11,12,13,14,15},{16,17,18,19,20,21,22,23,24,25,..., dimensions={0} | all-to-all | bytes 327680 | tf_op jit(solution)/shard_map/all_to_all | solution.py:544
  54.8 0.0 copy-done.4
  54.8 0.1 shard_map.80
  54.9 10.6 %all_to_all.57.got = bf16[16,72,128]{2,1,0:T(8,128)(2,1)S(1)} all-to-all(bf16[16,72,128]{2,1,0:T(8,128)(2,1)S(1)} %get-tuple-element.37), channel_id=1, replica_groups={{0,16,32,48,64,80,96,112,128,144,160,176,192,208,224,240},{8,24,40,56,7..., dimensions={0} | all-to-all | bytes 589824 | tf_op jit(solution)/shard_map/all_to_all | solution.py:548
  65.5 0.4 shard_map.81
  65.9 15.0 %all_to_all.58.got = bf16[16,56,128]{2,1,0:T(8,128)(2,1)S(1)} all-to-all(bf16[16,56,128]{2,1,0:T(8,128)(2,1)S(1)} %shard_map.81), channel_id=1, replica_groups={{0,1,2,3,4,5,6,7,8,9,10,11,12,13,14,15},{16,17,18,19,20,21,22,23,24,25,..., dimensions={0} | all-to-all | bytes 458752 | tf_op jit(solution)/shard_map/all_to_all | solution.py:544
  80.9 1.6 %shard_map.82 = (bf16[16,16,128]{2,1,0:T(8,128)(2,1)S(1)}, f32[6,128,128]{2,1,0:T(8,128)S(1)}, f32[64,128]{1,0:T(8,128)S(1)}, f32[64,128]{1,0:T(8,128)S(1)}, f32[8,128]{1,0:T(8,128)S(1)}) custom-call(s32[8,128]{1,0:T(8,128)S(1)} %copy-done.3, bf16[16,56,128]{2,1,0:T(8,128)(2,1)S(1)} %all_to_all.58.got, bf16[4,16,128,128]{3,2,1,0:T(8,128)(2,1)S(1)} %copy-done.1, ...), custom_call_target="tpu_custom_call" | custom-call | flops 536870912 | bytes 6291456 | tf_op jit(solution)/shard_map/pallas_call | solution.py:618
  82.5 11.8 %all_to_all.59.got = bf16[16,16,128]{2,1,0:T(8,128)(2,1)S(1)} all-to-all(bf16[16,16,128]{2,1,0:T(8,128)(2,1)S(1)} %get-tuple-element.43), channel_id=1, replica_groups={{0,1,2,3,4,5,6,7,8,9,10,11,12,13,14,15},{16,17,18,19,20,21,22,23,24,25,..., dimensions={0} | all-to-all | bytes 131072 | tf_op jit(solution)/shard_map/all_to_all | solution.py:544
  94.2 0.1 shard_map.83
  94.4 10.7 %all_to_all.60.got = bf16[16,72,128]{2,1,0:T(8,128)(2,1)S(1)} all-to-all(bf16[16,72,128]{2,1,0:T(8,128)(2,1)S(1)} %get-tuple-element.47), channel_id=1, replica_groups={{0,16,32,48,64,80,96,112,128,144,160,176,192,208,224,240},{8,24,40,56,7..., dimensions={0} | all-to-all | bytes 589824 | tf_op jit(solution)/shard_map/all_to_all | solution.py:548
  105.1 0.2 shard_map.84
  105.3 13.9 %all_to_all.61.got = bf16[16,56,128]{2,1,0:T(8,128)(2,1)S(1)} all-to-all(bf16[16,56,128]{2,1,0:T(8,128)(2,1)S(1)} %shard_map.84), channel_id=1, replica_groups={{0,1,2,3,4,5,6,7,8,9,10,11,12,13,14,15},{16,17,18,19,20,21,22,23,24,25,..., dimensions={0} | all-to-all | bytes 458752 | tf_op jit(solution)/shard_map/all_to_all | solution.py:544
  119.2 1.6 %shard_map.85 = (bf16[16,24,128]{2,1,0:T(8,128)(2,1)S(1)}, f32[64,128]{1,0:T(8,128)S(1)}, f32[8,128]{1,0:T(8,128)S(1)}) custom-call(s32[8,128]{1,0:T(8,128)S(1)} %copy-done.3, bf16[16,56,128]{2,1,0:T(8,128)(2,1)S(1)} %all_to_all.61.got, bf16[4,16,128,128]{3,2,1,0:T(8,128)(2,1)S(1)} %copy-done.1, bf16[4,16,128,128]{3,2,1,0:T(8,128)(2,1)S(1)} %copy-done, ...), custom_call_target="tpu_custom_call" | custom-call | flops 536870912 | bytes 6291456 | tf_op jit(solution)/shard_map/pallas_call | solution.py:630
  120.8 12.0 %all_to_all.62.got = bf16[16,24,128]{2,1,0:T(8,128)(2,1)S(1)} all-to-all(bf16[16,24,128]{2,1,0:T(8,128)(2,1)S(1)} %get-tuple-element.50), channel_id=1, replica_groups={{0,1,2,3,4,5,6,7,8,9,10,11,12,13,14,15},{16,17,18,19,20,21,22,23,24,25,..., dimensions={0} | all-to-all | bytes 196608 | tf_op jit(solution)/shard_map/all_to_all | solution.py:544
  132.8 9.7 %all_to_all.63.got = f32[16,8,128]{2,1,0:T(8,128)S(1)} all-to-all(f32[16,8,128]{2,1,0:T(8,128)S(1)} %get-tuple-element.52), channel_id=1, replica_groups={{0,16,32,48,64,80,96,112,128,144,160,176,192,208,224,240},{8,24,40,56,7..., dimensions={0} | all-to-all | bytes 131072 | tf_op jit(solution)/shard_map/all_to_all | solution.py:548
  142.5 0.1 shard_map.87
  142.6 12.8 %all_to_all.64.got = bf16[16,40,128]{2,1,0:T(8,128)(2,1)S(1)} all-to-all(bf16[16,40,128]{2,1,0:T(8,128)(2,1)S(1)} %get-tuple-element.55), channel_id=1, replica_groups={{0,1,2,3,4,5,6,7,8,9,10,11,12,13,14,15},{16,17,18,19,20,21,22,23,24,25,..., dimensions={0} | all-to-all | bytes 327680 | tf_op jit(solution)/shard_map/all_to_all | solution.py:544
  155.4 1.2 shard_map.88
  (1 shorter events, 0.0 us)
Async XLA Ops:
  0.6 18.5 %copy-start.5 = (s32[128]{0:T(128)S(1)}, s32[128]{0:T(128)}, u32[]{:S(2)}) copy-start(s32[128]{0:T(128)} %param.8) | copy-start | bytes 1540
  0.6 25.8 %copy-start = (bf16[4,16,128,128]{3,2,1,0:T(8,128)(2,1)S(1)}, bf16[4,16,128,128]{3,2,1,0:T(8,128)(2,1)}, u32[]{:S(2)}) copy-start(bf16[4,16,128,128]{3,2,1,0:T(8,128)(2,1)} %right.7) | copy-start | bytes 6291460
  4.1 35.3 %collective-permute-start.1 = (bf16[2,16,128,128]{3,2,1,0:T(8,128)(2,1)}, bf16[2,16,128,128]{3,2,1,0:T(8,128)(2,1)}, u32[]{:S(2)}, u32[]{:S(2)}) collective-permute-start(bf16[2,16,128,128]{3,2,1,0:T(8,128)(2,1)} %get-tuple-element.33), channel_id=1, source_target_pairs={{0,7},{1,0},{2,1},{3,2},{4,3},{5,4},{6,5},{7,6},{8,15},{9,8},{10,9... | collective-permute-start | bytes 3145736 | tf_op jit(solution)/shard_map/ppermute | solution.py:588
  10.6 28.8 %collective-permute-start.2 = (bf16[2,16,128,128]{3,2,1,0:T(8,128)(2,1)}, bf16[2,16,128,128]{3,2,1,0:T(8,128)(2,1)}, u32[]{:S(2)}, u32[]{:S(2)}) collective-permute-start(bf16[2,16,128,128]{3,2,1,0:T(8,128)(2,1)} %get-tuple-element.34), channel_id=1, source_target_pairs={{0,1},{1,2},{2,3},{3,4},{4,5},{5,6},{6,7},{7,0},{8,9},{9,10},{10,1... | collective-permute-start | bytes 3145736 | tf_op jit(solution)/shard_map/ppermute | solution.py:589
  10.6 28.8 %copy-start.2 = (f32[4,128,128]{2,1,0:T(8,128)S(1)}, f32[4,128,128]{2,1,0:T(8,128)}, u32[]{:S(2)}) copy-start(f32[4,128,128]{2,1,0:T(8,128)} %theta.3) | copy-start | bytes 786436
  10.6 28.8 %copy-start.3 = (s32[8,128]{1,0:T(8,128)S(1)}, s32[8,128]{1,0:T(8,128)}, u32[]{:S(2)}) copy-start(s32[8,128]{1,0:T(8,128)} %get-tuple-element.30.limits) | copy-start | bytes 12292
  10.6 15.9 %all-to-all-start = ((bf16[32,16,128]{2,1,0:T(8,128)(2,1)}), bf16[32,16,128]{2,1,0:T(8,128)(2,1)S(1)}, u32[]{:S(2)}, u32[]{:S(2)}) async-start(bf16[32,16,128]{2,1,0:T(8,128)(2,1)} %get-tuple-element.31), calls=%async_computation | async-start | bytes 262144 | tf_op jit(solution)/shard_map/all_to_all | solution.py:590
  18.8 1.5 collective-permute-start
  26.5 13.0 %copy-start.1 = (bf16[4,16,128,128]{3,2,1,0:T(8,128)(2,1)S(1)}, bf16[4,16,128,128]{3,2,1,0:T(8,128)(2,1)}, u32[]{:S(2)}) copy-start(bf16[4,16,128,128]{3,2,1,0:T(8,128)(2,1)} %left.7) | copy-start | bytes 6291460
  39.4 15.3 %copy-start.4 = (f32[32,128]{1,0:T(8,128)S(1)}, f32[32,128]{1,0:T(8,128)}, u32[]{:S(2)}) copy-start(f32[32,128]{1,0:T(8,128)} %get-tuple-element.36.keep) | copy-start | bytes 49156
